TPU v7x, 128 devices: a whole 4x4x4 slice. The times are simulated.
128 devices in a mesh: wide: 32 (over z_hi, x, y), narrow: 4 (over z_lo, core).
Axes of the slice: x: 4, y: 4, z: 4 (z_hi: 2, z_lo: 2; z = z_hi * 2 + z_lo), core: 2. Of those that a mesh axis runs over, the one named last changes fastest.
Arguments:
- activations: bfloat16 [16, 2560, 768], P('narrow', 'wide'), may hold values from -6 to 6
- conditioning: bfloat16 [16, 2560, 384], P('narrow', 'wide'), may hold values from -6 to 6
- pair_features: bfloat16 [2560, 2560, 128], P('wide', 'narrow'), may hold values from -6 to 6
- key_mask: int32 [2560], P('wide'), may hold values from 0 to 1, as said below
- w_scale: bfloat16 [384, 768], replicated, may hold values from -0.3125 to 0.3125
- w_shift: bfloat16 [384, 768], replicated, may hold values from -0.3125 to 0.3125
- w_query: bfloat16 [768, 768], replicated, may hold values from -0.21875 to 0.21875
- w_key: bfloat16 [768, 768], replicated, may hold values from -0.21875 to 0.21875
- w_value: bfloat16 [768, 768], replicated, may hold values from -0.21875 to 0.21875
- w_gate: bfloat16 [768, 768], replicated, may hold values from -0.21875 to 0.21875
- w_out: bfloat16 [768, 768], replicated, may hold values from -0.21875 to 0.21875
- w_outgate: bfloat16 [384, 768], replicated, may hold values from -0.3125 to 0.3125
- w_bias: bfloat16 [128, 16], replicated, may hold values from -9 to 9
Outputs:
- updated: bfloat16 [16, 2560, 768], P('narrow', 'wide')
Inputs may be any that keep to these rules, and one draw needn't show every extreme that they name: key_mask is 1 on the first token of every aligned block of 80 tokens and 0 on the last of the 2560 tokens; every other token is 0 or 1 independently.
All inputs are finite; a program needn't handle non-finite values.
Results may differ from a plain program's by a relative error of at most 0.0049.
Values may be sent and summed in bfloat16 or wider, within the bound.
No kernel may reach another device: no remote copies, remote signals or barrier semaphores. Data moves between devices by JAX's collectives and lax.ppermute only.
A program may use at most 192 MiB of HBM per device.

v0:
```python
import math

import jax
import jax.numpy as jnp
from jax import lax
from jax.sharding import PartitionSpec as P

EPSILON = 1e-05
NEGATIVE = -1e30


def layer_norm(entries):
    entries = entries.astype(jnp.float32)
    row_mean = jnp.mean(entries, axis=-1, keepdims=True)
    centered = entries - row_mean
    variance = jnp.mean(centered * centered, axis=-1, keepdims=True)
    return centered * lax.rsqrt(variance + EPSILON)


def project(rows_in, weight):
    return jnp.dot(rows_in, weight, preferred_element_type=jnp.float32)


def split_heads(matrix, head_count):
    return matrix.reshape(
        matrix.shape[0], matrix.shape[1], head_count, matrix.shape[2] // head_count
    )


def head_scores(sample_queries, sample_keys, pair_bias, key_valid, score_scale):
    scores = jnp.einsum(
        "qhd,khd->hqk", sample_queries, sample_keys, preferred_element_type=jnp.float32
    )
    scores = scores * score_scale + pair_bias.astype(jnp.float32)
    visible = key_valid[None, None, :] > 0
    return (jnp.where(visible, scores, NEGATIVE), visible)


def per_device(
    activations,
    conditioning,
    pair_features,
    key_mask,
    w_scale,
    w_shift,
    w_query,
    w_key,
    w_value,
    w_gate,
    w_out,
    w_outgate,
    w_bias,
):
    head_count = w_bias.shape[1]
    model_width = activations.shape[2]
    score_scale = 1.0 / math.sqrt(model_width // head_count)
    pair_norm = layer_norm(pair_features).astype(jnp.bfloat16)
    local_bias = jnp.einsum(
        "ijc,ch->hij", pair_norm, w_bias, preferred_element_type=jnp.float32
    ).astype(jnp.bfloat16)
    pair_bias = lax.all_gather(local_bias, "narrow", axis=2, tiled=True)
    cond_norm = layer_norm(conditioning).astype(jnp.bfloat16)
    modulated = (
        jax.nn.sigmoid(project(cond_norm, w_scale)) * layer_norm(activations)
        + project(cond_norm, w_shift)
    ).astype(jnp.bfloat16)
    queries = split_heads(project(modulated, w_query).astype(jnp.bfloat16), head_count)
    gate_rows = jax.nn.sigmoid(project(modulated, w_gate))
    out_gate = jax.nn.sigmoid(project(cond_norm, w_outgate))
    mask_row = key_mask.reshape(1, key_mask.shape[0])
    key_rows = project(modulated, w_key).astype(jnp.bfloat16)
    value_rows = project(modulated, w_value).astype(jnp.bfloat16)
    all_keys, all_values, all_valid = (
        lax.all_gather(key_rows, "wide", axis=1, tiled=True),
        lax.all_gather(value_rows, "wide", axis=1, tiled=True),
        lax.all_gather(mask_row, "wide", axis=1, tiled=True),
    )
    key_valid = all_valid[0]

    def one_sample(item):
        sample_queries, sample_keys, sample_values = item
        scores, visible = head_scores(
            sample_queries, sample_keys, pair_bias, key_valid, score_scale
        )
        row_top = jnp.max(scores, axis=2, keepdims=True)
        exponent = jnp.exp(scores - row_top)
        probabilities = (exponent / jnp.sum(exponent, axis=2, keepdims=True)).astype(jnp.bfloat16)
        return jnp.einsum(
            "hqk,khd->qhd", probabilities, sample_values, preferred_element_type=jnp.float32
        )

    attended = lax.map(
        one_sample,
        (queries, split_heads(all_keys, head_count), split_heads(all_values, head_count)),
    )
    attended = attended.reshape(activations.shape)
    gated = (gate_rows * attended).astype(jnp.bfloat16)
    return (activations.astype(jnp.float32) + out_gate * project(gated, w_out)).astype(jnp.bfloat16)


def solution(mesh):
    in_specs = (
        P("narrow", "wide", None),
        P("narrow", "wide", None),
        P("wide", "narrow", None),
        P("wide"),
        P(),
        P(),
        P(),
        P(),
        P(),
        P(),
        P(),
        P(),
        P(),
    )
    out_specs = P("narrow", "wide", None)
    return jax.shard_map(
        per_device, mesh=mesh, in_specs=in_specs, out_specs=out_specs, check_vma=False
    )
```

profile of v0, /device:TPU:0, one launch (start us, length us, event | category | flops | bytes accessed | tf_op | source)
XLA Modules:
  0.0 591.5 jit_solution(17753165706437048832)
XLA Ops:
  6.5 9.4 %convert_reduce_fusion = f32[80,640]{1,0:T(8,128)S(1)} fusion(bf16[80,640,128]{2,1,0:T(8,128)(2,1)} %param.17), kind=kLoop, calls=%fused_computation.21 | loop fusion | flops 13056000 | bytes 13312000 | tf_op jit(solution)/shard_map/reduce_sum | solution.py:14
  16.0 15.3 %fusion.27 = f32[80,640]{1,0:T(8,128)S(1)} fusion(bf16[80,640,128]{2,1,0:T(8,128)(2,1)S(1)} %copy-done.2, f32[80,640]{1,0:T(8,128)S(1)} %broadcast_multiply_fusion), kind=kLoop, calls=%fused_computation.24 | loop fusion | flops 26163200 | bytes 13516800 | tf_op jit(solution)/shard_map/reduce_sum | solution.py:16
  31.4 0.0 copy-start.3
  31.4 0.0 copy-start.4
  31.4 0.0 copy-start.8
  31.4 0.0 copy-start.6
  31.4 21.9 %fusion.36 = bf16[16,80,640]{2,0,1:T(8,128)(2,1)} fusion(bf16[80,640,128]{2,1,0:T(8,128)(2,1)S(1)} %copy-done.2, f32[80,640]{1,0:T(8,128)S(1)} %add_rsqrt_fusion, f32[80,640]{1,0:T(8,128)S(1)} %broadcast_multiply_fusion, bf16[128,16]{0,1:T(8,128)(2,1)S(1)} %copy-done.9), kind=kOutput, calls=%fused_computation.30 | convolution fusion | flops 236748800 | bytes 15159296 | tf_op jit(solution)/shard_map/ijc,ch->hij/dot_general | solution.py:58
  53.3 0.0 all-gather.9.cloned.1.call-update
  53.3 0.0 all-gather.5.cloned.1.call-start
  53.4 0.1 convert_reduce_fusion.2
  53.5 0.2 fusion.68
  53.8 0.2 convert_reduce_fusion.1
  53.9 0.3 fusion.60
  54.3 0.0 copy-done.8
  54.3 0.6 fusion.46
  54.9 0.5 fusion.51
  55.4 0.0 copy-done
  55.4 1.3 convolution_convert_fusion.2
  56.7 0.0 all-gather.5.cloned.1.call-update
  56.7 0.0 all-gather.7.cloned.1.call-start
  56.8 2.7 convolution_convert_fusion
  59.5 0.0 all-gather.7.cloned.1.call-update
  59.5 1.8 convolution_convert_fusion.1
  61.3 0.4 copy.20
  61.7 0.7 dynamic-slice
  63.1 0.3 dynamic-update-slice
  63.4 187.0 %all-reduce = s32[2560]{0:T(1024)S(1)} all-reduce(s32[2560]{0:T(1024)S(1)} %dynamic-update-slice), channel_id=2, replica_groups=mesh['wide'=32,'narrow'=4] {'wide'}, use_global_device_ids=true, to_apply=%add | all-reduce | flops 2560 | bytes 20480
  250.4 2.6 fusion.49
  253.0 9.1 %copy.22 = bf16[16,80,2560]{2,1,0:T(8,128)(2,1)} copy(bf16[16,80,2560]{2,0,1:T(8,128)(2,1)} %all-gather.9.cloned.1.call-done) | data formatting | bytes 13107200 | tf_op jit(solution)/shard_map/while | solution.py:92
  262.2 14.4 %all-gather.5.cloned.1.call-done = bf16[4,2560,768]{2,1,0:T(8,128)(2,1)} async-done(((bf16[4,80,768]{2,1,0:T(8,128)(2,1)}), bf16[4,2560,768]{2,1,0:T(8,128)(2,1)}) %all-gather.5.cloned.1.call-update) | async-done | bytes 15728656 | tf_op jit(solution)/shard_map/all_gather | solution.py:75
  276.6 19.4 %copy.19 = bf16[4,2560,768]{1,2,0:T(8,128)(2,1)} copy(bf16[4,2560,768]{2,1,0:T(8,128)(2,1)} %all-gather.5.cloned.1.call-done) | data formatting | bytes 31457280 | tf_op jit(solution)/shard_map/all_gather | solution.py:75
  296.0 131.6 %all-gather.7.cloned.1.call-done = bf16[4,2560,768]{2,1,0:T(8,128)(2,1)} async-done(((bf16[4,80,768]{2,1,0:T(8,128)(2,1)}), bf16[4,2560,768]{2,1,0:T(8,128)(2,1)}) %all-gather.7.cloned.1.call-update) | async-done | bytes 15728656 | tf_op jit(solution)/shard_map/all_gather | solution.py:74
  427.6 19.2 %copy.21 = bf16[4,2560,768]{1,2,0:T(8,128)(2,1)} copy(bf16[4,2560,768]{2,1,0:T(8,128)(2,1)} %all-gather.7.cloned.1.call-done) | data formatting | bytes 31457280 | tf_op jit(solution)/shard_map/all_gather | solution.py:74
  446.8 132.3 %while.10 = (s32[]{:T(128)}, f32[4,80,16,48]{1,3,2,0:T(8,128)}, bf16[4,2560,16,48]{1,3,2,0:T(8,128)(2,1)}, s32[1,2560]{1,0:T(1,128)S(1)}, bf16[4,80,16,48]{1,3,2...) while((s32[]{:T(128)}, f32[4,80,16,48]{1,3,2,0:T(8,128)}, ...), condition=%wide.region_9.10_spmd, body=%wide.region_6.9_spmd.sunk | while | flops 986325760 | bytes 65044052 | solution.py:92
  446.9 11.0 %add_select_fusion.2 = f32[16,80,2560]{2,1,0:T(8,128)} fusion(bf16[16,80,2560]{2,1,0:T(8,128)(2,1)} %get-tuple-element.138, pred[2560]{0:T(1024)(128)(4,1)S(1)} %compare_reduce_fusion.2, bf16[4,2560,16,48]{1,3,2,0:T(8,128)(2,1)} %get-tuple-element.137, s32[]{:T(128)} %get-tuple-element.124, bf16[4,80,16,48]{1,3,2,0:T(8,128)(2,1)S(1)} %get-tuple-element.136), kind=kOutput, calls=%fused_computation.3.clone.2 | convolution fusion | flops 327680000 | bytes 23793664 | tf_op jit(solution)/shard_map/while/body/eval_jaxpr/qhd,khd->hqk/dot_general | solution.py:31
  457.8 9.0 %fusion.103 = f32[16,80]{1,0:T(8,128)S(1)} fusion(bf16[16,80,2560]{2,1,0:T(8,128)(2,1)} %get-tuple-element.138, pred[2560]{0:T(1024)(128)(4,1)S(1)} %compare_reduce_fusion.2, bf16[4,2560,16,48]{1,3,2,0:T(8,128)(2,1)} %get-tuple-element.137, s32[]{:T(128)} %get-tuple-element.124, bf16[4,80,16,48]{1,3,2,0:T(8,128)(2,1)S(1)} %get-tuple-element.136), kind=kOutput, calls=%fused_computation.82.clone.1 | convolution fusion | flops 334236160 | bytes 10691584 | tf_op jit(solution)/shard_map/while/body/eval_jaxpr/sub | solution.py:86
  466.8 13.1 %fusion.104 = f32[4,80,16,48]{1,3,2,0:T(8,128)} fusion(f32[4,80,16,48]{1,3,2,0:T(8,128)} %get-tuple-element.125, s32[]{:T(128)} %get-tuple-element.124, f32[16,80]{1,0:T(8,128)S(1)} %fusion.103, bf16[4,2560,16,48]{1,3,2,0:T(8,128)(2,1)} %get-tuple-element.134, f32[16,80,2560]{2,1,0:T(8,128)} %add_select_fusion.2), kind=kOutput, calls=%fused_computation.10.clone.1 | convolution fusion | flops 324407040 | bytes 30545920 | tf_op jit(solution)/shard_map/while/body/eval_jaxpr/hqk,khd->qhd/dot_general | solution.py:88
  480.0 10.9 %add_select_fusion.2 = f32[16,80,2560]{2,1,0:T(8,128)} fusion(bf16[16,80,2560]{2,1,0:T(8,128)(2,1)} %get-tuple-element.138, pred[2560]{0:T(1024)(128)(4,1)S(1)} %compare_reduce_fusion.2, bf16[4,2560,16,48]{1,3,2,0:T(8,128)(2,1)} %get-tuple-element.137, s32[]{:T(128)} %get-tuple-element.124, bf16[4,80,16,48]{1,3,2,0:T(8,128)(2,1)S(1)} %get-tuple-element.136), kind=kOutput, calls=%fused_computation.3.clone.2 | convolution fusion | flops 327680000 | bytes 23793664 | tf_op jit(solution)/shard_map/while/body/eval_jaxpr/qhd,khd->hqk/dot_general | solution.py:31
  490.9 9.0 %fusion.103 = f32[16,80]{1,0:T(8,128)S(1)} fusion(bf16[16,80,2560]{2,1,0:T(8,128)(2,1)} %get-tuple-element.138, pred[2560]{0:T(1024)(128)(4,1)S(1)} %compare_reduce_fusion.2, bf16[4,2560,16,48]{1,3,2,0:T(8,128)(2,1)} %get-tuple-element.137, s32[]{:T(128)} %get-tuple-element.124, bf16[4,80,16,48]{1,3,2,0:T(8,128)(2,1)S(1)} %get-tuple-element.136), kind=kOutput, calls=%fused_computation.82.clone.1 | convolution fusion | flops 334236160 | bytes 10691584 | tf_op jit(solution)/shard_map/while/body/eval_jaxpr/sub | solution.py:86
  499.9 13.1 %fusion.104 = f32[4,80,16,48]{1,3,2,0:T(8,128)} fusion(f32[4,80,16,48]{1,3,2,0:T(8,128)} %get-tuple-element.125, s32[]{:T(128)} %get-tuple-element.124, f32[16,80]{1,0:T(8,128)S(1)} %fusion.103, bf16[4,2560,16,48]{1,3,2,0:T(8,128)(2,1)} %get-tuple-element.134, f32[16,80,2560]{2,1,0:T(8,128)} %add_select_fusion.2), kind=kOutput, calls=%fused_computation.10.clone.1 | convolution fusion | flops 324407040 | bytes 30545920 | tf_op jit(solution)/shard_map/while/body/eval_jaxpr/hqk,khd->qhd/dot_general | solution.py:88
  513.0 10.9 %add_select_fusion.2 = f32[16,80,2560]{2,1,0:T(8,128)} fusion(bf16[16,80,2560]{2,1,0:T(8,128)(2,1)} %get-tuple-element.138, pred[2560]{0:T(1024)(128)(4,1)S(1)} %compare_reduce_fusion.2, bf16[4,2560,16,48]{1,3,2,0:T(8,128)(2,1)} %get-tuple-element.137, s32[]{:T(128)} %get-tuple-element.124, bf16[4,80,16,48]{1,3,2,0:T(8,128)(2,1)S(1)} %get-tuple-element.136), kind=kOutput, calls=%fused_computation.3.clone.2 | convolution fusion | flops 327680000 | bytes 23793664 | tf_op jit(solution)/shard_map/while/body/eval_jaxpr/qhd,khd->hqk/dot_general | solution.py:31
  523.9 9.0 %fusion.103 = f32[16,80]{1,0:T(8,128)S(1)} fusion(bf16[16,80,2560]{2,1,0:T(8,128)(2,1)} %get-tuple-element.138, pred[2560]{0:T(1024)(128)(4,1)S(1)} %compare_reduce_fusion.2, bf16[4,2560,16,48]{1,3,2,0:T(8,128)(2,1)} %get-tuple-element.137, s32[]{:T(128)} %get-tuple-element.124, bf16[4,80,16,48]{1,3,2,0:T(8,128)(2,1)S(1)} %get-tuple-element.136), kind=kOutput, calls=%fused_computation.82.clone.1 | convolution fusion | flops 334236160 | bytes 10691584 | tf_op jit(solution)/shard_map/while/body/eval_jaxpr/sub | solution.py:86
  532.9 13.1 %fusion.104 = f32[4,80,16,48]{1,3,2,0:T(8,128)} fusion(f32[4,80,16,48]{1,3,2,0:T(8,128)} %get-tuple-element.125, s32[]{:T(128)} %get-tuple-element.124, f32[16,80]{1,0:T(8,128)S(1)} %fusion.103, bf16[4,2560,16,48]{1,3,2,0:T(8,128)(2,1)} %get-tuple-element.134, f32[16,80,2560]{2,1,0:T(8,128)} %add_select_fusion.2), kind=kOutput, calls=%fused_computation.10.clone.1 | convolution fusion | flops 324407040 | bytes 30545920 | tf_op jit(solution)/shard_map/while/body/eval_jaxpr/hqk,khd->qhd/dot_general | solution.py:88
  546.0 10.9 %add_select_fusion.2 = f32[16,80,2560]{2,1,0:T(8,128)} fusion(bf16[16,80,2560]{2,1,0:T(8,128)(2,1)} %get-tuple-element.138, pred[2560]{0:T(1024)(128)(4,1)S(1)} %compare_reduce_fusion.2, bf16[4,2560,16,48]{1,3,2,0:T(8,128)(2,1)} %get-tuple-element.137, s32[]{:T(128)} %get-tuple-element.124, bf16[4,80,16,48]{1,3,2,0:T(8,128)(2,1)S(1)} %get-tuple-element.136), kind=kOutput, calls=%fused_computation.3.clone.2 | convolution fusion | flops 327680000 | bytes 23793664 | tf_op jit(solution)/shard_map/while/body/eval_jaxpr/qhd,khd->hqk/dot_general | solution.py:31
  557.0 9.0 %fusion.103 = f32[16,80]{1,0:T(8,128)S(1)} fusion(bf16[16,80,2560]{2,1,0:T(8,128)(2,1)} %get-tuple-element.138, pred[2560]{0:T(1024)(128)(4,1)S(1)} %compare_reduce_fusion.2, bf16[4,2560,16,48]{1,3,2,0:T(8,128)(2,1)} %get-tuple-element.137, s32[]{:T(128)} %get-tuple-element.124, bf16[4,80,16,48]{1,3,2,0:T(8,128)(2,1)S(1)} %get-tuple-element.136), kind=kOutput, calls=%fused_computation.82.clone.1 | convolution fusion | flops 334236160 | bytes 10691584 | tf_op jit(solution)/shard_map/while/body/eval_jaxpr/sub | solution.py:86
  565.9 13.1 %fusion.104 = f32[4,80,16,48]{1,3,2,0:T(8,128)} fusion(f32[4,80,16,48]{1,3,2,0:T(8,128)} %get-tuple-element.125, s32[]{:T(128)} %get-tuple-element.124, f32[16,80]{1,0:T(8,128)S(1)} %fusion.103, bf16[4,2560,16,48]{1,3,2,0:T(8,128)(2,1)} %get-tuple-element.134, f32[16,80,2560]{2,1,0:T(8,128)} %add_select_fusion.2), kind=kOutput, calls=%fused_computation.10.clone.1 | convolution fusion | flops 324407040 | bytes 30545920 | tf_op jit(solution)/shard_map/while/body/eval_jaxpr/hqk,khd->qhd/dot_general | solution.py:88
  579.1 2.0 copy.23
  581.0 3.9 fusion.50
  (32 shorter events, 0.3 us)
Async XLA Ops:
  6.5 48.8 %copy-start = (bf16[768,768]{1,0:T(8,128)(2,1)S(1)}, bf16[768,768]{1,0:T(8,128)(2,1)}, u32[]{:S(2)}) copy-start(bf16[768,768]{1,0:T(8,128)(2,1)} %param.23) | copy-start | bytes 3538948
  6.5 24.8 %copy-start.9 = (bf16[128,16]{0,1:T(8,128)(2,1)S(1)}, bf16[128,16]{0,1:T(8,128)(2,1)}, u32[]{:S(2)}) copy-start(bf16[128,16]{0,1:T(8,128)(2,1)} %param.27) | copy-start | bytes 12292
  6.5 246.5 %all-gather.9.cloned.1.call-start = ((), (), s32[]{:S(2)}) async-start(), calls=%async_computation.2 | async-start | bytes 8192000 | tf_op jit(solution)/shard_map/all_gather | solution.py:61
  6.5 9.4 %copy-start.2 = (bf16[80,640,128]{2,1,0:T(8,128)(2,1)S(1)}, bf16[80,640,128]{2,1,0:T(8,128)(2,1)}, u32[]{:S(2)}) copy-start(bf16[80,640,128]{2,1,0:T(8,128)(2,1)} %param.17) | copy-start | bytes 39321604
  31.4 22.0 %copy-start.3 = (bf16[4,80,384]{2,1,0:T(8,128)(2,1)S(1)}, bf16[4,80,384]{2,1,0:T(8,128)(2,1)}, u32[]{:S(2)}) copy-start(bf16[4,80,384]{2,1,0:T(8,128)(2,1)} %param.16) | copy-start | bytes 737284
  31.4 22.4 %copy-start.4 = (bf16[4,80,768]{2,1,0:T(8,128)(2,1)S(1)}, bf16[4,80,768]{2,1,0:T(8,128)(2,1)}, u32[]{:S(2)}) copy-start(bf16[4,80,768]{2,1,0:T(8,128)(2,1)} %param.15) | copy-start | bytes 1474564
  31.4 22.9 %copy-start.8 = (bf16[384,768]{1,0:T(8,128)(2,1)S(1)}, bf16[384,768]{1,0:T(8,128)(2,1)}, u32[]{:S(2)}) copy-start(bf16[384,768]{1,0:T(8,128)(2,1)} %param.19) | copy-start | bytes 1769476
  31.4 23.5 %copy-start.6 = (bf16[384,768]{1,0:T(8,128)(2,1)S(1)}, bf16[384,768]{1,0:T(8,128)(2,1)}, u32[]{:S(2)}) copy-start(bf16[384,768]{1,0:T(8,128)(2,1)} %param.20) | copy-start | bytes 1769476
  53.3 8.5 %copy-start.11 = (u32[128]{0:T(128)S(1)}, u32[128]{0:T(128)}, u32[]{:S(2)}) copy-start(u32[128]{0:T(128)} %constant.49) | copy-start | bytes 1540
  53.3 9.8 %copy-start.10 = (s32[80]{0:T(128)S(1)}, s32[80]{0:T(128)}, u32[]{:S(2)}) copy-start(s32[80]{0:T(128)} %param.18) | copy-start | bytes 964
  53.3 223.3 %all-gather.5.cloned.1.call-start = ((), (), s32[]{:S(2)}) async-start(), calls=%async_computation | async-start | bytes 16220160 | tf_op jit(solution)/shard_map/all_gather | solution.py:75
  55.4 4.1 copy-start.7
  56.7 370.8 %all-gather.7.cloned.1.call-start = ((), (), s32[]{:S(2)}) async-start(), calls=%async_computation.1 | async-start | bytes 16220160 | tf_op jit(solution)/shard_map/all_gather | solution.py:74
  446.8 134.2 %copy-start.5 = (bf16[4,80,768]{2,1,0:T(8,128)(2,1)S(1)}, bf16[4,80,768]{2,1,0:T(8,128)(2,1)}, u32[]{:S(2)}) copy-start(bf16[4,80,768]{2,1,0:T(8,128)(2,1)} %param.15) | copy-start | bytes 1474564
  579.1 5.9 copy-start.1
Sparse Core Ops, SparseCore 0:
  53.4 68.6 all-gather.8
  125.2 151.3 all-gather.4
  279.7 147.8 all-gather.6
where the time goes:
time: 593 us; the launch traced here: 592 us
  blocking collectives  187 us (32%)
  matrix products  167 us (28%)
  waiting for transfers between devices  146 us (25%)
  local copies, waits for them, and re-layouts  51.1 us (9%)
  other arithmetic  25.8 us (4%)
  between operations  14.1 us (2%)
    unnamed x1, blocking collectives  187 us
    all_gather x1, waiting for transfers between devices, per_device(): lax.all_gather(key_rows, 'wide', axis=1, tiled=True)  132 us
    dot_general x4, matrix products, one_sample(): jnp.einsum('hqk,khd->qhd', probabilities, sample_values, preferred_elemen...  52.5 us
    dot_general x4, matrix products, head_scores(): jnp.einsum('qhd,khd->hqk', sample_queries, sample_keys, preferred_element...  43.7 us
    sub x4, matrix products, one_sample(): exponent = jnp.exp(scores - row_top)  35.9 us
    dot_general x1, matrix products, per_device(): jnp.einsum('ijc,ch->hij', pair_norm, w_bias, preferred_element_type=jnp.f...  21.9 us
    all_gather x1, local copies, waits for them, and re-layouts, per_device(): lax.all_gather(value_rows, 'wide', axis=1, tiled=True)  19.4 us
    all_gather x1, local copies, waits for them, and re-layouts, per_device(): lax.all_gather(key_rows, 'wide', axis=1, tiled=True)  19.2 us
  transfers between devices with their start and end apart: 3, of which 2 were waited for; matrix products, arithmetic and copies ran while one was open for 7% of the time, Pallas kernels for 0%

commit v1 on v0

v1 whole, which is shorter than its diff:
```python
import math

import jax
import jax.numpy as jnp
import numpy as np
from jax import lax
from jax.experimental import pallas as pl
from jax.experimental.pallas import tpu as pltpu
from jax.sharding import Mesh, PartitionSpec as P

EPSILON = 1e-05
NEGATIVE = -1e30
LOG2E = math.log2(math.e)
HEADS = 16
HEAD = 48
LANES = 128
GROUP = 8
XZ = ("zh", "x", "zl")
BF = jnp.bfloat16
F32 = jnp.float32
VMEM_BYTES = 56 * 1024 * 1024
NT = (((1,), (1,)), ((), ()))


def layer_norm(entries):
    entries = entries.astype(F32)
    row_mean = jnp.mean(entries, axis=-1, keepdims=True)
    centered = entries - row_mean
    variance = jnp.mean(centered * centered, axis=-1, keepdims=True)
    return centered * lax.rsqrt(variance + EPSILON)


def dot(left, right):
    return jnp.dot(left, right, preferred_element_type=F32)


def placement():
    table = np.zeros((2, GROUP, HEAD, GROUP, 2, 64), np.float32)
    for head in range(GROUP):
        for channel in range(HEAD):
            table[0, head, channel, head, 0, channel] = 1
            table[1, head, channel, head, 1, channel] = 1
    return jnp.asarray(table.reshape(2 * GROUP * HEAD, GROUP * LANES), BF)


def qkv_kernel(act, cond, extra, place, ws, wsh, wq, wk, wv, kv_out, q_out, mod_out, cn_out, mod):
    samples, tokens, width = act.shape
    rows = samples * tokens

    @pl.when(pl.program_id(0) == 0)
    def _():
        cond_norm = layer_norm(cond[...].reshape(rows, cond.shape[2])).astype(BF)
        normed = layer_norm(act[...].reshape(rows, width))
        modulated = jax.nn.sigmoid(dot(cond_norm, ws[...])) * normed + dot(cond_norm, wsh[...])
        mod[...] = modulated.astype(BF)
        mod_out[...] = mod[...].reshape(mod_out.shape)
        cn_out[...] = cond_norm.reshape(cn_out.shape)

    modulated = mod[...]
    q = (dot(modulated, wq[...]) * (LOG2E / math.sqrt(HEAD))).astype(BF)
    k = dot(modulated, wk[...]).astype(BF)
    v = dot(modulated, wv[...]).astype(BF)
    table = place[...]
    for s in range(samples):
        row = slice(s * tokens, (s + 1) * tokens)
        pair = [k[row], v[row]] if s % 2 == 0 else [v[row], k[row]]
        placed = dot(jnp.concatenate(pair, axis=1), table).astype(BF)
        for h in range(GROUP):
            kv_out[h, s] = placed[:, h * LANES:(h + 1) * LANES] + extra[s % 2]
    lane = lax.broadcasted_iota(jnp.int32, (tokens, LANES), 1)
    one = jnp.where((lane == HEAD) | (lane == 64 + HEAD), 1.0, 0.0).astype(BF)
    for p in range(samples // 2):
        first = slice(2 * p * tokens, (2 * p + 1) * tokens)
        second = slice((2 * p + 1) * tokens, (2 * p + 2) * tokens)
        placed = dot(jnp.concatenate([q[first], q[second]], axis=1), table).astype(BF)
        for h in range(GROUP):
            q_out[h, p] = placed[:, h * LANES:(h + 1) * LANES] + one


def project_qkv(act, cond, extra, place, ws, wsh, wq, wk, wv):
    samples, tokens, width = act.shape
    steps = HEADS // GROUP
    columns = GROUP * HEAD
    whole = lambda a: pl.BlockSpec(a.shape, lambda g: (0,) * a.ndim)
    part = pl.BlockSpec((width, columns), lambda g: (0, g))
    return pl.pallas_call(
        qkv_kernel,
        grid=(steps,),
        in_specs=[whole(act), whole(cond), whole(extra), whole(place), whole(ws), whole(wsh), part, part, part],
        out_specs=[
            pl.BlockSpec((GROUP, samples, tokens, LANES), lambda g: (g, 0, 0, 0)),
            pl.BlockSpec((GROUP, samples // 2, tokens, LANES), lambda g: (g, 0, 0, 0)),
            whole(act),
            whole(cond),
        ],
        out_shape=[
            jax.ShapeDtypeStruct((HEADS, samples, tokens, LANES), BF),
            jax.ShapeDtypeStruct((HEADS, samples // 2, tokens, LANES), BF),
            jax.ShapeDtypeStruct(act.shape, BF),
            jax.ShapeDtypeStruct(cond.shape, BF),
        ],
        scratch_shapes=[pltpu.VMEM((samples * tokens, width), BF)],
        compiler_params=pltpu.CompilerParams(vmem_limit_bytes=VMEM_BYTES),
        cost_estimate=pl.CostEstimate(flops=4_000_000_000, bytes_accessed=10_000_000, transcendentals=300_000),
        name="qkv",
    )(act, cond, extra, place, ws, wsh, wq, wk, wv)


def bias_kernel(pair, weights, sums, out, rows):
    count = pair.shape[0]
    mean_table = jnp.full((LANES, LANES), 1.0 / LANES, BF)
    for i in range(count):
        x = pair[i]
        c = x - dot(x, mean_table).astype(BF)
        both = jnp.concatenate([c, c * c], axis=1)
        r = lax.dot_general(weights[...], both, NT, preferred_element_type=F32)
        shift = r[HEADS:HEADS + 1]
        scale = lax.rsqrt(r[HEADS + 8:HEADS + 9] - shift * shift + EPSILON) * LOG2E
        rows[i] = (r[:HEADS] - shift * sums[...]) * scale
    out[...] = jnp.swapaxes(rows[...], 0, 1).astype(BF)


def project_bias(pair, w_bias):
    queries, keys, channels = pair.shape
    step = 16
    wt = w_bias.T
    zero = jnp.zeros((HEADS, channels), BF)
    part = jnp.full((8, channels), 1.0 / channels, BF)
    weights = jnp.concatenate(
        [
            jnp.concatenate([wt, zero], axis=1),
            jnp.concatenate([part, zero[:8]], axis=1),
            jnp.concatenate([zero[:8], part], axis=1),
        ],
        axis=0,
    )
    sums = jnp.sum(wt.astype(F32), axis=1, keepdims=True)
    return pl.pallas_call(
        bias_kernel,
        grid=(queries // step,),
        in_specs=[
            pl.BlockSpec((step, keys, channels), lambda i: (i, 0, 0)),
            pl.BlockSpec(weights.shape, lambda i: (0, 0)),
            pl.BlockSpec(sums.shape, lambda i: (0, 0)),
        ],
        out_specs=pl.BlockSpec((HEADS, step, keys), lambda i: (0, i, 0)),
        out_shape=jax.ShapeDtypeStruct((HEADS, queries, keys), BF),
        scratch_shapes=[pltpu.VMEM((step, HEADS, keys), F32)],
        compiler_params=pltpu.CompilerParams(vmem_limit_bytes=VMEM_BYTES),
        cost_estimate=pl.CostEstimate(flops=10_000_000_000, bytes_accessed=15_000_000, transcendentals=100_000),
        name="bias",
    )(pair, weights, sums)


T = 4


def attend_kernel(core, q, kv, own, other, out, keys):
    tokens = q.shape[3]
    me = core[0]
    for z in range(2):
        for o in range(2):
            quarter = me if o == 0 else 1 - me
            for low in range(2):
                for y in range(4):
                    at = ((z * 2 + o) * 8 + low * 4 + y) * tokens
                    for s in range(2):
                        keys[s, at:at + tokens] = kv[y, z, 2 * quarter + low, 0, s]
    span = T * tokens
    lane = lax.broadcasted_iota(jnp.int32, (span, LANES), 1)
    low_half = lane < 64

    def block(t, carry):
        pair_q = q[pl.ds(t * T, T), 0, 0].reshape(span, LANES)
        results = []
        for s in range(2):
            mine = jnp.where(low_half if s == 0 else ~low_half, pair_q, jnp.zeros_like(pair_q))
            scores = []
            for z in range(2):
                for o in range(2):
                    at = (z * 2 + o) * 8 * tokens
                    b = (own if o == 0 else other)[pl.ds(t * T, T), z].reshape(span, 8 * tokens)
                    part = lax.dot_general(mine, keys[s, at:at + 8 * tokens], NT, preferred_element_type=F32)
                    scores.append(part + b.astype(F32))
            tops = [jnp.max(part, axis=1, keepdims=True) for part in scores]
            top = jnp.maximum(jnp.maximum(tops[0], tops[1]), jnp.maximum(tops[2], tops[3]))
            total = None
            for n, part in enumerate(scores):
                p = jnp.exp2(part - top).astype(BF)
                o_part = dot(p, keys[s, n * 8 * tokens:(n + 1) * 8 * tokens])
                total = o_part if total is None else total + o_part
            at = 64 + HEAD if s == 0 else HEAD
            results.append(total / total[:, at:at + 1])
        merged = jnp.where(low_half, results[1], results[0]).astype(BF)
        out[pl.ds(t * T, T), 0, 0] = merged.reshape(T, tokens, LANES)
        return carry

    lax.fori_loop(0, 8 // T, block, 0)


def attend(core, q, kv, own, other):
    tokens = q.shape[3]
    q_spec = pl.BlockSpec((8, 1, 1, tokens, LANES), lambda z, p, c: (0, z, p, 0, 0))
    b_spec = pl.BlockSpec(own.shape, lambda z, p, c: (0, 0, 0, 0))
    return pl.pallas_call(
        attend_kernel,
        grid_spec=pltpu.PrefetchScalarGridSpec(
            num_scalar_prefetch=1,
            grid=(2, 2),
            in_specs=[
                q_spec,
                pl.BlockSpec((4, 2, 4, 1, 2, tokens, LANES), lambda z, p, c: (0, 0, 0, z, p, 0, 0)),
                b_spec,
                b_spec,
            ],
            out_specs=q_spec,
            scratch_shapes=[pltpu.VMEM((2, 32 * tokens, LANES), BF)],
        ),
        out_shape=jax.ShapeDtypeStruct(q.shape, BF),
        compiler_params=pltpu.CompilerParams(vmem_limit_bytes=VMEM_BYTES),
        cost_estimate=pl.CostEstimate(flops=14_000_000_000, bytes_accessed=10_000_000, transcendentals=13_000_000),
        name="attend",
    )(core, q, kv, own, other)


def gate_kernel(mod, cn, place, wg, wog, gate_out, og_out):
    samples, tokens, width = mod.shape
    rows = samples * tokens
    og_out[...] = jax.nn.sigmoid(dot(cn[...].reshape(rows, cn.shape[2]), wog[...])).reshape(og_out.shape)
    columns = GROUP * HEAD
    low = place[0:columns]
    high = place[columns:2 * columns]
    for g in range(HEADS // GROUP):
        w = wg[:, g * columns:(g + 1) * columns]
        w_low = dot(w, low).astype(BF)
        w_high = dot(w, high).astype(BF)
        for p in range(samples // 2):
            value = dot(mod[2 * p + 1], w_low) + dot(mod[2 * p], w_high)
            gate_out[p, :, g * GROUP * LANES:(g + 1) * GROUP * LANES] = jax.nn.sigmoid(value)


def gates(mod, cn, place, wg, wog):
    samples, tokens, width = mod.shape
    return pl.pallas_call(
        gate_kernel,
        out_shape=[
            jax.ShapeDtypeStruct((samples // 2, tokens, HEADS * LANES), F32),
            jax.ShapeDtypeStruct(mod.shape, F32),
        ],
        compiler_params=pltpu.CompilerParams(vmem_limit_bytes=VMEM_BYTES),
        cost_estimate=pl.CostEstimate(flops=4_000_000_000, bytes_accessed=9_000_000, transcendentals=1_000_000),
        name="gates",
    )(mod, cn, place, wg, wog)


def out_kernel(attended, gate, og, act, wo, out, low, high):
    samples, tokens, width = act.shape
    low[...] = jnp.zeros_like(low)
    high[...] = jnp.zeros_like(high)
    for h in range(HEADS):
        rows = wo[h * HEAD:(h + 1) * HEAD]
        low[h * LANES:h * LANES + HEAD] = rows
        high[h * LANES + 64:h * LANES + 64 + HEAD] = rows
    for p in range(samples // 2):
        gated = jnp.concatenate(
            [
                (attended[h, p].astype(F32) * gate[p, :, h * LANES:(h + 1) * LANES]).astype(BF)
                for h in range(HEADS)
            ],
            axis=1,
        )
        for s, table in ((2 * p, high), (2 * p + 1, low)):
            out[s] = (act[s].astype(F32) + og[s] * dot(gated, table[...])).astype(BF)


def project_out(attended, gate, og, act, wo):
    width = act.shape[2]
    return pl.pallas_call(
        out_kernel,
        out_shape=jax.ShapeDtypeStruct(act.shape, BF),
        scratch_shapes=[pltpu.VMEM((HEADS * LANES, width), BF)] * 2,
        compiler_params=pltpu.CompilerParams(vmem_limit_bytes=VMEM_BYTES),
        cost_estimate=pl.CostEstimate(flops=2_000_000_000, bytes_accessed=6_000_000, transcendentals=0),
        name="out",
    )(attended, gate, og, act, wo)


def key_extras(key_mask):
    pad = jnp.where(key_mask > 0, 0.0, NEGATIVE)[:, None]
    lane = jnp.arange(LANES)[None, :]
    first = jnp.where(lane == HEAD, pad, jnp.where(lane == 64 + HEAD, 1.0, 0.0))
    second = jnp.where(lane == 64 + HEAD, pad, jnp.where(lane == HEAD, 1.0, 0.0))
    return jnp.stack([first, second]).astype(BF)


def per_device(
    activations,
    conditioning,
    pair_features,
    key_mask,
    w_scale,
    w_shift,
    w_query,
    w_key,
    w_value,
    w_gate,
    w_out,
    w_outgate,
    w_bias,
):
    tokens = activations.shape[1]
    place = placement()
    kv, q, modulated, cond_norm = project_qkv(
        activations, conditioning, key_extras(key_mask), place, w_scale, w_shift, w_query, w_key, w_value
    )
    exchange = lambda a: lax.all_to_all(a, XZ, 0, 0, tiled=True)
    kv = exchange(kv)
    kv = lax.all_gather(kv, "y", axis=0)
    q = exchange(q)
    own = exchange(project_bias(pair_features, w_bias))
    other = lax.ppermute(own, "co", [(0, 1), (1, 0)])
    gate, out_gate = gates(modulated, cond_norm, place, w_gate, w_outgate)
    core = lax.axis_index("co").astype(jnp.int32).reshape(1)
    keys = own.shape[2]
    attended = attend(
        core,
        q.reshape(8, 2, 2, tokens, LANES),
        kv.reshape(4, 2, 4, 2, 4, tokens, LANES),
        own.reshape(8, 2, tokens, keys),
        other.reshape(8, 2, tokens, keys),
    )
    attended = exchange(attended.reshape(HEADS, 2, tokens, LANES))
    return project_out(attended, gate, out_gate, activations, w_out)


def solution(mesh):
    fine = Mesh(mesh.devices.reshape(2, 4, 4, 2, 2), ("zh", "x", "y", "zl", "co"))
    wide, narrow = ("zh", "x", "y"), ("zl", "co")
    in_specs = (
        P(narrow, wide, None),
        P(narrow, wide, None),
        P(wide, narrow, None),
        P(wide),
    ) + (P(),) * 9
    return jax.shard_map(
        per_device, mesh=fine, in_specs=in_specs, out_specs=P(narrow, wide, None), check_vma=False
    )
```

time: 593 us -> 170 us (0.29)
  matrix products: 167 us -> 0 us
  blocking collectives: 187 us -> 54.1 us
  waiting for transfers between devices: 146 us -> 18.2 us
  Pallas kernels: 0 us -> 71 us
  local copies, waits for them, and re-layouts: 51.1 us -> 3.05 us
  other arithmetic: 25.8 us -> 2.09 us
  starting transfers between devices: 0.09 us -> 7.37 us
    unnamed x1 -> x0, blocking collectives: 187 us -> none
    all_gather x3 -> x1, waiting for transfers between devices: 146 us -> 0.01 us  [per_device(): kv = lax.all_gather(kv, 'y', axis=0)]
    dot_general x16 -> x0, matrix products: 131 us -> none  [the longest x4 52.5 us: one_sample(): jnp.einsum('hqk,khd->qhd', probabilities, sample_values, preferred_elemen...]
    pallas_call x0 -> x5, Pallas kernels: none -> 71 us  [the longest x1 24.8 us: attend(): pl.pallas_call(attend_kernel, grid_spec=pltpu.PrefetchScalarGridSpec(num_...]
    all_to_all x0 -> x2, blocking collectives: none -> 54.1 us  [per_device(): exchange = lambda a: lax.all_to_all(a, XZ, 0, 0, tiled=True)]
    all_gather x3 -> x0, local copies, waits for them, and re-layouts: 38.7 us -> none  [the longest x1 19.4 us: per_device(): lax.all_gather(value_rows, 'wide', axis=1, tiled=True)]
    sub x4 -> x0, matrix products: 35.9 us -> none  [one_sample(): exponent = jnp.exp(scores - row_top)]
    reduce_sum x6 -> x1, other arithmetic: 25.6 us -> 0.11 us  [project_bias(): sums = jnp.sum(wt.astype(F32), axis=1, keepdims=True)]
  transfers between devices with their start and end apart: 3 -> 4, of which waited for: 2 -> 2; matrix products, arithmetic and copies ran while one was open for 7% -> 1% of each run, Pallas kernels for 0% -> 18%
where the time goes in v1:
time: 170 us; the launch traced here: 169 us
  Pallas kernels  71 us (42%)
  blocking collectives  54.1 us (32%)
  waiting for transfers between devices  18.2 us (11%)
  between operations  13.4 us (8%)
  starting transfers between devices  7.37 us (4%)
  local copies, waits for them, and re-layouts  3.05 us (2%)
  other arithmetic  2.09 us (1%)
    all_to_all x2, blocking collectives, per_device(): exchange = lambda a: lax.all_to_all(a, XZ, 0, 0, tiled=True)  54.1 us
    pallas_call x1, Pallas kernels, attend(): pl.pallas_call(attend_kernel, grid_spec=pltpu.PrefetchScalarGridSpec(num_...  24.8 us
    pallas_call x1, Pallas kernels, project_bias(): pl.pallas_call(bias_kernel, grid=(queries // step,), in_specs=[pl.BlockSp...  22.6 us
    all_to_all x2, waiting for transfers between devices, per_device(): exchange = lambda a: lax.all_to_all(a, XZ, 0, 0, tiled=True)  18.2 us
    pallas_call x1, Pallas kernels, project_qkv(): pl.pallas_call(qkv_kernel, grid=(steps,), in_specs=[whole(act), whole(con...  9.51 us
    pallas_call x1, Pallas kernels, gates(): pl.pallas_call(gate_kernel, out_shape=[jax.ShapeDtypeStruct((samples // 2...  8.73 us
    all_to_all x2, starting transfers between devices, per_device(): exchange = lambda a: lax.all_to_all(a, XZ, 0, 0, tiled=True)  7.37 us
    pallas_call x1, Pallas kernels, project_out(): pl.pallas_call(out_kernel, out_shape=jax.ShapeDtypeStruct(act.shape, BF),...  5.37 us
  transfers between devices with their start and end apart: 4, of which 2 were waited for; matrix products, arithmetic and copies ran while one was open for 1% of the time, Pallas kernels for 18%

profile of v1, /device:TPU:0, one launch (start us, length us, event | category | flops | bytes accessed | tf_op | source)
XLA Modules:
  0.0 169.3 jit_solution(6078798902783023421)
XLA Ops:
  6.5 0.0 all-gather.3.cloned.1.call-start
  6.5 0.7 compare_select_fusion
  7.2 0.1 select_convert_fusion.1
  7.3 0.6 pad_maximum_fusion.extra
  7.9 9.5 %qkv.1 = (bf16[16,4,80,128]{3,2,1,0:T(8,128)(2,1)}, bf16[16,2,80,128]{3,2,1,0:T(8,128)(2,1)}, bf16[4,80,768]{2,1,0:T(8,128)(2,1)}, bf16[4,80,384]{2,1,0:T(8,128)(2,1)}) custom-call(bf16[4,80,768]{2,1,0:T(8,128)(2,1)} %act.3, bf16[4,80,384]{2,1,0:T(8,128)(2,1)} %cond.1, bf16[2,80,128]{2,1,0:T(8,128)(2,1)} %pad_maximum_fusion.extra, ...), custom_call_target="tpu_custom_call" | custom-call | flops 4000000000 | bytes 10000000 | tf_op jit(solution)/shard_map/qkv/pallas_call | solution.py:86
  17.4 27.8 %all_to_all.20 = bf16[16,4,80,128]{3,2,1,0:T(8,128)(2,1)} all-to-all(bf16[16,4,80,128]{3,2,1,0:T(8,128)(2,1)} %get-tuple-element.12), channel_id=1, replica_groups=mesh['zh'=2,'x'=4,'y'=4,'zl'=2,'co'=2] {'zh','x','zl'}, dimensions={0} | all-to-all | bytes 2621440 | tf_op jit(solution)/shard_map/all_to_all | solution.py:316
  45.2 0.0 copy-start.3
  45.2 0.0 copy-start.4
  45.2 0.0 copy-start.5
  45.2 0.0 all-gather.3.cloned.1.call-update
  45.3 0.7 copy-done.3
  45.9 0.1 convert_reduce_fusion
  46.0 0.7 copy.16.sums
  46.7 0.0 copy-done.4
  46.7 0.0 copy-done.5
  46.7 0.6 fusion.2.weights
  47.3 22.6 %bias.1 = bf16[16,80,640]{2,1,0:T(8,128)(2,1)} custom-call(bf16[80,640,128]{2,1,0:T(8,128)(2,1)} %pair.1, bf16[32,256]{1,0:T(8,128)(2,1)} %fusion.2.weights, f32[16,1]{1,0:T(8,128)} %copy.16.sums), custom_call_target="tpu_custom_call" | custom-call | flops 10000000000 | bytes 15000000 | tf_op jit(solution)/shard_map/bias/pallas_call | solution.py:138
  69.9 26.3 %all_to_all.21 = bf16[16,80,640]{2,1,0:T(8,128)(2,1)S(1)} all-to-all(bf16[16,80,640]{2,1,0:T(8,128)(2,1)} %bias.1), channel_id=1, replica_groups=mesh['zh'=2,'x'=4,'y'=4,'zl'=2,'co'=2] {'zh','x','zl'}, dimensions={0} | all-to-all | bytes 3276800 | tf_op jit(solution)/shard_map/all_to_all | solution.py:316
  96.2 0.0 copy-start
  96.2 0.0 collective-permute-start
  96.2 3.6 %all-to-all-start = ((bf16[16,2,80,128]{3,2,1,0:T(8,128)(2,1)}), bf16[16,2,80,128]{3,2,1,0:T(8,128)(2,1)S(1)}, u32[]{:S(2)}, u32[]{:S(2)}) async-start(bf16[16,2,80,128]{3,2,1,0:T(8,128)(2,1)} %get-tuple-element.11), calls=%async_computation | async-start | bytes 1310720 | tf_op jit(solution)/shard_map/all_to_all | solution.py:316
  99.8 14.4 %all-to-all-done = bf16[16,2,80,128]{3,2,1,0:T(8,128)(2,1)S(1)} async-done(((bf16[16,2,80,128]{3,2,1,0:T(8,128)(2,1)}), bf16[16,2,80,128]{3,2,1,0:T(8,128)(2,1)S(1)}, u32[]{:S(2)}, u32[]{:S(2)}) %all-to-all-start) | async-done | bytes 655392 | tf_op jit(solution)/shard_map/all_to_all | solution.py:316
  114.3 0.0 copy-start.1
  114.3 0.0 collective-permute-done
  114.3 0.0 all-gather.3.cloned.1.call-done
  114.3 0.0 copy-done
  114.3 0.9 copy-done.1
  115.1 24.8 %attend.1 = bf16[8,2,2,80,128]{4,3,2,1,0:T(8,128)(2,1)} custom-call(s32[1]{0:T(128)} %bitcast.core, bf16[8,2,2,80,128]{4,3,2,1,0:T(8,128)(2,1)} %bitcast.10, bf16[4,2,4,2,4,80,128]{6,5,4,3,2,1,0:T(8,128)(2,1)} %bitcast.14, bf16[8,2,80,640]{3,2,1,0:T(8,128)(2,1)} %bitcast.9, bf16[8,2,80,640]{3,2,1,0:T(8,128)(2,1)} %bitcast.6.other), custom_call_target="tpu_custom_call" | custom-call | flops 14000000000 | bytes 10000000 | tf_op jit(solution)/shard_map/attend/pallas_call | solution.py:205
  139.9 3.8 %all-to-all-start.3 = ((bf16[16,2,80,128]{3,2,1,0:T(8,128)(2,1)}), bf16[16,2,80,128]{3,2,1,0:T(8,128)(2,1)S(1)}, u32[]{:S(2)}, u32[]{:S(2)}) async-start(bf16[16,2,80,128]{3,2,1,0:T(8,128)(2,1)} %bitcast.11), calls=%async_computation.3 | async-start | bytes 1310720 | tf_op jit(solution)/shard_map/all_to_all | solution.py:316
  143.7 8.7 %gates.1 = (f32[2,80,2048]{2,1,0:T(8,128)}, f32[4,80,768]{2,1,0:T(8,128)}) custom-call(bf16[4,80,768]{2,1,0:T(8,128)(2,1)} %get-tuple-element.13.mod, bf16[4,80,384]{2,1,0:T(8,128)(2,1)} %get-tuple-element.14.cn, bf16[768,1024]{1,0:T(8,128)(2,1)} %constant.24.clone.place, bf16[768,768]{1,0:T(8,128)(2,1)} %wg.1, bf16[384,768]{1,0:T(8,128)(2,1)} %wog.1), custom_call_target="tpu_custom_call" | custom-call | flops 4000000000 | bytes 9000000 | tf_op jit(solution)/shard_map/gates/pallas_call | solution.py:244
  152.4 3.8 %all-to-all-done.3.attended = bf16[16,2,80,128]{3,2,1,0:T(8,128)(2,1)S(1)} async-done(((bf16[16,2,80,128]{3,2,1,0:T(8,128)(2,1)}), bf16[16,2,80,128]{3,2,1,0:T(8,128)(2,1)S(1)}, u32[]{:S(2)}, u32[]{:S(2)}) %all-to-all-start.3) | async-done | bytes 655392 | tf_op jit(solution)/shard_map/all_to_all | solution.py:316
  156.2 0.0 copy-start.2
  156.2 0.8 copy-done.2
  157.1 5.4 %out.1 = bf16[4,80,768]{2,1,0:T(8,128)(2,1)} custom-call(bf16[16,2,80,128]{3,2,1,0:T(8,128)(2,1)} %copy-done.2, f32[2,80,2048]{2,1,0:T(8,128)} %get-tuple-element.15.gate, f32[4,80,768]{2,1,0:T(8,128)} %get-tuple-element.16.og, bf16[4,80,768]{2,1,0:T(8,128)(2,1)} %act.3, bf16[768,768]{1,0:T(8,128)(2,1)} %wo.1), custom_call_target="tpu_custom_call" | custom-call | flops 2000000000 | bytes 6000000 | tf_op jit(solution)/shard_map/out/pallas_call | solution.py:278
  (2 shorter events, 0.0 us)
Async XLA Ops:
  6.5 107.7 %all-gather.3.cloned.1.call-start = ((), (), s32[]{:S(2)}) async-start(), calls=%async_computation.4 | async-start | bytes 6553600 | tf_op jit(solution)/shard_map/all_gather | solution.py:318
  45.2 0.7 copy-start.3
  45.2 1.5 copy-start.4
  45.2 1.5 copy-start.5
  96.2 18.0 %copy-start = (bf16[16,80,640]{2,1,0:T(8,128)(2,1)}, bf16[16,80,640]{2,1,0:T(8,128)(2,1)S(1)}, u32[]{:S(2)}) copy-start(bf16[16,80,640]{2,1,0:T(8,128)(2,1)S(1)} %all_to_all.21) | copy-start | bytes 4915204
  96.2 18.0 %collective-permute-start = (bf16[16,80,640]{2,1,0:T(8,128)(2,1)S(1)}, bf16[16,80,640]{2,1,0:T(8,128)(2,1)}, u32[]{:S(2)}, u32[]{:S(2)}) collective-permute-start(bf16[16,80,640]{2,1,0:T(8,128)(2,1)S(1)} %all_to_all.21), channel_id=1, source_target_pairs={{0,1},{1,0},{2,3},{3,2},{4,5},{5,4},{6,7},{7,6},{8,9},{9,8},{10,11... | collective-permute-start | bytes 4915208 | tf_op jit(solution)/shard_map/ppermute | solution.py:321
  96.2 18.0 %all-to-all-start = ((bf16[16,2,80,128]{3,2,1,0:T(8,128)(2,1)}), bf16[16,2,80,128]{3,2,1,0:T(8,128)(2,1)S(1)}, u32[]{:S(2)}, u32[]{:S(2)}) async-start(bf16[16,2,80,128]{3,2,1,0:T(8,128)(2,1)} %get-tuple-element.11), calls=%async_computation | async-start | bytes 1310720 | tf_op jit(solution)/shard_map/all_to_all | solution.py:316
  114.3 0.9 copy-start.1
  139.9 16.3 %all-to-all-start.3 = ((bf16[16,2,80,128]{3,2,1,0:T(8,128)(2,1)}), bf16[16,2,80,128]{3,2,1,0:T(8,128)(2,1)S(1)}, u32[]{:S(2)}, u32[]{:S(2)}) async-start(bf16[16,2,80,128]{3,2,1,0:T(8,128)(2,1)} %bitcast.11), calls=%async_computation.3 | async-start | bytes 1310720 | tf_op jit(solution)/shard_map/all_to_all | solution.py:316
  156.2 0.8 copy-start.2
Sparse Core Ops, SparseCore 0:
  45.4 55.1 all-gather.2

commit v2 on v1

v2 whole, which is shorter than its diff:
```python
import math

import jax
import jax.numpy as jnp
import numpy as np
from jax import lax
from jax.experimental import pallas as pl
from jax.experimental.pallas import tpu as pltpu
from jax.sharding import Mesh, PartitionSpec as P

EPSILON = 1e-05
NEGATIVE = -1e30
LOG2E = math.log2(math.e)
HEADS = 16
HEAD = 48
LANES = 128
GROUP = 8
MARK_LANE = 95
PAD_LANE = 96
SUM_LANE = 97
XZ = ("zh", "x", "zl")
BF = jnp.bfloat16
F32 = jnp.float32
VMEM_BYTES = 56 * 1024 * 1024
NT = (((1,), (1,)), ((), ()))


def layer_norm(entries):
    entries = entries.astype(F32)
    row_mean = jnp.mean(entries, axis=-1, keepdims=True)
    centered = entries - row_mean
    variance = jnp.mean(centered * centered, axis=-1, keepdims=True)
    return centered * lax.rsqrt(variance + EPSILON)


def dot(left, right):
    return jnp.dot(left, right, preferred_element_type=F32)


def placement():
    table = np.zeros((2, 2, GROUP, HEAD, GROUP, LANES), np.float32)
    for head in range(GROUP):
        for channel in range(HEAD):
            for which, offset in ((0, HEAD), (1, 64)):
                table[which, 0, head, channel, head, channel] = 1
                table[which, 1, head, channel, head, offset + channel] = 1
    table = table.reshape(2, 2 * GROUP * HEAD, GROUP * LANES)
    return jnp.asarray(table[0], BF), jnp.asarray(table[1], BF)


def qkv_kernel(act, cond, mask, kv_place, q_place, ws, wsh, wq, wk, wv, kv_out, q_out, mod_out, cn_out, mod):
    samples, tokens, width = act.shape
    rows = samples * tokens

    @pl.when(pl.program_id(0) == 0)
    def _():
        cond_norm = layer_norm(cond[...].reshape(rows, cond.shape[2])).astype(BF)
        normed = layer_norm(act[...].reshape(rows, width))
        modulated = jax.nn.sigmoid(dot(cond_norm, ws[...])) * normed + dot(cond_norm, wsh[...])
        mod[...] = modulated.astype(BF)
        mod_out[...] = mod[...].reshape(mod_out.shape)
        cn_out[...] = cond_norm.reshape(cn_out.shape)

    modulated = mod[...]
    k = dot(modulated, wk[...]).astype(BF)
    v = dot(modulated, wv[...]).astype(BF)
    placed = dot(jnp.concatenate([k, v], axis=1), kv_place[...])
    lane = lax.broadcasted_iota(jnp.int32, (tokens, LANES), 1)
    square = (tokens, tokens)
    diagonal = lax.broadcasted_iota(jnp.int32, square, 0) == lax.broadcasted_iota(jnp.int32, square, 1)
    padded = jnp.broadcast_to(jnp.where(mask[...] > 0, 0.0, 1.0), square)
    padded = jnp.sum(jnp.where(diagonal, padded, 0.0), axis=1, keepdims=True)
    marked = (lane == MARK_LANE) & (padded > 0.5)
    for h in range(GROUP):
        tile = placed[:, h * LANES:(h + 1) * LANES]
        last = tile[3 * tokens:]
        for s in range(3):
            spare = pltpu.roll(last, 96 - 32 * s, axis=1)
            merged = jnp.where(lane < 96, tile[s * tokens:(s + 1) * tokens], spare)
            if s == 0:
                merged = jnp.where(marked, NEGATIVE, merged)
            kv_out[h, :, s * LANES:(s + 1) * LANES] = merged.astype(BF)
    q = (dot(modulated, wq[...]) * (LOG2E / math.sqrt(HEAD))).astype(BF)
    first = jnp.concatenate([q[:tokens], q[2 * tokens:3 * tokens]], axis=0)
    second = jnp.concatenate([q[tokens:2 * tokens], q[3 * tokens:]], axis=0)
    placed = dot(jnp.concatenate([first, second], axis=1), q_place[...]).astype(BF)
    for p in range(samples // 2):
        for h in range(GROUP):
            q_out[h, :, p * LANES:(p + 1) * LANES] = placed[p * tokens:(p + 1) * tokens, h * LANES:(h + 1) * LANES]


def project_qkv(act, cond, mask, kv_place, q_place, ws, wsh, wq, wk, wv):
    samples, tokens, width = act.shape
    steps = HEADS // GROUP
    columns = GROUP * HEAD
    whole = lambda a: pl.BlockSpec(a.shape, lambda g: (0,) * a.ndim)
    part = pl.BlockSpec((width, columns), lambda g: (0, g))
    return pl.pallas_call(
        qkv_kernel,
        grid=(steps,),
        in_specs=[whole(act), whole(cond), whole(mask), whole(kv_place), whole(q_place), whole(ws), whole(wsh), part, part, part],
        out_specs=[
            pl.BlockSpec((GROUP, tokens, 3 * LANES), lambda g: (g, 0, 0)),
            pl.BlockSpec((GROUP, tokens, 2 * LANES), lambda g: (g, 0, 0)),
            whole(act),
            whole(cond),
        ],
        out_shape=[
            jax.ShapeDtypeStruct((HEADS, tokens, 3 * LANES), BF),
            jax.ShapeDtypeStruct((HEADS, tokens, 2 * LANES), BF),
            jax.ShapeDtypeStruct(act.shape, BF),
            jax.ShapeDtypeStruct(cond.shape, BF),
        ],
        scratch_shapes=[pltpu.VMEM((samples * tokens, width), BF)],
        compiler_params=pltpu.CompilerParams(vmem_limit_bytes=VMEM_BYTES),
        cost_estimate=pl.CostEstimate(flops=4_000_000_000, bytes_accessed=10_000_000, transcendentals=300_000),
        name="qkv",
    )(act, cond, mask, kv_place, q_place, ws, wsh, wq, wk, wv)


def bias_kernel(pair, w_bias, q, out, rows):
    count, keys, channels = pair.shape
    wt = w_bias[...].astype(F32).T.astype(BF)
    zero = jnp.zeros((HEADS, channels), BF)
    part = jnp.full((HEADS, channels), 1.0 / channels, BF)
    weights = jnp.concatenate(
        [jnp.concatenate([wt, zero], axis=1), jnp.concatenate([zero, part], axis=1)], axis=0
    )
    for i in range(count):
        x = pair[i].astype(F32)
        c = (x - jnp.mean(x, axis=1, keepdims=True)).astype(BF)
        both = jnp.concatenate([c, c * c], axis=1)
        r = lax.dot_general(weights, both, NT, preferred_element_type=F32)
        rows[i] = r[:HEADS] * (lax.rsqrt(r[HEADS:] + EPSILON) * LOG2E)
    out[:, :, :keys] = jnp.swapaxes(rows[...], 0, 1).astype(BF)
    out[:, :, keys:] = q[...]


def project_bias(pair, w_bias, q):
    queries, keys, channels = pair.shape
    step = 16
    extent = keys + q.shape[2]
    return pl.pallas_call(
        bias_kernel,
        grid=(queries // step,),
        in_specs=[
            pl.BlockSpec((step, keys, channels), lambda i: (i, 0, 0)),
            pl.BlockSpec(w_bias.shape, lambda i: (0, 0)),
            pl.BlockSpec((HEADS, step, q.shape[2]), lambda i: (0, i, 0)),
        ],
        out_specs=pl.BlockSpec((HEADS, step, extent), lambda i: (0, i, 0)),
        out_shape=jax.ShapeDtypeStruct((HEADS, queries, extent), BF),
        scratch_shapes=[pltpu.VMEM((step, HEADS, keys), F32)],
        compiler_params=pltpu.CompilerParams(vmem_limit_bytes=VMEM_BYTES),
        cost_estimate=pl.CostEstimate(flops=10_000_000_000, bytes_accessed=15_000_000, transcendentals=100_000),
        name="bias",
    )(pair, w_bias, q)


T = 4


def attend_kernel(core, q, kv, own, other, out, keys):
    tokens = q.shape[2]
    chunk = 8 * tokens
    me = core[0]
    lane_k = lax.broadcasted_iota(jnp.int32, (tokens, LANES), 1)

    @pl.when(pl.program_id(1) == 0)
    def _():
        for z in range(2):
            for o in range(2):
                quarter = me if o == 0 else 1 - me
                for low in range(2):
                    for y in range(4):
                        block = low * 4 + y
                        at = (z * 2 + o) * chunk + block * tokens
                        tiles = [kv[y, z, 2 * quarter + low, 0, :, i * LANES:(i + 1) * LANES] for i in range(3)]
                        wide = [t.astype(F32) for t in tiles]
                        pad = jnp.where(pltpu.roll(wide[0], PAD_LANE - MARK_LANE, axis=1) < 0.5 * NEGATIVE, NEGATIVE, 0.0)
                        tail = jnp.where(lane_k == PAD_LANE, pad, jnp.where(lane_k == SUM_LANE, 1.0, 0.0)).astype(BF)
                        for s in range(3):
                            keys[s, at:at + tokens] = jnp.where(lane_k < 96, tiles[s], tail)
                        last = jnp.where(
                            lane_k < 32,
                            pltpu.roll(wide[0], 32, axis=1),
                            jnp.where(lane_k < 64, pltpu.roll(wide[1], 64, axis=1), pltpu.roll(wide[2], 96, axis=1)),
                        ).astype(BF)
                        keys[3, at:at + tokens] = jnp.where(lane_k < 96, last, tail)

    first_sample = 2 * pl.program_id(1)
    span = T * tokens
    lane = lax.broadcasted_iota(jnp.int32, (span, LANES), 1)
    pad_one = jnp.where(lane == PAD_LANE, 1.0, 0.0).astype(BF)
    blocks = [(t, s) for t in range(8 // T) for s in range(2)]

    def scores_of(t, s, c):
        pair_q = q[t * T:(t + 1) * T, 0].reshape(span, LANES)
        if s == 1:
            pair_q = pltpu.roll(pair_q.astype(F32), 64, axis=1).astype(BF)
        mine = jnp.where(lane < HEAD, pair_q, pad_one)
        part = lax.dot_general(
            mine, keys[first_sample + s, c * chunk:(c + 1) * chunk], NT, preferred_element_type=F32
        )
        b = (own if c % 2 == 0 else other)[t * T:(t + 1) * T, c // 2].reshape(span, chunk)
        return part + b.astype(F32)

    current = [scores_of(*blocks[0], c) for c in range(4)]
    for i, (t, s) in enumerate(blocks):
        tops = [jnp.max(part, axis=1, keepdims=True) for part in current]
        top = jnp.maximum(jnp.maximum(tops[0], tops[1]), jnp.maximum(tops[2], tops[3]))
        following, total = [], None
        for c in range(4):
            if i + 1 < len(blocks):
                following.append(scores_of(*blocks[i + 1], c))
            p = jnp.exp2(current[c] - top).astype(BF)
            part = dot(p, keys[first_sample + s, c * chunk:(c + 1) * chunk])
            total = part if total is None else total + part
        current = following
        result = total / total[:, SUM_LANE:SUM_LANE + 1]
        if s == 0:
            low = pltpu.roll(result, LANES - HEAD, axis=1)
        else:
            high = pltpu.roll(result, 64 - HEAD, axis=1)
            merged = jnp.where(lane < 64, low, high).astype(BF)
            out[t * T:(t + 1) * T, 0] = merged.reshape(T, tokens, LANES)


def attend(core, kv, own, other):
    tokens = own.shape[2]
    chunk = 8 * tokens
    b_spec = pl.BlockSpec((8, 2, tokens, chunk), lambda z, p, c: (0, 0, 0, 0))
    return pl.pallas_call(
        attend_kernel,
        grid_spec=pltpu.PrefetchScalarGridSpec(
            num_scalar_prefetch=1,
            grid=(2, 2),
            in_specs=[
                pl.BlockSpec((8, 1, tokens, LANES), lambda z, p, c: (0, z, 0, chunk // LANES + p)),
                pl.BlockSpec((4, 2, 4, 1, tokens, 3 * LANES), lambda z, p, c: (0, 0, 0, z, 0, 0)),
                b_spec,
                b_spec,
            ],
            out_specs=pl.BlockSpec((8, 1, tokens, LANES), lambda z, p, c: (0, z, 0, p)),
            scratch_shapes=[pltpu.VMEM((4, 4 * chunk, LANES), BF)],
        ),
        out_shape=jax.ShapeDtypeStruct((8, 2, tokens, 2 * LANES), BF),
        compiler_params=pltpu.CompilerParams(vmem_limit_bytes=VMEM_BYTES),
        cost_estimate=pl.CostEstimate(flops=14_000_000_000, bytes_accessed=10_000_000, transcendentals=13_000_000),
        name="attend",
    )(core, own, kv, own, other)


def gate_kernel(mod, cn, place, wg, wog, gate_out, og_out):
    samples, tokens, width = mod.shape
    rows = samples * tokens
    og_out[...] = jax.nn.sigmoid(dot(cn[...].reshape(rows, cn.shape[2]), wog[...])).reshape(og_out.shape)
    columns = GROUP * HEAD
    low = place[0:columns]
    high = place[columns:2 * columns]
    for g in range(HEADS // GROUP):
        w = wg[:, g * columns:(g + 1) * columns]
        w_low = dot(w, low).astype(BF)
        w_high = dot(w, high).astype(BF)
        for p in range(samples // 2):
            value = dot(mod[2 * p], w_low) + dot(mod[2 * p + 1], w_high)
            gate_out[p, :, g * GROUP * LANES:(g + 1) * GROUP * LANES] = jax.nn.sigmoid(value)


def gates(mod, cn, place, wg, wog):
    samples, tokens, width = mod.shape
    return pl.pallas_call(
        gate_kernel,
        out_shape=[
            jax.ShapeDtypeStruct((samples // 2, tokens, HEADS * LANES), F32),
            jax.ShapeDtypeStruct(mod.shape, F32),
        ],
        compiler_params=pltpu.CompilerParams(vmem_limit_bytes=VMEM_BYTES),
        cost_estimate=pl.CostEstimate(flops=4_000_000_000, bytes_accessed=9_000_000, transcendentals=1_000_000),
        name="gates",
    )(mod, cn, place, wg, wog)


def out_kernel(attended, gate, og, act, wo, out, low, high):
    samples, tokens, width = act.shape
    low[...] = jnp.zeros_like(low)
    high[...] = jnp.zeros_like(high)
    for h in range(HEADS):
        rows = wo[h * HEAD:(h + 1) * HEAD]
        low[h * LANES:h * LANES + HEAD] = rows
        high[h * LANES + 64:h * LANES + 64 + HEAD] = rows
    for p in range(samples // 2):
        gated = jnp.concatenate(
            [
                (attended[h, :, p * LANES:(p + 1) * LANES].astype(F32) * gate[p, :, h * LANES:(h + 1) * LANES]).astype(BF)
                for h in range(HEADS)
            ],
            axis=1,
        )
        for s, table in ((2 * p, low), (2 * p + 1, high)):
            out[s] = (act[s].astype(F32) + og[s] * dot(gated, table[...])).astype(BF)


def project_out(attended, gate, og, act, wo):
    width = act.shape[2]
    return pl.pallas_call(
        out_kernel,
        out_shape=jax.ShapeDtypeStruct(act.shape, BF),
        scratch_shapes=[pltpu.VMEM((HEADS * LANES, width), BF)] * 2,
        compiler_params=pltpu.CompilerParams(vmem_limit_bytes=VMEM_BYTES),
        cost_estimate=pl.CostEstimate(flops=2_000_000_000, bytes_accessed=6_000_000, transcendentals=0),
        name="out",
    )(attended, gate, og, act, wo)


def per_device(
    activations,
    conditioning,
    pair_features,
    key_mask,
    w_scale,
    w_shift,
    w_query,
    w_key,
    w_value,
    w_gate,
    w_out,
    w_outgate,
    w_bias,
):
    tokens = activations.shape[1]
    kv_place, q_place = placement()
    kv, q, modulated, cond_norm = project_qkv(
        activations, conditioning, key_mask.reshape(1, tokens), kv_place, q_place, w_scale, w_shift, w_query, w_key, w_value
    )
    exchange = lambda a: lax.all_to_all(a, XZ, 0, 0, tiled=True)
    bias = project_bias(pair_features, w_bias, q)
    kv, bias = lax.optimization_barrier((exchange(kv), bias))
    kv = lax.all_gather(kv, "y", axis=0)
    own = exchange(bias)
    other = lax.ppermute(own, "co", [(0, 1), (1, 0)])
    gate, out_gate = gates(modulated, cond_norm, q_place, w_gate, w_outgate)
    other, gate, out_gate = lax.optimization_barrier((other, gate, out_gate))
    core = lax.axis_index("co").astype(jnp.int32).reshape(1)
    attended = attend(
        core,
        kv.reshape(4, 2, 4, 2, tokens, kv.shape[-1]),
        own.reshape(8, 2, tokens, own.shape[-1]),
        other.reshape(8, 2, tokens, own.shape[-1]),
    )
    attended = exchange(attended.reshape(HEADS, tokens, 2 * LANES))
    return project_out(attended, gate, out_gate, activations, w_out)


def solution(mesh):
    fine = Mesh(mesh.devices.reshape(2, 4, 4, 2, 2), ("zh", "x", "y", "zl", "co"))
    wide, narrow = ("zh", "x", "y"), ("zl", "co")
    in_specs = (
        P(narrow, wide, None),
        P(narrow, wide, None),
        P(wide, narrow, None),
        P(wide),
    ) + (P(),) * 9
    return jax.shard_map(
        per_device, mesh=fine, in_specs=in_specs, out_specs=P(narrow, wide, None), check_vma=False
    )
```

time: 170 us -> 141 us (0.83)
  Pallas kernels: 71 us -> 58.7 us
  waiting for transfers between devices: 18.2 us -> 6.19 us
  other arithmetic: 2.09 us -> 0 us
  blocking collectives: 54.1 us -> 52.2 us
    all_to_all x2 -> x1, waiting for transfers between devices: 18.2 us -> 4.64 us  [per_device(): exchange = lambda a: lax.all_to_all(a, XZ, 0, 0, tiled=True)]
    pallas_call x1, Pallas kernels: 22.6 us -> 11.7 us  [project_bias(): pl.pallas_call(bias_kernel, grid=(queries // step,), in_specs=[pl.BlockSp...]
    all_to_all x2, blocking collectives: 54.1 us -> 52.2 us  [per_device(): exchange = lambda a: lax.all_to_all(a, XZ, 0, 0, tiled=True)]
    all_to_all x2 -> x1, starting transfers between devices: 7.37 us -> 7.97 us  [per_device(): exchange = lambda a: lax.all_to_all(a, XZ, 0, 0, tiled=True)]
  transfers between devices with their start and end apart: 4 -> 3, of which waited for: 2 -> 2; matrix products, arithmetic and copies ran while one was open for 1% -> 1% of each run, Pallas kernels for 18% -> 15%
where the time goes in v2:
time: 141 us; the launch traced here: 140 us
  Pallas kernels  58.7 us (42%)
  blocking collectives  52.2 us (37%)
  between operations  13.4 us (10%)
  starting transfers between devices  8.01 us (6%)
  waiting for transfers between devices  6.19 us (4%)
  local copies, waits for them, and re-layouts  1.68 us (1%)
    all_to_all x2, blocking collectives, per_device(): exchange = lambda a: lax.all_to_all(a, XZ, 0, 0, tiled=True)  52.2 us
    pallas_call x1, Pallas kernels, attend(): pl.pallas_call(attend_kernel, grid_spec=pltpu.PrefetchScalarGridSpec(num_...  23.5 us
    pallas_call x1, Pallas kernels, project_bias(): pl.pallas_call(bias_kernel, grid=(queries // step,), in_specs=[pl.BlockSp...  11.7 us
    pallas_call x1, Pallas kernels, gates(): pl.pallas_call(gate_kernel, out_shape=[jax.ShapeDtypeStruct((samples // 2...  9.69 us
    pallas_call x1, Pallas kernels, project_qkv(): pl.pallas_call(qkv_kernel, grid=(steps,), in_specs=[whole(act), whole(con...  8.45 us
    all_to_all x1, starting transfers between devices, per_device(): exchange = lambda a: lax.all_to_all(a, XZ, 0, 0, tiled=True)  7.97 us
    pallas_call x1, Pallas kernels, project_out(): pl.pallas_call(out_kernel, out_shape=jax.ShapeDtypeStruct(act.shape, BF),...  5.37 us
    all_to_all x1, waiting for transfers between devices, per_device(): exchange = lambda a: lax.all_to_all(a, XZ, 0, 0, tiled=True)  4.64 us
  transfers between devices with their start and end apart: 3, of which 2 were waited for; matrix products, arithmetic and copies ran while one was open for 1% of the time, Pallas kernels for 15%

profile of v2, /device:TPU:0, one launch (start us, length us, event | category | flops | bytes accessed | tf_op | source)
XLA Modules:
  0.0 140.2 jit_solution(11881781588210792356)
XLA Ops:
  6.5 8.4 %qkv.1 = (bf16[16,80,384]{2,1,0:T(8,128)(2,1)}, bf16[16,80,256]{2,1,0:T(8,128)(2,1)}, bf16[4,80,768]{2,1,0:T(8,128)(2,1)}, bf16[4,80,384]{2,1,0:T(8,128)(2,1)}) custom-call(bf16[4,80,768]{2,1,0:T(8,128)(2,1)} %act.3, bf16[4,80,384]{2,1,0:T(8,128)(2,1)} %cond.1, s32[1,80]{1,0:T(1,128)} %bitcast.10, bf16[768,1024]{1,0:T(8,128)(2,1)} %constant.8.clone.kv_place, ...), custom_call_target="tpu_custom_call" | custom-call | flops 4000000000 | bytes 10000000 | tf_op jit(solution)/shard_map/qkv/pallas_call | solution.py:98
  15.0 0.0 copy-start.2
  15.0 8.0 %all-to-all-start = ((bf16[16,80,384]{2,1,0:T(8,128)(2,1)}), bf16[16,80,384]{2,1,0:T(8,128)(2,1)S(1)}, u32[]{:S(2)}, u32[]{:S(2)}) async-start(bf16[16,80,384]{2,1,0:T(8,128)(2,1)} %get-tuple-element.16), calls=%async_computation | async-start | bytes 1966080 | tf_op jit(solution)/shard_map/all_to_all | solution.py:336
  23.0 0.0 all-gather.3.cloned.1.call-start
  23.0 0.0 copy-done.2
  23.0 0.7 copy.17.w_bias
  23.7 11.7 %bias.1 = bf16[16,80,896]{2,1,0:T(8,128)(2,1)} custom-call(bf16[80,640,128]{2,1,0:T(8,128)(2,1)} %pair.1, bf16[128,16]{1,0:T(8,128)(2,1)} %copy.17.w_bias, bf16[16,80,256]{2,1,0:T(8,128)(2,1)} %get-tuple-element.17.q), custom_call_target="tpu_custom_call" | custom-call | flops 10000000000 | bytes 15000000 | tf_op jit(solution)/shard_map/bias/pallas_call | solution.py:143
  35.4 4.6 %all-to-all-done = bf16[16,80,384]{2,1,0:T(8,128)(2,1)S(1)} async-done(((bf16[16,80,384]{2,1,0:T(8,128)(2,1)}), bf16[16,80,384]{2,1,0:T(8,128)(2,1)S(1)}, u32[]{:S(2)}, u32[]{:S(2)}) %all-to-all-start) | async-done | bytes 983072 | tf_op jit(solution)/shard_map/all_to_all | solution.py:336
  40.0 0.0 copy-start
  40.0 1.0 copy-done
  41.0 0.0 all-gather.3.cloned.1.call-update
  41.0 32.4 %all_to_all.15 = bf16[16,80,896]{2,1,0:T(8,128)(2,1)S(1)} all-to-all(bf16[16,80,896]{2,1,0:T(8,128)(2,1)} %bias.1), channel_id=1, replica_groups=mesh['zh'=2,'x'=4,'y'=4,'zl'=2,'co'=2] {'zh','x','zl'}, dimensions={0} | all-to-all | bytes 4587520 | tf_op jit(solution)/shard_map/all_to_all | solution.py:336
  73.5 0.0 copy-start.1
  73.5 0.0 collective-permute-start
  73.5 9.7 %gates.1 = (f32[2,80,2048]{2,1,0:T(8,128)}, f32[4,80,768]{2,1,0:T(8,128)}) custom-call(bf16[4,80,768]{2,1,0:T(8,128)(2,1)} %get-tuple-element.20.mod, bf16[4,80,384]{2,1,0:T(8,128)(2,1)} %get-tuple-element.21.cn, bf16[768,1024]{1,0:T(8,128)(2,1)} %constant.9.clone.q_place.place, bf16[768,768]{1,0:T(8,128)(2,1)} %wg.1, bf16[384,768]{1,0:T(8,128)(2,1)} %wog.1), custom_call_target="tpu_custom_call" | custom-call | flops 4000000000 | bytes 9000000 | tf_op jit(solution)/shard_map/gates/pallas_call | solution.py:272
  83.2 0.0 copy-done.1
  83.2 0.0 collective-permute-done
  83.2 1.5 %all-gather.3.cloned.1.call-done = bf16[64,80,384]{2,1,0:T(8,128)(2,1)} async-done(((bf16[16,80,384]{2,1,0:T(8,128)(2,1)}), bf16[64,80,384]{2,1,0:T(8,128)(2,1)}) %all-gather.3.cloned.1.call-update) | async-done | bytes 3932176 | tf_op jit(solution)/shard_map/all_gather | solution.py:339
  84.7 23.5 %attend.1 = bf16[8,2,80,256]{3,2,1,0:T(8,128)(2,1)} custom-call(s32[1]{0:T(128)} %bitcast.core, bf16[8,2,80,896]{3,2,1,0:T(8,128)(2,1)} %bitcast.6, bf16[4,2,4,2,80,384]{5,4,3,2,1,0:T(8,128)(2,1)} %bitcast.9, bf16[8,2,80,896]{3,2,1,0:T(8,128)(2,1)} %bitcast.7, bf16[8,2,80,896]{3,2,1,0:T(8,128)(2,1)} %bitcast.4.other), custom_call_target="tpu_custom_call" | custom-call | flops 14000000000 | bytes 10000000 | tf_op jit(solution)/shard_map/attend/pallas_call | solution.py:233
  108.2 19.8 %all_to_all.16.attended = bf16[16,80,256]{2,1,0:T(8,128)(2,1)} all-to-all(bf16[16,80,256]{2,1,0:T(8,128)(2,1)} %bitcast.8), channel_id=1, replica_groups=mesh['zh'=2,'x'=4,'y'=4,'zl'=2,'co'=2] {'zh','x','zl'}, dimensions={0} | all-to-all | bytes 1310720 | tf_op jit(solution)/shard_map/all_to_all | solution.py:336
  128.0 5.4 %out.1 = bf16[4,80,768]{2,1,0:T(8,128)(2,1)} custom-call(bf16[16,80,256]{2,1,0:T(8,128)(2,1)} %all_to_all.16.attended, f32[2,80,2048]{2,1,0:T(8,128)} %get-tuple-element.25.gate, f32[4,80,768]{2,1,0:T(8,128)} %get-tuple-element.26.og, bf16[4,80,768]{2,1,0:T(8,128)(2,1)} %act.3, bf16[768,768]{1,0:T(8,128)(2,1)} %wo.1), custom_call_target="tpu_custom_call" | custom-call | flops 2000000000 | bytes 6000000 | tf_op jit(solution)/shard_map/out/pallas_call | solution.py:306
Async XLA Ops:
  15.0 8.0 %copy-start.2 = (bf16[128,16]{0,1:T(8,128)(2,1)S(1)}, bf16[128,16]{0,1:T(8,128)(2,1)}, u32[]{:S(2)}) copy-start(bf16[128,16]{0,1:T(8,128)(2,1)} %param.27) | copy-start | bytes 12292
  15.0 25.1 %all-to-all-start = ((bf16[16,80,384]{2,1,0:T(8,128)(2,1)}), bf16[16,80,384]{2,1,0:T(8,128)(2,1)S(1)}, u32[]{:S(2)}, u32[]{:S(2)}) async-start(bf16[16,80,384]{2,1,0:T(8,128)(2,1)} %get-tuple-element.16), calls=%async_computation | async-start | bytes 1966080 | tf_op jit(solution)/shard_map/all_to_all | solution.py:336
  23.0 61.7 %all-gather.3.cloned.1.call-start = ((), (), s32[]{:S(2)}) async-start(), calls=%async_computation.3 | async-start | bytes 4915200 | tf_op jit(solution)/shard_map/all_gather | solution.py:339
  40.0 1.0 copy-start
  73.5 9.7 %copy-start.1 = (bf16[16,80,896]{2,1,0:T(8,128)(2,1)}, bf16[16,80,896]{2,1,0:T(8,128)(2,1)S(1)}, u32[]{:S(2)}) copy-start(bf16[16,80,896]{2,1,0:T(8,128)(2,1)S(1)} %all_to_all.15) | copy-start | bytes 6881284
  73.5 9.7 %collective-permute-start = (bf16[16,80,896]{2,1,0:T(8,128)(2,1)S(1)}, bf16[16,80,896]{2,1,0:T(8,128)(2,1)}, u32[]{:S(2)}, u32[]{:S(2)}) collective-permute-start(bf16[16,80,896]{2,1,0:T(8,128)(2,1)S(1)} %all_to_all.15), channel_id=1, source_target_pairs={{0,1},{1,0},{2,3},{3,2},{4,5},{5,4},{6,7},{7,6},{8,9},{9,8},{10,11... | collective-permute-start | bytes 6881288 | tf_op jit(solution)/shard_map/ppermute | solution.py:341
Sparse Core Ops, SparseCore 0:
  41.1 43.5 all-gather.2

commit v3 on v2

--- a/solution.py
+++ b/solution.py
@@ -120,7 +120,7 @@
 
 def bias_kernel(pair, w_bias, q, out, rows):
     count, keys, channels = pair.shape
-    wt = w_bias[...].astype(F32).T.astype(BF)
+    wt = w_bias[...]
     zero = jnp.zeros((HEADS, channels), BF)
     part = jnp.full((HEADS, channels), 1.0 / channels, BF)
     weights = jnp.concatenate(
@@ -160,33 +160,34 @@
 T = 4
 
 
-def attend_kernel(core, q, kv, own, other, out, keys):
+def attend_kernel(place, q, near, up, far_low, far_high, down, own, other, out, keys):
     tokens = q.shape[2]
     chunk = 8 * tokens
-    me = core[0]
+    core, row = place[0], place[1]
     lane_k = lax.broadcasted_iota(jnp.int32, (tokens, LANES), 1)
 
     @pl.when(pl.program_id(1) == 0)
     def _():
         for z in range(2):
+            sources = (near.at[z], up.at[z], (far_low, far_high)[z].at[0], down.at[z])
             for o in range(2):
-                quarter = me if o == 0 else 1 - me
+                quarter = core if o == 0 else 1 - core
                 for low in range(2):
-                    for y in range(4):
-                        block = low * 4 + y
-                        at = (z * 2 + o) * chunk + block * tokens
-                        tiles = [kv[y, z, 2 * quarter + low, 0, :, i * LANES:(i + 1) * LANES] for i in range(3)]
+                    for step, source in enumerate(sources):
+                        block = low * 4 + lax.rem(row + 4 - step, 4)
+                        at = pl.ds(pl.multiple_of((z * 2 + o) * chunk + block * tokens, 16), tokens)
+                        tiles = [source[2 * quarter + low, 0, :, i * LANES:(i + 1) * LANES] for i in range(3)]
                         wide = [t.astype(F32) for t in tiles]
                         pad = jnp.where(pltpu.roll(wide[0], PAD_LANE - MARK_LANE, axis=1) < 0.5 * NEGATIVE, NEGATIVE, 0.0)
                         tail = jnp.where(lane_k == PAD_LANE, pad, jnp.where(lane_k == SUM_LANE, 1.0, 0.0)).astype(BF)
                         for s in range(3):
-                            keys[s, at:at + tokens] = jnp.where(lane_k < 96, tiles[s], tail)
+                            keys[s, at] = jnp.where(lane_k < 96, tiles[s], tail)
                         last = jnp.where(
                             lane_k < 32,
                             pltpu.roll(wide[0], 32, axis=1),
                             jnp.where(lane_k < 64, pltpu.roll(wide[1], 64, axis=1), pltpu.roll(wide[2], 96, axis=1)),
                         ).astype(BF)
-                        keys[3, at:at + tokens] = jnp.where(lane_k < 96, last, tail)
+                        keys[3, at] = jnp.where(lane_k < 96, last, tail)
 
     first_sample = 2 * pl.program_id(1)
     span = T * tokens
@@ -226,7 +227,7 @@
             out[t * T:(t + 1) * T, 0] = merged.reshape(T, tokens, LANES)
 
 
-def attend(core, kv, own, other):
+def attend(place, kv, own, other):
     tokens = own.shape[2]
     chunk = 8 * tokens
     b_spec = pl.BlockSpec((8, 2, tokens, chunk), lambda z, p, c: (0, 0, 0, 0))
@@ -237,7 +238,9 @@
             grid=(2, 2),
             in_specs=[
                 pl.BlockSpec((8, 1, tokens, LANES), lambda z, p, c: (0, z, 0, chunk // LANES + p)),
-                pl.BlockSpec((4, 2, 4, 1, tokens, 3 * LANES), lambda z, p, c: (0, 0, 0, z, 0, 0)),
+            ]
+            + [pl.BlockSpec((a.shape[0], 4, 1, tokens, 3 * LANES), lambda z, p, c: (0, 0, z, 0, 0)) for a in kv]
+            + [
                 b_spec,
                 b_spec,
             ],
@@ -248,7 +251,7 @@
         compiler_params=pltpu.CompilerParams(vmem_limit_bytes=VMEM_BYTES),
         cost_estimate=pl.CostEstimate(flops=14_000_000_000, bytes_accessed=10_000_000, transcendentals=13_000_000),
         name="attend",
-    )(core, own, kv, own, other)
+    )(place, own, *kv, own, other)
 
 
 def gate_kernel(mod, cn, place, wg, wog, gate_out, og_out):
@@ -311,6 +314,10 @@
         cost_estimate=pl.CostEstimate(flops=2_000_000_000, bytes_accessed=6_000_000, transcendentals=0),
         name="out",
     )(attended, gate, og, act, wo)
+
+
+def ring(block, step):
+    return lax.ppermute(block, "y", [(i, (i + step) % 4) for i in range(4)])
 
 
 def per_device(
@@ -334,17 +341,18 @@
         activations, conditioning, key_mask.reshape(1, tokens), kv_place, q_place, w_scale, w_shift, w_query, w_key, w_value
     )
     exchange = lambda a: lax.all_to_all(a, XZ, 0, 0, tiled=True)
-    bias = project_bias(pair_features, w_bias, q)
+    bias = project_bias(pair_features, w_bias.T, q)
     kv, bias = lax.optimization_barrier((exchange(kv), bias))
-    kv = lax.all_gather(kv, "y", axis=0)
+    up, down = ring(kv, 1), ring(kv, 3)
+    far = (ring(up[:HEADS // 2], 1), ring(down[HEADS // 2:], 3))
     own = exchange(bias)
+    gate, out_gate = gates(modulated, cond_norm, q_place, w_gate, w_outgate)
+    own, up, down, far, gate, out_gate = lax.optimization_barrier((own, up, down, far, gate, out_gate))
     other = lax.ppermute(own, "co", [(0, 1), (1, 0)])
-    gate, out_gate = gates(modulated, cond_norm, q_place, w_gate, w_outgate)
-    other, gate, out_gate = lax.optimization_barrier((other, gate, out_gate))
-    core = lax.axis_index("co").astype(jnp.int32).reshape(1)
+    place = jnp.stack([lax.axis_index("co"), lax.axis_index("y")]).astype(jnp.int32)
     attended = attend(
-        core,
-        kv.reshape(4, 2, 4, 2, tokens, kv.shape[-1]),
+        place,
+        [a.reshape(-1, 4, 2, tokens, kv.shape[-1]) for a in (kv, up, *far, down)],
         own.reshape(8, 2, tokens, own.shape[-1]),
         other.reshape(8, 2, tokens, own.shape[-1]),
     )

time: 141 us -> 129 us (0.915)
  blocking collectives: 52.2 us -> 19.7 us
  waiting for transfers between devices: 6.19 us -> 29.5 us
  between operations: 13.4 us -> 0.07 us
  starting transfers between devices: 8.01 us -> 18.9 us
    all_to_all x2 -> x1, blocking collectives: 52.2 us -> 19.7 us  [per_device(): exchange = lambda a: lax.all_to_all(a, XZ, 0, 0, tiled=True)]
    ppermute x0 -> x4, waiting for transfers between devices: none -> 20.7 us  [ring(): return lax.ppermute(block, 'y', [(i, (i + step) % 4) for i in range(4)])]
    ppermute x0 -> x4, starting transfers between devices: none -> 6.92 us  [ring(): return lax.ppermute(block, 'y', [(i, (i + step) % 4) for i in range(4)])]
    all_to_all x1 -> x2, starting transfers between devices: 7.97 us -> 11.7 us  [per_device(): exchange = lambda a: lax.all_to_all(a, XZ, 0, 0, tiled=True)]
    ppermute x1, waiting for transfers between devices: 0.01 us -> 3.64 us  [per_device(): other = lax.ppermute(own, 'co', [(0, 1), (1, 0)])]
    all_gather x1 -> x0, waiting for transfers between devices: 1.54 us -> none  [per_device(): kv = lax.all_gather(kv, 'y', axis=0)]
    all_to_all x1 -> x2, waiting for transfers between devices: 4.64 us -> 5.21 us  [per_device(): exchange = lambda a: lax.all_to_all(a, XZ, 0, 0, tiled=True)]
  transfers between devices with their start and end apart: 3 -> 7, of which waited for: 2 -> 4; matrix products, arithmetic and copies ran while one was open for 1% -> 1% of each run, Pallas kernels for 15% -> 16%
where the time goes in v3:
time: 129 us
  Pallas kernels  58.9 us (46%)
  waiting for transfers between devices  29.5 us (23%)
  blocking collectives  19.7 us (15%)
  starting transfers between devices  18.9 us (15%)
    pallas_call x1, Pallas kernels, attend(): pl.pallas_call(attend_kernel, grid_spec=pltpu.PrefetchScalarGridSpec(num_...  24.3 us
    ppermute x4, waiting for transfers between devices, ring(): return lax.ppermute(block, 'y', [(i, (i + step) % 4) for i in range(4)])  20.7 us
    all_to_all x1, blocking collectives, per_device(): exchange = lambda a: lax.all_to_all(a, XZ, 0, 0, tiled=True)  19.7 us
    pallas_call x1, Pallas kernels, project_bias(): pl.pallas_call(bias_kernel, grid=(queries // step,), in_specs=[pl.BlockSp...  11.9 us
    all_to_all x2, starting transfers between devices, per_device(): exchange = lambda a: lax.all_to_all(a, XZ, 0, 0, tiled=True)  11.7 us
    pallas_call x1, Pallas kernels, gates(): pl.pallas_call(gate_kernel, out_shape=[jax.ShapeDtypeStruct((samples // 2...  8.97 us
    pallas_call x1, Pallas kernels, project_qkv(): pl.pallas_call(qkv_kernel, grid=(steps,), in_specs=[whole(act), whole(con...  8.44 us
    ppermute x4, starting transfers between devices, ring(): return lax.ppermute(block, 'y', [(i, (i + step) % 4) for i in range(4)])  6.92 us
  transfers between devices with their start and end apart: 7, of which 4 were waited for; matrix products, arithmetic and copies ran while one was open for 1% of the time, Pallas kernels for 16%

profile of v3, /device:TPU:0, one launch (start us, length us, event | category | flops | bytes accessed | tf_op | source)
XLA Modules:
  0.0 128.9 jit_solution(5979154868548689901)
XLA Ops:
  0.0 8.4 %qkv.1 = (bf16[16,80,384]{2,1,0:T(8,128)(2,1)}, bf16[16,80,256]{2,1,0:T(8,128)(2,1)}, bf16[4,80,768]{2,1,0:T(8,128)(2,1)}, bf16[4,80,384]{2,1,0:T(8,128)(2,1)}) custom-call(bf16[4,80,768]{2,1,0:T(8,128)(2,1)} %act.3, bf16[4,80,384]{2,1,0:T(8,128)(2,1)} %cond.1, s32[1,80]{1,0:T(1,128)} %bitcast.21, bf16[768,1024]{1,0:T(8,128)(2,1)} %constant.13.clone.kv_place, ...), custom_call_target="tpu_custom_call" | custom-call | flops 4000000000 | bytes 10000000 | tf_op jit(solution)/shard_map/qkv/pallas_call | solution.py:98
  8.4 8.0 %all-to-all-start = ((bf16[16,80,384]{2,1,0:T(8,128)(2,1)}), bf16[16,80,384]{2,1,0:T(8,128)(2,1)S(1)}, u32[]{:S(2)}, u32[]{:S(2)}) async-start(bf16[16,80,384]{2,1,0:T(8,128)(2,1)} %get-tuple-element.20), calls=%async_computation | async-start | bytes 1966080 | tf_op jit(solution)/shard_map/all_to_all | solution.py:343
  16.4 11.9 %bias.1 = bf16[16,80,896]{2,1,0:T(8,128)(2,1)} custom-call(bf16[80,640,128]{2,1,0:T(8,128)(2,1)} %pair.1, bf16[16,128]{1,0:T(8,128)(2,1)} %bitcast.20, bf16[16,80,256]{2,1,0:T(8,128)(2,1)} %get-tuple-element.21.q), custom_call_target="tpu_custom_call" | custom-call | flops 10000000000 | bytes 15000000 | tf_op jit(solution)/shard_map/bias/pallas_call | solution.py:143
  28.3 5.2 %all-to-all-done = bf16[16,80,384]{2,1,0:T(8,128)(2,1)S(1)} async-done(((bf16[16,80,384]{2,1,0:T(8,128)(2,1)}), bf16[16,80,384]{2,1,0:T(8,128)(2,1)S(1)}, u32[]{:S(2)}, u32[]{:S(2)}) %all-to-all-start) | async-done | bytes 983072 | tf_op jit(solution)/shard_map/all_to_all | solution.py:343
  33.5 0.0 copy-start.1
  33.5 3.7 %all-to-all-start.1 = ((bf16[16,80,896]{2,1,0:T(8,128)(2,1)}), bf16[16,80,896]{2,1,0:T(8,128)(2,1)S(1)}, u32[]{:S(2)}, u32[]{:S(2)}) async-start(bf16[16,80,896]{2,1,0:T(8,128)(2,1)} %bias.1), calls=%async_computation.1 | async-start | bytes 4587520 | tf_op jit(solution)/shard_map/all_to_all | solution.py:343
  37.2 3.1 %collective-permute-start.1 = (bf16[16,80,384]{2,1,0:T(8,128)(2,1)S(1)}, bf16[16,80,384]{2,1,0:T(8,128)(2,1)S(1)}, u32[]{:S(2)}, u32[]{:S(2)}) collective-permute-start(bf16[16,80,384]{2,1,0:T(8,128)(2,1)S(1)} %all-to-all-done), channel_id=1, source_target_pairs={{0,12},{4,0},{8,4},{12,8},{1,13},{5,1},{9,5},{13,9},{2,14},{6,2},{... | collective-permute-start | bytes 2949128 | tf_op jit(solution)/shard_map/ppermute | solution.py:320
  40.3 0.0 copy-done.1
  40.3 0.0 collective-permute-start
  40.3 19.2 %collective-permute-done.1 = bf16[16,80,384]{2,1,0:T(8,128)(2,1)S(1)} collective-permute-done((bf16[16,80,384]{2,1,0:T(8,128)(2,1)S(1)}, bf16[16,80,384]{2,1,0:T(8,128)(2,1)S(1)}, u32[]{:S(2)}, u32[]{:S(2)}) %collective-permute-start.1) | collective-permute-done | bytes 983072 | tf_op jit(solution)/shard_map/ppermute | solution.py:320
  59.6 0.0 copy-start.2
  59.6 0.1 slice.9
  59.6 3.8 %collective-permute-start.3 = (bf16[8,80,384]{2,1,0:T(8,128)(2,1)S(1)}, bf16[8,80,384]{2,1,0:T(8,128)(2,1)S(1)}, u32[]{:S(2)}, u32[]{:S(2)}) collective-permute-start(bf16[8,80,384]{2,1,0:T(8,128)(2,1)S(1)} %slice.9), channel_id=1, source_target_pairs={{0,12},{4,0},{8,4},{12,8},{1,13},{5,1},{9,5},{13,9},{2,14},{6,2},{... | collective-permute-start | bytes 1474568 | tf_op jit(solution)/shard_map/ppermute | solution.py:320
  63.4 0.0 copy-done.2
  63.4 0.0 collective-permute-done
  63.4 0.0 copy-start.3
  63.4 0.1 slice.8
  63.4 0.1 collective-permute-start.2
  63.5 9.0 %gates.1 = (f32[2,80,2048]{2,1,0:T(8,128)}, f32[4,80,768]{2,1,0:T(8,128)}) custom-call(bf16[4,80,768]{2,1,0:T(8,128)(2,1)} %get-tuple-element.24.mod, bf16[4,80,384]{2,1,0:T(8,128)(2,1)} %get-tuple-element.25.cn, bf16[768,1024]{1,0:T(8,128)(2,1)} %constant.14.clone.q_place.place, bf16[768,768]{1,0:T(8,128)(2,1)} %wg.1, bf16[384,768]{1,0:T(8,128)(2,1)} %wog.1), custom_call_target="tpu_custom_call" | custom-call | flops 4000000000 | bytes 9000000 | tf_op jit(solution)/shard_map/gates/pallas_call | solution.py:275
  72.5 0.0 copy-done.3
  72.5 0.0 collective-permute-done.3
  72.5 0.0 copy-start.4
  72.5 0.8 copy-done.4
  73.3 1.4 %collective-permute-done.2 = bf16[8,80,384]{2,1,0:T(8,128)(2,1)S(1)} collective-permute-done((bf16[8,80,384]{2,1,0:T(8,128)(2,1)S(1)}, bf16[8,80,384]{2,1,0:T(8,128)(2,1)S(1)}, u32[]{:S(2)}, u32[]{:S(2)}) %collective-permute-start.2) | collective-permute-done | bytes 491552 | tf_op jit(solution)/shard_map/ppermute | solution.py:320
  74.7 0.0 copy-start.5
  74.7 0.0 all-to-all-done.1
  74.7 0.0 copy-start
  74.7 0.3 collective-permute-start.4
  75.0 0.9 pad_add_fusion.place
  75.9 3.6 %collective-permute-done.4 = bf16[16,80,896]{2,1,0:T(8,128)(2,1)} collective-permute-done((bf16[16,80,896]{2,1,0:T(8,128)(2,1)S(1)}, bf16[16,80,896]{2,1,0:T(8,128)(2,1)}, u32[]{:S(2)}, u32[]{:S(2)}) %collective-permute-start.4) | collective-permute-done | bytes 2293792 | tf_op jit(solution)/shard_map/ppermute | solution.py:351
  79.6 0.0 copy-done.5
  79.6 0.0 copy-done
  79.6 24.3 %attend.1 = bf16[8,2,80,256]{3,2,1,0:T(8,128)(2,1)} custom-call(s32[2]{0:T(128)} %pad_add_fusion.place, bf16[8,2,80,896]{3,2,1,0:T(8,128)(2,1)} %bitcast.12, bf16[2,4,2,80,384]{4,3,2,1,0:T(8,128)(2,1)} %bitcast.14, bf16[2,4,2,80,384]{4,3,2,1,0:T(8,128)(2,1)} %bitcast.17, bf16[1,4,2,80,384]{4,3,2,1,0:T(8,128)(2,1)} %bitcast.19, ...), custom_call_target="tpu_custom_call" | custom-call | flops 14000000000 | bytes 10000000 | tf_op jit(solution)/shard_map/attend/pallas_call | solution.py:234
  103.8 19.7 %all_to_all.15.attended = bf16[16,80,256]{2,1,0:T(8,128)(2,1)} all-to-all(bf16[16,80,256]{2,1,0:T(8,128)(2,1)} %bitcast.15), channel_id=1, replica_groups=mesh['zh'=2,'x'=4,'y'=4,'zl'=2,'co'=2] {'zh','x','zl'}, dimensions={0} | all-to-all | bytes 1310720 | tf_op jit(solution)/shard_map/all_to_all | solution.py:343
  123.5 5.4 %out.1 = bf16[4,80,768]{2,1,0:T(8,128)(2,1)} custom-call(bf16[16,80,256]{2,1,0:T(8,128)(2,1)} %all_to_all.15.attended, f32[2,80,2048]{2,1,0:T(8,128)} %get-tuple-element.33.gate, f32[4,80,768]{2,1,0:T(8,128)} %get-tuple-element.34.og, bf16[4,80,768]{2,1,0:T(8,128)(2,1)} %act.3, bf16[768,768]{1,0:T(8,128)(2,1)} %wo.1), custom_call_target="tpu_custom_call" | custom-call | flops 2000000000 | bytes 6000000 | tf_op jit(solution)/shard_map/out/pallas_call | solution.py:309
Async XLA Ops:
  8.4 25.1 %all-to-all-start = ((bf16[16,80,384]{2,1,0:T(8,128)(2,1)}), bf16[16,80,384]{2,1,0:T(8,128)(2,1)S(1)}, u32[]{:S(2)}, u32[]{:S(2)}) async-start(bf16[16,80,384]{2,1,0:T(8,128)(2,1)} %get-tuple-element.20), calls=%async_computation | async-start | bytes 1966080 | tf_op jit(solution)/shard_map/all_to_all | solution.py:343
  33.5 6.8 %copy-start.1 = (bf16[16,80,384]{2,1,0:T(8,128)(2,1)}, bf16[16,80,384]{2,1,0:T(8,128)(2,1)S(1)}, u32[]{:S(2)}) copy-start(bf16[16,80,384]{2,1,0:T(8,128)(2,1)S(1)} %all-to-all-done) | copy-start | bytes 2949124
  33.5 41.2 %all-to-all-start.1 = ((bf16[16,80,896]{2,1,0:T(8,128)(2,1)}), bf16[16,80,896]{2,1,0:T(8,128)(2,1)S(1)}, u32[]{:S(2)}, u32[]{:S(2)}) async-start(bf16[16,80,896]{2,1,0:T(8,128)(2,1)} %bias.1), calls=%async_computation.1 | async-start | bytes 4587520 | tf_op jit(solution)/shard_map/all_to_all | solution.py:343
  37.2 22.3 %collective-permute-start.1 = (bf16[16,80,384]{2,1,0:T(8,128)(2,1)S(1)}, bf16[16,80,384]{2,1,0:T(8,128)(2,1)S(1)}, u32[]{:S(2)}, u32[]{:S(2)}) collective-permute-start(bf16[16,80,384]{2,1,0:T(8,128)(2,1)S(1)} %all-to-all-done), channel_id=1, source_target_pairs={{0,12},{4,0},{8,4},{12,8},{1,13},{5,1},{9,5},{13,9},{2,14},{6,2},{... | collective-permute-start | bytes 2949128 | tf_op jit(solution)/shard_map/ppermute | solution.py:320
  40.3 23.1 %collective-permute-start = (bf16[16,80,384]{2,1,0:T(8,128)(2,1)S(1)}, bf16[16,80,384]{2,1,0:T(8,128)(2,1)S(1)}, u32[]{:S(2)}, u32[]{:S(2)}) collective-permute-start(bf16[16,80,384]{2,1,0:T(8,128)(2,1)S(1)} %all-to-all-done), channel_id=1, source_target_pairs={{0,4},{4,8},{8,12},{12,0},{1,5},{5,9},{9,13},{13,1},{2,6},{6,10},{... | collective-permute-start | bytes 2949128 | tf_op jit(solution)/shard_map/ppermute | solution.py:320
  59.6 3.8 %copy-start.2 = (bf16[16,80,384]{2,1,0:T(8,128)(2,1)}, bf16[16,80,384]{2,1,0:T(8,128)(2,1)S(1)}, u32[]{:S(2)}) copy-start(bf16[16,80,384]{2,1,0:T(8,128)(2,1)S(1)} %collective-permute-done.1) | copy-start | bytes 2949124
  59.6 12.9 %collective-permute-start.3 = (bf16[8,80,384]{2,1,0:T(8,128)(2,1)S(1)}, bf16[8,80,384]{2,1,0:T(8,128)(2,1)S(1)}, u32[]{:S(2)}, u32[]{:S(2)}) collective-permute-start(bf16[8,80,384]{2,1,0:T(8,128)(2,1)S(1)} %slice.9), channel_id=1, source_target_pairs={{0,12},{4,0},{8,4},{12,8},{1,13},{5,1},{9,5},{13,9},{2,14},{6,2},{... | collective-permute-start | bytes 1474568 | tf_op jit(solution)/shard_map/ppermute | solution.py:320
  63.4 9.1 %copy-start.3 = (bf16[16,80,384]{2,1,0:T(8,128)(2,1)}, bf16[16,80,384]{2,1,0:T(8,128)(2,1)S(1)}, u32[]{:S(2)}) copy-start(bf16[16,80,384]{2,1,0:T(8,128)(2,1)S(1)} %collective-permute-done) | copy-start | bytes 2949124
  63.4 11.3 %collective-permute-start.2 = (bf16[8,80,384]{2,1,0:T(8,128)(2,1)S(1)}, bf16[8,80,384]{2,1,0:T(8,128)(2,1)S(1)}, u32[]{:S(2)}, u32[]{:S(2)}) collective-permute-start(bf16[8,80,384]{2,1,0:T(8,128)(2,1)S(1)} %slice.8), channel_id=1, source_target_pairs={{0,4},{4,8},{8,12},{12,0},{1,5},{5,9},{9,13},{13,1},{2,6},{6,10},{... | collective-permute-start | bytes 1474568 | tf_op jit(solution)/shard_map/ppermute | solution.py:320
  72.5 0.8 copy-start.4
  74.7 4.8 %copy-start.5 = (bf16[8,80,384]{2,1,0:T(8,128)(2,1)}, bf16[8,80,384]{2,1,0:T(8,128)(2,1)S(1)}, u32[]{:S(2)}) copy-start(bf16[8,80,384]{2,1,0:T(8,128)(2,1)S(1)} %collective-permute-done.2) | copy-start | bytes 1474564
  74.7 4.8 %copy-start = (bf16[16,80,896]{2,1,0:T(8,128)(2,1)}, bf16[16,80,896]{2,1,0:T(8,128)(2,1)S(1)}, u32[]{:S(2)}) copy-start(bf16[16,80,896]{2,1,0:T(8,128)(2,1)S(1)} %all-to-all-done.1) | copy-start | bytes 6881284
  74.7 4.8 %collective-permute-start.4 = (bf16[16,80,896]{2,1,0:T(8,128)(2,1)S(1)}, bf16[16,80,896]{2,1,0:T(8,128)(2,1)}, u32[]{:S(2)}, u32[]{:S(2)}) collective-permute-start(bf16[16,80,896]{2,1,0:T(8,128)(2,1)S(1)} %all-to-all-done.1), channel_id=1, source_target_pairs={{0,1},{1,0},{2,3},{3,2},{4,5},{5,4},{6,7},{7,6},{8,9},{9,8},{10,11... | collective-permute-start | bytes 6881288 | tf_op jit(solution)/shard_map/ppermute | solution.py:351

commit v4 on v3

--- a/solution.py
+++ b/solution.py
@@ -45,7 +45,12 @@
                 table[which, 0, head, channel, head, channel] = 1
                 table[which, 1, head, channel, head, offset + channel] = 1
     table = table.reshape(2, 2 * GROUP * HEAD, GROUP * LANES)
-    return jnp.asarray(table[0], BF), jnp.asarray(table[1], BF)
+    pairs = np.zeros((HEADS // 2, 2 * HEAD, HEADS // 2, LANES), np.float32)
+    for pair in range(HEADS // 2):
+        for channel in range(2 * HEAD):
+            pairs[pair, channel, pair, channel] = 1
+    pairs = pairs.reshape(HEADS * HEAD, HEADS // 2 * LANES)
+    return jnp.asarray(table[0], BF), jnp.asarray(table[1], BF), jnp.asarray(pairs, BF)
 
 
 def qkv_kernel(act, cond, mask, kv_place, q_place, ws, wsh, wq, wk, wv, kv_out, q_out, mod_out, cn_out, mod):
@@ -158,116 +163,151 @@
 
 
 T = 4
-
-
-def attend_kernel(place, q, near, up, far_low, far_high, down, own, other, out, keys):
+PIECE = 128
+LIMIT = 2.0**100
+
+
+def lay_kernel(place, near, up, far_low, far_high, down, keys):
+    tokens = near.shape[-2]
+    core, row = place[0], place[1]
+    lane = lax.broadcasted_iota(jnp.int32, (tokens, LANES), 1)
+    for z in range(2):
+        parts = (near.at[z], up.at[z], (far_low, far_high)[z].at[0], down.at[z])
+        for o in range(2):
+            quarter = core if o == 0 else 1 - core
+            for low in range(2):
+                for step, part in enumerate(parts):
+                    block = (z * 2 + o) * 8 + low * 4 + lax.rem(row + 4 - step, 4)
+                    at = pl.ds(pl.multiple_of(block * tokens, 16), tokens)
+                    tiles = [part[2 * quarter + low, 0, :, i * LANES:(i + 1) * LANES] for i in range(3)]
+                    wide = [t.astype(F32) for t in tiles]
+                    mark = pltpu.roll(wide[0], PAD_LANE - MARK_LANE, axis=1)
+                    pad = jnp.where(mark < 0.5 * NEGATIVE, NEGATIVE, 0.0)
+                    tail = jnp.where(lane == PAD_LANE, pad, jnp.where(lane == SUM_LANE, 1.0, 0.0)).astype(BF)
+                    for s in range(3):
+                        keys[0, s, at] = jnp.where(lane < 96, tiles[s], tail)
+                    last = jnp.where(
+                        lane < 32,
+                        pltpu.roll(wide[0], 32, axis=1),
+                        jnp.where(lane < 64, pltpu.roll(wide[1], 64, axis=1), pltpu.roll(wide[2], 96, axis=1)),
+                    ).astype(BF)
+                    keys[0, 3, at] = jnp.where(lane < 96, last, tail)
+
+
+def lay_keys(place, kv):
+    tokens = kv[0].shape[3]
+    extent = 32 * tokens
+    return pl.pallas_call(
+        lay_kernel,
+        grid_spec=pltpu.PrefetchScalarGridSpec(
+            num_scalar_prefetch=1,
+            grid=(2,),
+            in_specs=[pl.BlockSpec((a.shape[0], 4, 1, tokens, 3 * LANES), lambda z, c: (0, 0, z, 0, 0)) for a in kv],
+            out_specs=pl.BlockSpec((1, 4, extent, LANES), lambda z, c: (z, 0, 0, 0)),
+        ),
+        out_shape=jax.ShapeDtypeStruct((2, 4, extent, LANES), BF),
+        compiler_params=pltpu.CompilerParams(vmem_limit_bytes=VMEM_BYTES),
+        cost_estimate=pl.CostEstimate(flops=40_000_000_000, bytes_accessed=10_000_000, transcendentals=0),
+        name="lay",
+    )(place, *kv)
+
+
+def attend_kernel(q, keys, own, other, out):
     tokens = q.shape[2]
     chunk = 8 * tokens
-    core, row = place[0], place[1]
-    lane_k = lax.broadcasted_iota(jnp.int32, (tokens, LANES), 1)
-
-    @pl.when(pl.program_id(1) == 0)
-    def _():
-        for z in range(2):
-            sources = (near.at[z], up.at[z], (far_low, far_high)[z].at[0], down.at[z])
-            for o in range(2):
-                quarter = core if o == 0 else 1 - core
-                for low in range(2):
-                    for step, source in enumerate(sources):
-                        block = low * 4 + lax.rem(row + 4 - step, 4)
-                        at = pl.ds(pl.multiple_of((z * 2 + o) * chunk + block * tokens, 16), tokens)
-                        tiles = [source[2 * quarter + low, 0, :, i * LANES:(i + 1) * LANES] for i in range(3)]
-                        wide = [t.astype(F32) for t in tiles]
-                        pad = jnp.where(pltpu.roll(wide[0], PAD_LANE - MARK_LANE, axis=1) < 0.5 * NEGATIVE, NEGATIVE, 0.0)
-                        tail = jnp.where(lane_k == PAD_LANE, pad, jnp.where(lane_k == SUM_LANE, 1.0, 0.0)).astype(BF)
-                        for s in range(3):
-                            keys[s, at] = jnp.where(lane_k < 96, tiles[s], tail)
-                        last = jnp.where(
-                            lane_k < 32,
-                            pltpu.roll(wide[0], 32, axis=1),
-                            jnp.where(lane_k < 64, pltpu.roll(wide[1], 64, axis=1), pltpu.roll(wide[2], 96, axis=1)),
-                        ).astype(BF)
-                        keys[3, at] = jnp.where(lane_k < 96, last, tail)
-
-    first_sample = 2 * pl.program_id(1)
     span = T * tokens
     lane = lax.broadcasted_iota(jnp.int32, (span, LANES), 1)
     pad_one = jnp.where(lane == PAD_LANE, 1.0, 0.0).astype(BF)
-    blocks = [(t, s) for t in range(8 // T) for s in range(2)]
-
-    def scores_of(t, s, c):
-        pair_q = q[t * T:(t + 1) * T, 0].reshape(span, LANES)
+
+    def query(t, s):
+        pair_q = q[pl.ds(t * T, T), 0].reshape(span, LANES)
         if s == 1:
             pair_q = pltpu.roll(pair_q.astype(F32), 64, axis=1).astype(BF)
-        mine = jnp.where(lane < HEAD, pair_q, pad_one)
-        part = lax.dot_general(
-            mine, keys[first_sample + s, c * chunk:(c + 1) * chunk], NT, preferred_element_type=F32
-        )
-        b = (own if c % 2 == 0 else other)[t * T:(t + 1) * T, c // 2].reshape(span, chunk)
-        return part + b.astype(F32)
-
-    current = [scores_of(*blocks[0], c) for c in range(4)]
-    for i, (t, s) in enumerate(blocks):
-        tops = [jnp.max(part, axis=1, keepdims=True) for part in current]
-        top = jnp.maximum(jnp.maximum(tops[0], tops[1]), jnp.maximum(tops[2], tops[3]))
-        following, total = [], None
-        for c in range(4):
-            if i + 1 < len(blocks):
-                following.append(scores_of(*blocks[i + 1], c))
-            p = jnp.exp2(current[c] - top).astype(BF)
-            part = dot(p, keys[first_sample + s, c * chunk:(c + 1) * chunk])
-            total = part if total is None else total + part
+        return jnp.where(lane < HEAD, pair_q, pad_one)
+
+    def scores(t, s, at, width):
+        part = lax.dot_general(query(t, s), keys[0, s, at:at + width], NT, preferred_element_type=F32)
+        columns = at % chunk
+        bias = own if at // chunk % 2 == 0 else other
+        bias = bias[pl.ds(t * T, T), at // chunk // 2, :, columns:columns + width].reshape(span, width)
+        return part + bias.astype(F32)
+
+    def values(p, s, at, width):
+        return dot(p, keys[0, s, at:at + width])
+
+    def store(t, pair):
+        low = pltpu.roll(pair[0], LANES - HEAD, axis=1)
+        high = pltpu.roll(pair[1], 64 - HEAD, axis=1)
+        merged = jnp.where(lane < 64, low, high).astype(BF)
+        out[pl.ds(t * T, T), 0] = merged.reshape(T, tokens, LANES)
+
+    pieces = [(t, s, at) for t in range(8 // T) for s in range(2) for at in range(0, 4 * chunk, PIECE)]
+    following = scores(*pieces[0], PIECE)
+    top, total, pair, worst = None, None, [], jnp.float32(0.0)
+    for i, (t, s, at) in enumerate(pieces):
         current = following
-        result = total / total[:, SUM_LANE:SUM_LANE + 1]
-        if s == 0:
-            low = pltpu.roll(result, LANES - HEAD, axis=1)
-        else:
-            high = pltpu.roll(result, 64 - HEAD, axis=1)
-            merged = jnp.where(lane < 64, low, high).astype(BF)
-            out[t * T:(t + 1) * T, 0] = merged.reshape(T, tokens, LANES)
-
-
-def attend(place, kv, own, other):
+        if at == 0:
+            top, total = jnp.max(current, axis=1, keepdims=True), None
+        if i + 1 < len(pieces):
+            following = scores(*pieces[i + 1], PIECE)
+        part = values(jnp.exp2(current - top).astype(BF), s, at, PIECE)
+        total = part if total is None else total + part
+        if at == 4 * chunk - PIECE:
+            weight = total[:, SUM_LANE:SUM_LANE + 1]
+            worst = jnp.maximum(worst, jnp.max(weight))
+            pair.append(total / weight)
+            if s == 1:
+                store(t, pair)
+                pair = []
+
+    @pl.when(jnp.logical_not(worst < LIMIT))
+    def _():
+        def block(t, carried):
+            pair = []
+            for s in range(2):
+                top = total = None
+                for at in range(0, 4 * chunk, chunk):
+                    peak = jnp.max(scores(t, s, at, chunk), axis=1, keepdims=True)
+                    top = peak if top is None else jnp.maximum(top, peak)
+                for at in range(0, 4 * chunk, chunk):
+                    p = jnp.exp2(scores(t, s, at, chunk) - top).astype(BF)
+                    part = values(p, s, at, chunk)
+                    total = part if total is None else total + part
+                pair.append(total / total[:, SUM_LANE:SUM_LANE + 1])
+            store(t, pair)
+            return carried
+
+        lax.fori_loop(0, 8 // T, block, 0)
+
+
+def attend(keys, own, other):
     tokens = own.shape[2]
     chunk = 8 * tokens
-    b_spec = pl.BlockSpec((8, 2, tokens, chunk), lambda z, p, c: (0, 0, 0, 0))
+    b_spec = pl.BlockSpec((8, 2, tokens, chunk), lambda z, p: (0, 0, 0, 0))
     return pl.pallas_call(
         attend_kernel,
-        grid_spec=pltpu.PrefetchScalarGridSpec(
-            num_scalar_prefetch=1,
-            grid=(2, 2),
-            in_specs=[
-                pl.BlockSpec((8, 1, tokens, LANES), lambda z, p, c: (0, z, 0, chunk // LANES + p)),
-            ]
-            + [pl.BlockSpec((a.shape[0], 4, 1, tokens, 3 * LANES), lambda z, p, c: (0, 0, z, 0, 0)) for a in kv]
-            + [
-                b_spec,
-                b_spec,
-            ],
-            out_specs=pl.BlockSpec((8, 1, tokens, LANES), lambda z, p, c: (0, z, 0, p)),
-            scratch_shapes=[pltpu.VMEM((4, 4 * chunk, LANES), BF)],
-        ),
+        grid=(2, 2),
+        in_specs=[
+            pl.BlockSpec((8, 1, tokens, LANES), lambda z, p: (0, z, 0, chunk // LANES + p)),
+            pl.BlockSpec((1, 2, 4 * chunk, LANES), lambda z, p: (z, p, 0, 0)),
+            b_spec,
+            b_spec,
+        ],
+        out_specs=pl.BlockSpec((8, 1, tokens, LANES), lambda z, p: (0, z, 0, p)),
         out_shape=jax.ShapeDtypeStruct((8, 2, tokens, 2 * LANES), BF),
         compiler_params=pltpu.CompilerParams(vmem_limit_bytes=VMEM_BYTES),
         cost_estimate=pl.CostEstimate(flops=14_000_000_000, bytes_accessed=10_000_000, transcendentals=13_000_000),
         name="attend",
-    )(place, own, *kv, own, other)
+    )(own, keys, own, other)
 
 
 def gate_kernel(mod, cn, place, wg, wog, gate_out, og_out):
     samples, tokens, width = mod.shape
     rows = samples * tokens
     og_out[...] = jax.nn.sigmoid(dot(cn[...].reshape(rows, cn.shape[2]), wog[...])).reshape(og_out.shape)
-    columns = GROUP * HEAD
-    low = place[0:columns]
-    high = place[columns:2 * columns]
-    for g in range(HEADS // GROUP):
-        w = wg[:, g * columns:(g + 1) * columns]
-        w_low = dot(w, low).astype(BF)
-        w_high = dot(w, high).astype(BF)
-        for p in range(samples // 2):
-            value = dot(mod[2 * p], w_low) + dot(mod[2 * p + 1], w_high)
-            gate_out[p, :, g * GROUP * LANES:(g + 1) * GROUP * LANES] = jax.nn.sigmoid(value)
+    placed = dot(wg[...], place[...]).astype(BF)
+    gate = jax.nn.sigmoid(dot(mod[...].reshape(rows, width), placed))
+    gate_out[...] = gate.reshape(gate_out.shape)
 
 
 def gates(mod, cn, place, wg, wog):
@@ -275,33 +315,38 @@
     return pl.pallas_call(
         gate_kernel,
         out_shape=[
-            jax.ShapeDtypeStruct((samples // 2, tokens, HEADS * LANES), F32),
+            jax.ShapeDtypeStruct((samples, tokens, HEADS // 2 * LANES), F32),
             jax.ShapeDtypeStruct(mod.shape, F32),
         ],
         compiler_params=pltpu.CompilerParams(vmem_limit_bytes=VMEM_BYTES),
-        cost_estimate=pl.CostEstimate(flops=4_000_000_000, bytes_accessed=9_000_000, transcendentals=1_000_000),
+        cost_estimate=pl.CostEstimate(flops=32_000_000_000, bytes_accessed=9_000_000, transcendentals=1_000_000),
         name="gates",
     )(mod, cn, place, wg, wog)
 
 
-def out_kernel(attended, gate, og, act, wo, out, low, high):
+def out_kernel(attended, gate, og, act, wo, out, table):
     samples, tokens, width = act.shape
-    low[...] = jnp.zeros_like(low)
-    high[...] = jnp.zeros_like(high)
-    for h in range(HEADS):
-        rows = wo[h * HEAD:(h + 1) * HEAD]
-        low[h * LANES:h * LANES + HEAD] = rows
-        high[h * LANES + 64:h * LANES + 64 + HEAD] = rows
-    for p in range(samples // 2):
-        gated = jnp.concatenate(
-            [
-                (attended[h, :, p * LANES:(p + 1) * LANES].astype(F32) * gate[p, :, h * LANES:(h + 1) * LANES]).astype(BF)
-                for h in range(HEADS)
-            ],
-            axis=1,
-        )
-        for s, table in ((2 * p, low), (2 * p + 1, high)):
-            out[s] = (act[s].astype(F32) + og[s] * dot(gated, table[...])).astype(BF)
+    table[...] = jnp.zeros_like(table)
+    for j in range(HEADS // 2):
+        table[j * LANES:j * LANES + 96] = wo[j * 96:(j + 1) * 96]
+    lane = lax.broadcasted_iota(jnp.int32, (tokens, LANES), 1)
+    rows = []
+    for s in range(samples):
+        lanes = slice(s // 2 * LANES, (s // 2 + 1) * LANES)
+        tiles = []
+        for j in range(HEADS // 2):
+            first = attended[2 * j, :, lanes].astype(F32)
+            second = attended[2 * j + 1, :, lanes].astype(F32)
+            if s % 2 == 0:
+                second = pltpu.roll(second, HEAD, axis=1)
+            else:
+                first = pltpu.roll(first, 64, axis=1)
+                second = pltpu.roll(second, 64 + HEAD, axis=1)
+            both = jnp.where(lane < HEAD, first, second)
+            tiles.append((both * gate[s, :, j * LANES:(j + 1) * LANES]).astype(BF))
+        rows.append(jnp.concatenate(tiles, axis=1))
+    projected = dot(jnp.concatenate(rows, axis=0), table[...])
+    out[...] = (act[...].astype(F32) + og[...] * projected.reshape(act.shape)).astype(BF)
 
 
 def project_out(attended, gate, og, act, wo):
@@ -309,7 +354,7 @@
     return pl.pallas_call(
         out_kernel,
         out_shape=jax.ShapeDtypeStruct(act.shape, BF),
-        scratch_shapes=[pltpu.VMEM((HEADS * LANES, width), BF)] * 2,
+        scratch_shapes=[pltpu.VMEM((HEADS // 2 * LANES, width), BF)],
         compiler_params=pltpu.CompilerParams(vmem_limit_bytes=VMEM_BYTES),
         cost_estimate=pl.CostEstimate(flops=2_000_000_000, bytes_accessed=6_000_000, transcendentals=0),
         name="out",
@@ -336,7 +381,7 @@
     w_bias,
 ):
     tokens = activations.shape[1]
-    kv_place, q_place = placement()
+    kv_place, q_place, gate_place = placement()
     kv, q, modulated, cond_norm = project_qkv(
         activations, conditioning, key_mask.reshape(1, tokens), kv_place, q_place, w_scale, w_shift, w_query, w_key, w_value
     )
@@ -344,18 +389,15 @@
     bias = project_bias(pair_features, w_bias.T, q)
     kv, bias = lax.optimization_barrier((exchange(kv), bias))
     up, down = ring(kv, 1), ring(kv, 3)
+    own = exchange(bias)
+    gate, out_gate = gates(modulated, cond_norm, gate_place, w_gate, w_outgate)
+    up, down, gate, out_gate = lax.optimization_barrier((up, down, gate, out_gate))
     far = (ring(up[:HEADS // 2], 1), ring(down[HEADS // 2:], 3))
-    own = exchange(bias)
-    gate, out_gate = gates(modulated, cond_norm, q_place, w_gate, w_outgate)
-    own, up, down, far, gate, out_gate = lax.optimization_barrier((own, up, down, far, gate, out_gate))
     other = lax.ppermute(own, "co", [(0, 1), (1, 0)])
     place = jnp.stack([lax.axis_index("co"), lax.axis_index("y")]).astype(jnp.int32)
-    attended = attend(
-        place,
-        [a.reshape(-1, 4, 2, tokens, kv.shape[-1]) for a in (kv, up, *far, down)],
-        own.reshape(8, 2, tokens, own.shape[-1]),
-        other.reshape(8, 2, tokens, own.shape[-1]),
-    )
+    kv = [a.reshape(-1, 4, 2, tokens, kv.shape[-1]) for a in (kv, up, *far, down)]
+    own, other = (a.reshape(8, 2, tokens, own.shape[-1]) for a in (own, other))
+    attended = attend(lay_keys(place, kv), own, other)
     attended = exchange(attended.reshape(HEADS, tokens, 2 * LANES))
     return project_out(attended, gate, out_gate, activations, w_out)
 

time: 129 us -> 120 us (0.930); the launches traced: 129 us -> 119 us
  blocking collectives: 19.7 us -> 15.1 us
  Pallas kernels: 58.9 us -> 54.7 us
  local copies, waits for them, and re-layouts: 0.9 us -> 3.57 us
  starting transfers between devices: 18.9 us -> 16.8 us
  waiting for transfers between devices: 29.5 us -> 27.8 us
    all_to_all x2, waiting for transfers between devices: 5.21 us -> 11 us  [per_device(): exchange = lambda a: lax.all_to_all(a, XZ, 0, 0, tiled=True)]
    all_to_all x1, blocking collectives: 19.7 us -> 15.1 us  [per_device(): exchange = lambda a: lax.all_to_all(a, XZ, 0, 0, tiled=True)]
    ppermute x4, waiting for transfers between devices: 20.7 us -> 16.8 us  [ring(): return lax.ppermute(block, 'y', [(i, (i + step) % 4) for i in range(4)])]
    ppermute x1, waiting for transfers between devices: 3.64 us -> 0.01 us  [per_device(): other = lax.ppermute(own, 'co', [(0, 1), (1, 0)])]
    pallas_call x2 -> x3, Pallas kernels: 33.3 us -> 30.5 us  [the longest x1 19.4 us: attend(): pl.pallas_call(attend_kernel, grid=(2, 2), in_specs=[pl.BlockSpec((8, 1,...]
    slice x2, local copies, waits for them, and re-layouts: 0.1 us -> 2.16 us  [per_device(): far = (ring(up[:HEADS // 2], 1), ring(down[HEADS // 2:], 3))]
    ppermute x4, starting transfers between devices: 6.92 us -> 5.11 us  [ring(): return lax.ppermute(block, 'y', [(i, (i + step) % 4) for i in range(4)])]
    pallas_call x1, Pallas kernels: 5.37 us -> 3.9 us  [project_out(): pl.pallas_call(out_kernel, out_shape=jax.ShapeDtypeStruct(act.shape, BF),...]
  transfers between devices with their start and end apart: 7 -> 7, of which waited for: 4 -> 6; matrix products, arithmetic and copies ran while one was open for 1% -> 2% of each run, Pallas kernels for 16% -> 19%
where the time goes in v4:
time: 120 us; the launch traced here: 119 us
  Pallas kernels  54.7 us (46%)
  waiting for transfers between devices  27.8 us (23%)
  starting transfers between devices  16.8 us (14%)
  blocking collectives  15.1 us (13%)
  local copies, waits for them, and re-layouts  3.57 us (3%)
    pallas_call x1, Pallas kernels, attend(): pl.pallas_call(attend_kernel, grid=(2, 2), in_specs=[pl.BlockSpec((8, 1,...  19.4 us
    ppermute x4, waiting for transfers between devices, ring(): return lax.ppermute(block, 'y', [(i, (i + step) % 4) for i in range(4)])  16.8 us
    all_to_all x1, blocking collectives, per_device(): exchange = lambda a: lax.all_to_all(a, XZ, 0, 0, tiled=True)  15.1 us
    pallas_call x1, Pallas kernels, project_bias(): pl.pallas_call(bias_kernel, grid=(queries // step,), in_specs=[pl.BlockSp...  11.9 us
    all_to_all x2, starting transfers between devices, per_device(): exchange = lambda a: lax.all_to_all(a, XZ, 0, 0, tiled=True)  11.7 us
    all_to_all x2, waiting for transfers between devices, per_device(): exchange = lambda a: lax.all_to_all(a, XZ, 0, 0, tiled=True)  11 us
    pallas_call x1, Pallas kernels, project_qkv(): pl.pallas_call(qkv_kernel, grid=(steps,), in_specs=[whole(act), whole(con...  8.42 us
    pallas_call x1, Pallas kernels, lay_keys(): pl.pallas_call(lay_kernel, grid_spec=pltpu.PrefetchScalarGridSpec(num_sca...  5.7 us
  transfers between devices with their start and end apart: 7, of which 6 were waited for; matrix products, arithmetic and copies ran while one was open for 2% of the time, Pallas kernels for 19%

profile of v4, /device:TPU:0, one launch (start us, length us, event | category | flops | bytes accessed | tf_op | source)
XLA Modules:
  0.0 118.6 jit_solution(2932068321026785773)
XLA Ops:
  0.0 8.4 %qkv.1 = (bf16[16,80,384]{2,1,0:T(8,128)(2,1)}, bf16[16,80,256]{2,1,0:T(8,128)(2,1)}, bf16[4,80,768]{2,1,0:T(8,128)(2,1)}, bf16[4,80,384]{2,1,0:T(8,128)(2,1)}) custom-call(bf16[4,80,768]{2,1,0:T(8,128)(2,1)} %act.3, bf16[4,80,384]{2,1,0:T(8,128)(2,1)} %cond.1, s32[1,80]{1,0:T(1,128)} %bitcast.18, bf16[768,1024]{1,0:T(8,128)(2,1)} %constant.15.clone.kv_place, ...), custom_call_target="tpu_custom_call" | custom-call | flops 4000000000 | bytes 10000000 | tf_op jit(solution)/shard_map/qkv/pallas_call | solution.py:103
  8.4 8.0 %all-to-all-start = ((bf16[16,80,384]{2,1,0:T(8,128)(2,1)}), bf16[16,80,384]{2,1,0:T(8,128)(2,1)S(1)}, u32[]{:S(2)}, u32[]{:S(2)}) async-start(bf16[16,80,384]{2,1,0:T(8,128)(2,1)} %get-tuple-element.17), calls=%async_computation | async-start | bytes 1966080 | tf_op jit(solution)/shard_map/all_to_all | solution.py:388
  16.4 11.9 %bias.1 = bf16[16,80,896]{2,1,0:T(8,128)(2,1)} custom-call(bf16[80,640,128]{2,1,0:T(8,128)(2,1)} %pair.1, bf16[16,128]{1,0:T(8,128)(2,1)} %bitcast.17, bf16[16,80,256]{2,1,0:T(8,128)(2,1)} %get-tuple-element.18.q), custom_call_target="tpu_custom_call" | custom-call | flops 10000000000 | bytes 15000000 | tf_op jit(solution)/shard_map/bias/pallas_call | solution.py:148
  28.3 5.2 %all-to-all-done = bf16[16,80,384]{2,1,0:T(8,128)(2,1)S(1)} async-done(((bf16[16,80,384]{2,1,0:T(8,128)(2,1)}), bf16[16,80,384]{2,1,0:T(8,128)(2,1)S(1)}, u32[]{:S(2)}, u32[]{:S(2)}) %all-to-all-start) | async-done | bytes 983072 | tf_op jit(solution)/shard_map/all_to_all | solution.py:388
  33.5 0.0 copy-start.1
  33.5 3.0 %collective-permute-start.1 = (bf16[16,80,384]{2,1,0:T(8,128)(2,1)S(1)}, bf16[16,80,384]{2,1,0:T(8,128)(2,1)}, u32[]{:S(2)}, u32[]{:S(2)}) collective-permute-start(bf16[16,80,384]{2,1,0:T(8,128)(2,1)S(1)} %all-to-all-done), channel_id=1, source_target_pairs={{0,12},{4,0},{8,4},{12,8},{1,13},{5,1},{9,5},{13,9},{2,14},{6,2},{... | collective-permute-start | bytes 2949128 | tf_op jit(solution)/shard_map/ppermute | solution.py:365
  36.5 0.0 collective-permute-start
  36.5 0.0 copy-done.1
  36.5 3.7 %all-to-all-start.1 = ((bf16[16,80,896]{2,1,0:T(8,128)(2,1)}), bf16[16,80,896]{2,1,0:T(8,128)(2,1)S(1)}, u32[]{:S(2)}, u32[]{:S(2)}) async-start(bf16[16,80,896]{2,1,0:T(8,128)(2,1)} %bias.1), calls=%async_computation.1 | async-start | bytes 4587520 | tf_op jit(solution)/shard_map/all_to_all | solution.py:388
  40.2 5.4 %gates.1 = (f32[4,80,1024]{2,1,0:T(8,128)}, f32[4,80,768]{2,1,0:T(8,128)}) custom-call(bf16[4,80,768]{2,1,0:T(8,128)(2,1)} %get-tuple-element.21.mod, bf16[4,80,384]{2,1,0:T(8,128)(2,1)} %get-tuple-element.22.cn, bf16[768,1024]{1,0:T(8,128)(2,1)} %constant.17.clone.place, bf16[768,768]{1,0:T(8,128)(2,1)} %wg.1, bf16[384,768]{1,0:T(8,128)(2,1)} %wog.1), custom_call_target="tpu_custom_call" | custom-call | flops 32000000000 | bytes 9000000 | tf_op jit(solution)/shard_map/gates/pallas_call | solution.py:315
  45.6 10.1 %collective-permute-done.1 = bf16[16,80,384]{2,1,0:T(8,128)(2,1)} collective-permute-done((bf16[16,80,384]{2,1,0:T(8,128)(2,1)S(1)}, bf16[16,80,384]{2,1,0:T(8,128)(2,1)}, u32[]{:S(2)}, u32[]{:S(2)}) %collective-permute-start.1) | collective-permute-done | bytes 983072 | tf_op jit(solution)/shard_map/ppermute | solution.py:365
  55.7 3.5 %collective-permute-done = bf16[16,80,384]{2,1,0:T(8,128)(2,1)} collective-permute-done((bf16[16,80,384]{2,1,0:T(8,128)(2,1)S(1)}, bf16[16,80,384]{2,1,0:T(8,128)(2,1)}, u32[]{:S(2)}, u32[]{:S(2)}) %collective-permute-start) | collective-permute-done | bytes 983072 | tf_op jit(solution)/shard_map/ppermute | solution.py:365
  59.3 1.1 slice.6
  60.3 1.1 slice.7
  61.4 0.4 collective-permute-start.3
  61.8 1.7 %collective-permute-start.2 = (bf16[8,80,384]{2,1,0:T(8,128)(2,1)S(1)}, bf16[8,80,384]{2,1,0:T(8,128)(2,1)}, u32[]{:S(2)}, u32[]{:S(2)}) collective-permute-start(bf16[8,80,384]{2,1,0:T(8,128)(2,1)S(1)} %slice.6), channel_id=1, source_target_pairs={{0,4},{4,8},{8,12},{12,0},{1,5},{5,9},{9,13},{13,1},{2,6},{6,10},{... | collective-permute-start | bytes 1474568 | tf_op jit(solution)/shard_map/ppermute | solution.py:365
  63.5 0.6 pad_add_fusion.place
  64.1 5.8 %all-to-all-done.1 = bf16[16,80,896]{2,1,0:T(8,128)(2,1)S(1)} async-done(((bf16[16,80,896]{2,1,0:T(8,128)(2,1)}), bf16[16,80,896]{2,1,0:T(8,128)(2,1)S(1)}, u32[]{:S(2)}, u32[]{:S(2)}) %all-to-all-start.1) | async-done | bytes 2293792 | tf_op jit(solution)/shard_map/all_to_all | solution.py:388
  69.9 0.0 copy-start
  69.9 0.0 collective-permute-start.4
  69.9 1.7 %collective-permute-done.3 = bf16[8,80,384]{2,1,0:T(8,128)(2,1)} collective-permute-done((bf16[8,80,384]{2,1,0:T(8,128)(2,1)S(1)}, bf16[8,80,384]{2,1,0:T(8,128)(2,1)}, u32[]{:S(2)}, u32[]{:S(2)}) %collective-permute-start.3) | collective-permute-done | bytes 491552 | tf_op jit(solution)/shard_map/ppermute | solution.py:365
  71.6 1.5 %collective-permute-done.2 = bf16[8,80,384]{2,1,0:T(8,128)(2,1)} collective-permute-done((bf16[8,80,384]{2,1,0:T(8,128)(2,1)S(1)}, bf16[8,80,384]{2,1,0:T(8,128)(2,1)}, u32[]{:S(2)}, u32[]{:S(2)}) %collective-permute-start.2) | collective-permute-done | bytes 491552 | tf_op jit(solution)/shard_map/ppermute | solution.py:365
  73.1 5.7 %lay.1.keys = bf16[2,4,2560,128]{3,2,1,0:T(8,128)(2,1)} custom-call(s32[2]{0:T(128)} %pad_add_fusion.place, bf16[2,4,2,80,384]{4,3,2,1,0:T(8,128)(2,1)} %bitcast.14, bf16[2,4,2,80,384]{4,3,2,1,0:T(8,128)(2,1)} %bitcast.6.up, bf16[1,4,2,80,384]{4,3,2,1,0:T(8,128)(2,1)} %bitcast.7.far_low, bf16[1,4,2,80,384]{4,3,2,1,0:T(8,128)(2,1)} %bitcast.8.far_high, ...), custom_call_target="tpu_custom_call" | custom-call | flops 40000000000 | bytes 10000000 | tf_op jit(solution)/shard_map/lay/pallas_call | solution.py:200
  78.8 0.0 copy-done
  78.8 0.0 collective-permute-done.4
  78.8 0.0 copy-start.2
  78.8 1.4 %copy-done.2 = bf16[16,80,896]{2,1,0:T(8,128)(2,1)} copy-done((bf16[16,80,896]{2,1,0:T(8,128)(2,1)}, bf16[16,80,896]{2,1,0:T(8,128)(2,1)S(1)}, u32[]{:S(2)}) %copy-start.2) | copy-done | bytes 2293784
  80.2 19.4 %attend.1 = bf16[8,2,80,256]{3,2,1,0:T(8,128)(2,1)} custom-call(bf16[8,2,80,896]{3,2,1,0:T(8,128)(2,1)} %bitcast.12, bf16[2,4,2560,128]{3,2,1,0:T(8,128)(2,1)} %lay.1.keys, bf16[8,2,80,896]{3,2,1,0:T(8,128)(2,1)} %bitcast.13, bf16[8,2,80,896]{3,2,1,0:T(8,128)(2,1)} %bitcast.16), custom_call_target="tpu_custom_call" | custom-call | flops 14000000000 | bytes 10000000 | tf_op jit(solution)/shard_map/attend/pallas_call | solution.py:287
  99.6 15.1 %all_to_all.15.attended = bf16[16,80,256]{2,1,0:T(8,128)(2,1)} all-to-all(bf16[16,80,256]{2,1,0:T(8,128)(2,1)} %bitcast.15), channel_id=1, replica_groups=mesh['zh'=2,'x'=4,'y'=4,'zl'=2,'co'=2] {'zh','x','zl'}, dimensions={0} | all-to-all | bytes 1310720 | tf_op jit(solution)/shard_map/all_to_all | solution.py:388
  114.7 3.9 %out.1 = bf16[4,80,768]{2,1,0:T(8,128)(2,1)} custom-call(bf16[16,80,256]{2,1,0:T(8,128)(2,1)} %all_to_all.15.attended, f32[4,80,1024]{2,1,0:T(8,128)} %get-tuple-element.27.gate, f32[4,80,768]{2,1,0:T(8,128)} %get-tuple-element.28.og, bf16[4,80,768]{2,1,0:T(8,128)(2,1)} %act.3, bf16[768,768]{1,0:T(8,128)(2,1)} %wo.1), custom_call_target="tpu_custom_call" | custom-call | flops 2000000000 | bytes 6000000 | tf_op jit(solution)/shard_map/out/pallas_call | solution.py:354
Async XLA Ops:
  8.4 25.1 %all-to-all-start = ((bf16[16,80,384]{2,1,0:T(8,128)(2,1)}), bf16[16,80,384]{2,1,0:T(8,128)(2,1)S(1)}, u32[]{:S(2)}, u32[]{:S(2)}) async-start(bf16[16,80,384]{2,1,0:T(8,128)(2,1)} %get-tuple-element.17), calls=%async_computation | async-start | bytes 1966080 | tf_op jit(solution)/shard_map/all_to_all | solution.py:388
  33.5 3.0 %copy-start.1 = (bf16[16,80,384]{2,1,0:T(8,128)(2,1)}, bf16[16,80,384]{2,1,0:T(8,128)(2,1)S(1)}, u32[]{:S(2)}) copy-start(bf16[16,80,384]{2,1,0:T(8,128)(2,1)S(1)} %all-to-all-done) | copy-start | bytes 2949124
  33.5 22.3 %collective-permute-start.1 = (bf16[16,80,384]{2,1,0:T(8,128)(2,1)S(1)}, bf16[16,80,384]{2,1,0:T(8,128)(2,1)}, u32[]{:S(2)}, u32[]{:S(2)}) collective-permute-start(bf16[16,80,384]{2,1,0:T(8,128)(2,1)S(1)} %all-to-all-done), channel_id=1, source_target_pairs={{0,12},{4,0},{8,4},{12,8},{1,13},{5,1},{9,5},{13,9},{2,14},{6,2},{... | collective-permute-start | bytes 2949128 | tf_op jit(solution)/shard_map/ppermute | solution.py:365
  36.5 22.8 %collective-permute-start = (bf16[16,80,384]{2,1,0:T(8,128)(2,1)S(1)}, bf16[16,80,384]{2,1,0:T(8,128)(2,1)}, u32[]{:S(2)}, u32[]{:S(2)}) collective-permute-start(bf16[16,80,384]{2,1,0:T(8,128)(2,1)S(1)} %all-to-all-done), channel_id=1, source_target_pairs={{0,4},{4,8},{8,12},{12,0},{1,5},{5,9},{9,13},{13,1},{2,6},{6,10},{... | collective-permute-start | bytes 2949128 | tf_op jit(solution)/shard_map/ppermute | solution.py:365
  36.5 33.4 %all-to-all-start.1 = ((bf16[16,80,896]{2,1,0:T(8,128)(2,1)}), bf16[16,80,896]{2,1,0:T(8,128)(2,1)S(1)}, u32[]{:S(2)}, u32[]{:S(2)}) async-start(bf16[16,80,896]{2,1,0:T(8,128)(2,1)} %bias.1), calls=%async_computation.1 | async-start | bytes 4587520 | tf_op jit(solution)/shard_map/all_to_all | solution.py:388
  61.4 10.2 %collective-permute-start.3 = (bf16[8,80,384]{2,1,0:T(8,128)(2,1)S(1)}, bf16[8,80,384]{2,1,0:T(8,128)(2,1)}, u32[]{:S(2)}, u32[]{:S(2)}) collective-permute-start(bf16[8,80,384]{2,1,0:T(8,128)(2,1)S(1)} %slice.7), channel_id=1, source_target_pairs={{0,12},{4,0},{8,4},{12,8},{1,13},{5,1},{9,5},{13,9},{2,14},{6,2},{... | collective-permute-start | bytes 1474568 | tf_op jit(solution)/shard_map/ppermute | solution.py:365
  61.8 11.3 %collective-permute-start.2 = (bf16[8,80,384]{2,1,0:T(8,128)(2,1)S(1)}, bf16[8,80,384]{2,1,0:T(8,128)(2,1)}, u32[]{:S(2)}, u32[]{:S(2)}) collective-permute-start(bf16[8,80,384]{2,1,0:T(8,128)(2,1)S(1)} %slice.6), channel_id=1, source_target_pairs={{0,4},{4,8},{8,12},{12,0},{1,5},{5,9},{9,13},{13,1},{2,6},{6,10},{... | collective-permute-start | bytes 1474568 | tf_op jit(solution)/shard_map/ppermute | solution.py:365
  69.9 8.9 %copy-start = (bf16[16,80,896]{2,1,0:T(8,128)(2,1)}, bf16[16,80,896]{2,1,0:T(8,128)(2,1)S(1)}, u32[]{:S(2)}) copy-start(bf16[16,80,896]{2,1,0:T(8,128)(2,1)S(1)} %all-to-all-done.1) | copy-start | bytes 6881284
  69.9 8.9 %collective-permute-start.4 = (bf16[16,80,896]{2,1,0:T(8,128)(2,1)S(1)}, bf16[16,80,896]{2,1,0:T(8,128)(2,1)S(1)}, u32[]{:S(2)}, u32[]{:S(2)}) collective-permute-start(bf16[16,80,896]{2,1,0:T(8,128)(2,1)S(1)} %all-to-all-done.1), channel_id=1, source_target_pairs={{0,1},{1,0},{2,3},{3,2},{4,5},{5,4},{6,7},{7,6},{8,9},{9,8},{10,11... | collective-permute-start | bytes 6881288 | tf_op jit(solution)/shard_map/ppermute | solution.py:396
  78.8 1.4 %copy-start.2 = (bf16[16,80,896]{2,1,0:T(8,128)(2,1)}, bf16[16,80,896]{2,1,0:T(8,128)(2,1)S(1)}, u32[]{:S(2)}) copy-start(bf16[16,80,896]{2,1,0:T(8,128)(2,1)S(1)} %collective-permute-done.4) | copy-start | bytes 6881284

commit v5 on v4

--- a/solution.py
+++ b/solution.py
@@ -22,6 +22,7 @@
 BF = jnp.bfloat16
 F32 = jnp.float32
 VMEM_BYTES = 56 * 1024 * 1024
+SMALL_VMEM_BYTES = 40 * 1024 * 1024
 NT = (((1,), (1,)), ((), ()))
 
 
@@ -38,22 +39,25 @@
 
 
 def placement():
-    table = np.zeros((2, 2, GROUP, HEAD, GROUP, LANES), np.float32)
-    for head in range(GROUP):
-        for channel in range(HEAD):
-            for which, offset in ((0, HEAD), (1, 64)):
-                table[which, 0, head, channel, head, channel] = 1
-                table[which, 1, head, channel, head, offset + channel] = 1
-    table = table.reshape(2, 2 * GROUP * HEAD, GROUP * LANES)
     pairs = np.zeros((HEADS // 2, 2 * HEAD, HEADS // 2, LANES), np.float32)
     for pair in range(HEADS // 2):
         for channel in range(2 * HEAD):
             pairs[pair, channel, pair, channel] = 1
-    pairs = pairs.reshape(HEADS * HEAD, HEADS // 2 * LANES)
-    return jnp.asarray(table[0], BF), jnp.asarray(table[1], BF), jnp.asarray(pairs, BF)
-
-
-def qkv_kernel(act, cond, mask, kv_place, q_place, ws, wsh, wq, wk, wv, kv_out, q_out, mod_out, cn_out, mod):
+    return jnp.asarray(pairs.reshape(HEADS * HEAD, HEADS // 2 * LANES), BF)
+
+
+def moved(columns, rows, head, to, lane):
+    tile, offset = divmod(head * HEAD, LANES)
+    shift = (to - offset) % LANES
+    take = lambda i: columns[rows, i * LANES:(i + 1) * LANES]
+    turn = lambda x: pltpu.roll(x, shift, axis=1) if shift else x
+    first = turn(take(tile))
+    if offset + HEAD <= LANES:
+        return first
+    return jnp.where(lane < to + LANES - offset, first, turn(take(tile + 1)))
+
+
+def qkv_kernel(act, cond, mask, ws, wsh, wq, wk, wv, kv_out, q_out, mod_out, cn_out, mod):
     samples, tokens, width = act.shape
     rows = samples * tokens
 
@@ -67,34 +71,34 @@
         cn_out[...] = cond_norm.reshape(cn_out.shape)
 
     modulated = mod[...]
-    k = dot(modulated, wk[...]).astype(BF)
-    v = dot(modulated, wv[...]).astype(BF)
-    placed = dot(jnp.concatenate([k, v], axis=1), kv_place[...])
     lane = lax.broadcasted_iota(jnp.int32, (tokens, LANES), 1)
     square = (tokens, tokens)
     diagonal = lax.broadcasted_iota(jnp.int32, square, 0) == lax.broadcasted_iota(jnp.int32, square, 1)
     padded = jnp.broadcast_to(jnp.where(mask[...] > 0, 0.0, 1.0), square)
     padded = jnp.sum(jnp.where(diagonal, padded, 0.0), axis=1, keepdims=True)
     marked = (lane == MARK_LANE) & (padded > 0.5)
+    sample = [slice(s * tokens, (s + 1) * tokens) for s in range(samples)]
+    k = dot(modulated, wk[...])
+    v = dot(modulated, wv[...])
     for h in range(GROUP):
-        tile = placed[:, h * LANES:(h + 1) * LANES]
-        last = tile[3 * tokens:]
+        tile = [
+            jnp.where(lane < HEAD, moved(k, row, h, 0, lane), moved(v, row, h, HEAD, lane)) for row in sample
+        ]
         for s in range(3):
-            spare = pltpu.roll(last, 96 - 32 * s, axis=1)
-            merged = jnp.where(lane < 96, tile[s * tokens:(s + 1) * tokens], spare)
+            spare = pltpu.roll(tile[3], 96 - 32 * s, axis=1)
+            merged = jnp.where(lane < 96, tile[s], spare)
             if s == 0:
                 merged = jnp.where(marked, NEGATIVE, merged)
             kv_out[h, :, s * LANES:(s + 1) * LANES] = merged.astype(BF)
-    q = (dot(modulated, wq[...]) * (LOG2E / math.sqrt(HEAD))).astype(BF)
-    first = jnp.concatenate([q[:tokens], q[2 * tokens:3 * tokens]], axis=0)
-    second = jnp.concatenate([q[tokens:2 * tokens], q[3 * tokens:]], axis=0)
-    placed = dot(jnp.concatenate([first, second], axis=1), q_place[...]).astype(BF)
-    for p in range(samples // 2):
-        for h in range(GROUP):
-            q_out[h, :, p * LANES:(p + 1) * LANES] = placed[p * tokens:(p + 1) * tokens, h * LANES:(h + 1) * LANES]
-
-
-def project_qkv(act, cond, mask, kv_place, q_place, ws, wsh, wq, wk, wv):
+    q = dot(modulated, wq[...]) * (LOG2E / math.sqrt(HEAD))
+    for h in range(GROUP):
+        for p in range(samples // 2):
+            first = moved(q, sample[2 * p], h, 0, lane)
+            second = moved(q, sample[2 * p + 1], h, 64, lane)
+            q_out[h, :, p * LANES:(p + 1) * LANES] = jnp.where(lane < 64, first, second).astype(BF)
+
+
+def project_qkv(act, cond, mask, ws, wsh, wq, wk, wv):
     samples, tokens, width = act.shape
     steps = HEADS // GROUP
     columns = GROUP * HEAD
@@ -103,7 +107,7 @@
     return pl.pallas_call(
         qkv_kernel,
         grid=(steps,),
-        in_specs=[whole(act), whole(cond), whole(mask), whole(kv_place), whole(q_place), whole(ws), whole(wsh), part, part, part],
+        in_specs=[whole(act), whole(cond), whole(mask), whole(ws), whole(wsh), part, part, part],
         out_specs=[
             pl.BlockSpec((GROUP, tokens, 3 * LANES), lambda g: (g, 0, 0)),
             pl.BlockSpec((GROUP, tokens, 2 * LANES), lambda g: (g, 0, 0)),
@@ -120,7 +124,7 @@
         compiler_params=pltpu.CompilerParams(vmem_limit_bytes=VMEM_BYTES),
         cost_estimate=pl.CostEstimate(flops=4_000_000_000, bytes_accessed=10_000_000, transcendentals=300_000),
         name="qkv",
-    )(act, cond, mask, kv_place, q_place, ws, wsh, wq, wk, wv)
+    )(act, cond, mask, ws, wsh, wq, wk, wv)
 
 
 def bias_kernel(pair, w_bias, q, out, rows):
@@ -206,7 +210,7 @@
             out_specs=pl.BlockSpec((1, 4, extent, LANES), lambda z, c: (z, 0, 0, 0)),
         ),
         out_shape=jax.ShapeDtypeStruct((2, 4, extent, LANES), BF),
-        compiler_params=pltpu.CompilerParams(vmem_limit_bytes=VMEM_BYTES),
+        compiler_params=pltpu.CompilerParams(vmem_limit_bytes=SMALL_VMEM_BYTES),
         cost_estimate=pl.CostEstimate(flops=40_000_000_000, bytes_accessed=10_000_000, transcendentals=0),
         name="lay",
     )(place, *kv)
@@ -295,7 +299,7 @@
         ],
         out_specs=pl.BlockSpec((8, 1, tokens, LANES), lambda z, p: (0, z, 0, p)),
         out_shape=jax.ShapeDtypeStruct((8, 2, tokens, 2 * LANES), BF),
-        compiler_params=pltpu.CompilerParams(vmem_limit_bytes=VMEM_BYTES),
+        compiler_params=pltpu.CompilerParams(vmem_limit_bytes=SMALL_VMEM_BYTES),
         cost_estimate=pl.CostEstimate(flops=14_000_000_000, bytes_accessed=10_000_000, transcendentals=13_000_000),
         name="attend",
     )(own, keys, own, other)
@@ -318,7 +322,7 @@
             jax.ShapeDtypeStruct((samples, tokens, HEADS // 2 * LANES), F32),
             jax.ShapeDtypeStruct(mod.shape, F32),
         ],
-        compiler_params=pltpu.CompilerParams(vmem_limit_bytes=VMEM_BYTES),
+        compiler_params=pltpu.CompilerParams(vmem_limit_bytes=SMALL_VMEM_BYTES),
         cost_estimate=pl.CostEstimate(flops=32_000_000_000, bytes_accessed=9_000_000, transcendentals=1_000_000),
         name="gates",
     )(mod, cn, place, wg, wog)
@@ -355,7 +359,7 @@
         out_kernel,
         out_shape=jax.ShapeDtypeStruct(act.shape, BF),
         scratch_shapes=[pltpu.VMEM((HEADS // 2 * LANES, width), BF)],
-        compiler_params=pltpu.CompilerParams(vmem_limit_bytes=VMEM_BYTES),
+        compiler_params=pltpu.CompilerParams(vmem_limit_bytes=SMALL_VMEM_BYTES),
         cost_estimate=pl.CostEstimate(flops=2_000_000_000, bytes_accessed=6_000_000, transcendentals=0),
         name="out",
     )(attended, gate, og, act, wo)
@@ -381,16 +385,15 @@
     w_bias,
 ):
     tokens = activations.shape[1]
-    kv_place, q_place, gate_place = placement()
     kv, q, modulated, cond_norm = project_qkv(
-        activations, conditioning, key_mask.reshape(1, tokens), kv_place, q_place, w_scale, w_shift, w_query, w_key, w_value
+        activations, conditioning, key_mask.reshape(1, tokens), w_scale, w_shift, w_query, w_key, w_value
     )
     exchange = lambda a: lax.all_to_all(a, XZ, 0, 0, tiled=True)
     bias = project_bias(pair_features, w_bias.T, q)
     kv, bias = lax.optimization_barrier((exchange(kv), bias))
     up, down = ring(kv, 1), ring(kv, 3)
     own = exchange(bias)
-    gate, out_gate = gates(modulated, cond_norm, gate_place, w_gate, w_outgate)
+    gate, out_gate = gates(modulated, cond_norm, placement(), w_gate, w_outgate)
     up, down, gate, out_gate = lax.optimization_barrier((up, down, gate, out_gate))
     far = (ring(up[:HEADS // 2], 1), ring(down[HEADS // 2:], 3))
     other = lax.ppermute(own, "co", [(0, 1), (1, 0)])

time: 120 us -> 111 us (0.925)
  Pallas kernels: 54.7 us -> 43 us
  local copies, waits for them, and re-layouts: 3.57 us -> 10.5 us
  waiting for transfers between devices: 27.8 us -> 25 us
    unnamed x6 -> x22, local copies, waits for them, and re-layouts: 1.41 us -> 6.81 us
    pallas_call x1, Pallas kernels: 5.41 us -> 2.15 us  [gates(): pl.pallas_call(gate_kernel, out_shape=[jax.ShapeDtypeStruct((samples, tok...]
    pallas_call x1, Pallas kernels: 19.4 us -> 16.9 us  [attend(): pl.pallas_call(attend_kernel, grid=(2, 2), in_specs=[pl.BlockSpec((8, 1,...]
    pallas_call x1, Pallas kernels: 3.9 us -> 1.61 us  [project_out(): pl.pallas_call(out_kernel, out_shape=jax.ShapeDtypeStruct(act.shape, BF),...]
    pallas_call x1, Pallas kernels: 8.42 us -> 6.57 us  [project_qkv(): pl.pallas_call(qkv_kernel, grid=(steps,), in_specs=[whole(act), whole(con...]
    pallas_call x1, Pallas kernels: 5.7 us -> 3.91 us  [lay_keys(): pl.pallas_call(lay_kernel, grid_spec=pltpu.PrefetchScalarGridSpec(num_sca...]
    ppermute x4, waiting for transfers between devices: 16.8 us -> 15 us  [ring(): return lax.ppermute(block, 'y', [(i, (i + step) % 4) for i in range(4)])]
    slice x2, local copies, waits for them, and re-layouts: 2.16 us -> 3.74 us  [per_device(): far = (ring(up[:HEADS // 2], 1), ring(down[HEADS // 2:], 3))]
  transfers between devices with their start and end apart: 7 -> 7, of which waited for: 6 -> 6; matrix products, arithmetic and copies ran while one was open for 2% -> 3% of each run, Pallas kernels for 19% -> 16%
where the time goes in v5:
time: 111 us; the launch traced here: 110 us
  Pallas kernels  43 us (39%)
  waiting for transfers between devices  25 us (23%)
  starting transfers between devices  16.7 us (15%)
  blocking collectives  14.7 us (13%)
  local copies, waits for them, and re-layouts  10.5 us (9%)
    pallas_call x1, Pallas kernels, attend(): pl.pallas_call(attend_kernel, grid=(2, 2), in_specs=[pl.BlockSpec((8, 1,...  16.9 us
    ppermute x4, waiting for transfers between devices, ring(): return lax.ppermute(block, 'y', [(i, (i + step) % 4) for i in range(4)])  15 us
    all_to_all x1, blocking collectives, per_device(): exchange = lambda a: lax.all_to_all(a, XZ, 0, 0, tiled=True)  14.7 us
    pallas_call x1, Pallas kernels, project_bias(): pl.pallas_call(bias_kernel, grid=(queries // step,), in_specs=[pl.BlockSp...  11.9 us
    all_to_all x2, starting transfers between devices, per_device(): exchange = lambda a: lax.all_to_all(a, XZ, 0, 0, tiled=True)  11.7 us
    all_to_all x2, waiting for transfers between devices, per_device(): exchange = lambda a: lax.all_to_all(a, XZ, 0, 0, tiled=True)  9.95 us
    unnamed x22, local copies, waits for them, and re-layouts  6.81 us
    pallas_call x1, Pallas kernels, project_qkv(): pl.pallas_call(qkv_kernel, grid=(steps,), in_specs=[whole(act), whole(con...  6.57 us
  transfers between devices with their start and end apart: 7, of which 6 were waited for; matrix products, arithmetic and copies ran while one was open for 3% of the time, Pallas kernels for 16%

profile of v5, /device:TPU:0, one launch (start us, length us, event | category | flops | bytes accessed | tf_op | source)
XLA Modules:
  0.0 110.2 jit_solution(2172050636757710802)
XLA Ops:
  0.0 6.6 %qkv.1 = (bf16[16,80,384]{2,1,0:T(8,128)(2,1)}, bf16[16,80,256]{2,1,0:T(8,128)(2,1)}, bf16[4,80,768]{2,1,0:T(8,128)(2,1)}, bf16[4,80,384]{2,1,0:T(8,128)(2,1)}) custom-call(bf16[4,80,768]{2,1,0:T(8,128)(2,1)} %act.3, bf16[4,80,384]{2,1,0:T(8,128)(2,1)} %cond.1, s32[1,80]{1,0:T(1,128)} %bitcast.18, bf16[384,768]{1,0:T(8,128)(2,1)} %ws.1, ...), custom_call_target="tpu_custom_call" | custom-call | flops 4000000000 | bytes 10000000 | tf_op jit(solution)/shard_map/qkv/pallas_call | solution.py:107
  6.6 8.0 %all-to-all-start = ((bf16[16,80,384]{2,1,0:T(8,128)(2,1)}), bf16[16,80,384]{2,1,0:T(8,128)(2,1)S(1)}, u32[]{:S(2)}, u32[]{:S(2)}) async-start(bf16[16,80,384]{2,1,0:T(8,128)(2,1)} %get-tuple-element.17), calls=%async_computation | async-start | bytes 1966080 | tf_op jit(solution)/shard_map/all_to_all | solution.py:391
  14.6 11.9 %bias.1 = bf16[16,80,896]{2,1,0:T(8,128)(2,1)} custom-call(bf16[80,640,128]{2,1,0:T(8,128)(2,1)} %pair.1, bf16[16,128]{1,0:T(8,128)(2,1)} %bitcast.17, bf16[16,80,256]{2,1,0:T(8,128)(2,1)} %get-tuple-element.18.q), custom_call_target="tpu_custom_call" | custom-call | flops 10000000000 | bytes 15000000 | tf_op jit(solution)/shard_map/bias/pallas_call | solution.py:152
  26.4 0.0 copy-start.10
  26.4 5.2 %all-to-all-done = bf16[16,80,384]{2,1,0:T(8,128)(2,1)S(1)} async-done(((bf16[16,80,384]{2,1,0:T(8,128)(2,1)}), bf16[16,80,384]{2,1,0:T(8,128)(2,1)S(1)}, u32[]{:S(2)}, u32[]{:S(2)}) %all-to-all-start) | async-done | bytes 983072 | tf_op jit(solution)/shard_map/all_to_all | solution.py:391
  31.6 3.0 %collective-permute-start.1 = (bf16[16,80,384]{2,1,0:T(8,128)(2,1)S(1)}, bf16[16,80,384]{2,1,0:T(8,128)(2,1)}, u32[]{:S(2)}, u32[]{:S(2)}) collective-permute-start(bf16[16,80,384]{2,1,0:T(8,128)(2,1)S(1)} %all-to-all-done), channel_id=1, source_target_pairs={{0,12},{4,0},{8,4},{12,8},{1,13},{5,1},{9,5},{13,9},{2,14},{6,2},{... | collective-permute-start | bytes 2949128 | tf_op jit(solution)/shard_map/ppermute | solution.py:369
  34.6 0.0 collective-permute-start
  34.6 3.7 %all-to-all-start.1 = ((bf16[16,80,896]{2,1,0:T(8,128)(2,1)}), bf16[16,80,896]{2,1,0:T(8,128)(2,1)S(1)}, u32[]{:S(2)}, u32[]{:S(2)}) async-start(bf16[16,80,896]{2,1,0:T(8,128)(2,1)} %bias.1), calls=%async_computation.1 | async-start | bytes 4587520 | tf_op jit(solution)/shard_map/all_to_all | solution.py:391
  38.4 0.0 copy-done.10
  38.4 0.0 copy-start
  38.4 1.3 %copy-done = bf16[768,768]{1,0:T(8,128)(2,1)S(1)} copy-done((bf16[768,768]{1,0:T(8,128)(2,1)S(1)}, bf16[768,768]{1,0:T(8,128)(2,1)}, u32[]{:S(2)}) %copy-start) | copy-done | bytes 1179672
  39.7 0.0 copy-start.2
  39.7 1.1 copy-done.2
  40.7 0.0 copy-start.4
  40.7 1.4 %copy-done.4 = bf16[768,1024]{1,0:T(8,128)(2,1)S(1)} copy-done((bf16[768,1024]{1,0:T(8,128)(2,1)S(1)}, bf16[768,1024]{1,0:T(8,128)(2,1)}, u32[]{:S(2)}) %copy-start.4) | copy-done | bytes 1572888
  42.1 0.0 copy-start.9
  42.1 1.0 copy-done.9
  43.2 2.1 %gates.1 = (f32[4,80,1024]{2,1,0:T(8,128)S(1)}, f32[4,80,768]{2,1,0:T(8,128)S(1)}) custom-call(bf16[4,80,768]{2,1,0:T(8,128)(2,1)S(1)} %copy-done.9, bf16[4,80,384]{2,1,0:T(8,128)(2,1)S(1)} %copy-done.10, bf16[768,1024]{1,0:T(8,128)(2,1)S(1)} %copy-done.4, bf16[768,768]{1,0:T(8,128)(2,1)S(1)} %copy-done, bf16[384,768]{1,0:T(8,128)(2,1)S(1)} %copy-done.2), custom_call_target="tpu_custom_call" | custom-call | flops 32000000000 | bytes 9000000 | tf_op jit(solution)/shard_map/gates/pallas_call | solution.py:319
  45.3 0.0 copy-start.5
  45.3 1.1 copy-done.5
  46.4 0.0 copy-start.7
  46.4 0.9 copy-done.7
  47.3 6.6 %collective-permute-done.1 = bf16[16,80,384]{2,1,0:T(8,128)(2,1)} collective-permute-done((bf16[16,80,384]{2,1,0:T(8,128)(2,1)S(1)}, bf16[16,80,384]{2,1,0:T(8,128)(2,1)}, u32[]{:S(2)}, u32[]{:S(2)}) %collective-permute-start.1) | collective-permute-done | bytes 983072 | tf_op jit(solution)/shard_map/ppermute | solution.py:369
  53.9 3.5 %collective-permute-done = bf16[16,80,384]{2,1,0:T(8,128)(2,1)} collective-permute-done((bf16[16,80,384]{2,1,0:T(8,128)(2,1)S(1)}, bf16[16,80,384]{2,1,0:T(8,128)(2,1)}, u32[]{:S(2)}, u32[]{:S(2)}) %collective-permute-start) | collective-permute-done | bytes 983072 | tf_op jit(solution)/shard_map/ppermute | solution.py:369
  57.4 1.9 %slice.6 = bf16[8,80,384]{2,1,0:T(8,128)(2,1)} slice(bf16[16,80,384]{2,1,0:T(8,128)(2,1)} %collective-permute-done), slice={[0:8], [0:80], [0:384]} | slice | bytes 983040 | tf_op jit(solution)/shard_map/slice | solution.py:398
  59.3 1.9 %slice.7 = bf16[8,80,384]{2,1,0:T(8,128)(2,1)} slice(bf16[16,80,384]{2,1,0:T(8,128)(2,1)} %collective-permute-done.1), slice={[8:16], [0:80], [0:384]} | slice | bytes 983040 | tf_op jit(solution)/shard_map/slice | solution.py:398
  61.2 0.3 collective-permute-start.3
  61.4 1.7 %collective-permute-start.2 = (bf16[8,80,384]{2,1,0:T(8,128)(2,1)}, bf16[8,80,384]{2,1,0:T(8,128)(2,1)}, u32[]{:S(2)}, u32[]{:S(2)}) collective-permute-start(bf16[8,80,384]{2,1,0:T(8,128)(2,1)} %slice.6), channel_id=1, source_target_pairs={{0,4},{4,8},{8,12},{12,0},{1,5},{5,9},{9,13},{13,1},{2,6},{6,10},{... | collective-permute-start | bytes 1474568 | tf_op jit(solution)/shard_map/ppermute | solution.py:369
  63.2 0.1 pad_add_fusion.place
  63.3 4.8 %all-to-all-done.1 = bf16[16,80,896]{2,1,0:T(8,128)(2,1)S(1)} async-done(((bf16[16,80,896]{2,1,0:T(8,128)(2,1)}), bf16[16,80,896]{2,1,0:T(8,128)(2,1)S(1)}, u32[]{:S(2)}, u32[]{:S(2)}) %all-to-all-start.1) | async-done | bytes 2293792 | tf_op jit(solution)/shard_map/all_to_all | solution.py:391
  68.0 0.0 collective-permute-start.4
  68.0 3.4 %collective-permute-done.3 = bf16[8,80,384]{2,1,0:T(8,128)(2,1)} collective-permute-done((bf16[8,80,384]{2,1,0:T(8,128)(2,1)}, bf16[8,80,384]{2,1,0:T(8,128)(2,1)}, u32[]{:S(2)}, u32[]{:S(2)}) %collective-permute-start.3) | collective-permute-done | bytes 491552 | tf_op jit(solution)/shard_map/ppermute | solution.py:369
  71.5 1.5 %collective-permute-done.2 = bf16[8,80,384]{2,1,0:T(8,128)(2,1)} collective-permute-done((bf16[8,80,384]{2,1,0:T(8,128)(2,1)}, bf16[8,80,384]{2,1,0:T(8,128)(2,1)}, u32[]{:S(2)}, u32[]{:S(2)}) %collective-permute-start.2) | collective-permute-done | bytes 491552 | tf_op jit(solution)/shard_map/ppermute | solution.py:369
  73.0 3.9 %lay.1.keys = bf16[2,4,2560,128]{3,2,1,0:T(8,128)(2,1)S(1)} custom-call(s32[2]{0:T(128)S(1)} %pad_add_fusion.place, bf16[2,4,2,80,384]{4,3,2,1,0:T(8,128)(2,1)S(1)} %bitcast.14, bf16[2,4,2,80,384]{4,3,2,1,0:T(8,128)(2,1)} %bitcast.6.up, bf16[1,4,2,80,384]{4,3,2,1,0:T(8,128)(2,1)} %bitcast.7.far_low, bf16[1,4,2,80,384]{4,3,2,1,0:T(8,128)(2,1)} %bitcast.8.far_high, ...), custom_call_target="tpu_custom_call" | custom-call | flops 40000000000 | bytes 10000000 | tf_op jit(solution)/shard_map/lay/pallas_call | solution.py:204
  76.9 0.0 collective-permute-done.4
  76.9 0.0 copy-start.1
  76.9 0.0 copy-start.3
  76.9 0.0 copy-start.6
  76.9 0.0 copy-start.8
  77.0 16.9 %attend.1 = bf16[8,2,80,256]{3,2,1,0:T(8,128)(2,1)S(1)} custom-call(bf16[8,2,80,896]{3,2,1,0:T(8,128)(2,1)S(1)} %bitcast.12, bf16[2,4,2560,128]{3,2,1,0:T(8,128)(2,1)S(1)} %lay.1.keys, bf16[8,2,80,896]{3,2,1,0:T(8,128)(2,1)S(1)} %bitcast.13, bf16[8,2,80,896]{3,2,1,0:T(8,128)(2,1)S(1)} %bitcast.16), custom_call_target="tpu_custom_call" | custom-call | flops 14000000000 | bytes 10000000 | tf_op jit(solution)/shard_map/attend/pallas_call | solution.py:291
  93.8 14.7 %all_to_all.15.attended = bf16[16,80,256]{2,1,0:T(8,128)(2,1)S(1)} all-to-all(bf16[16,80,256]{2,1,0:T(8,128)(2,1)S(1)} %bitcast.15), channel_id=1, replica_groups=mesh['zh'=2,'x'=4,'y'=4,'zl'=2,'co'=2] {'zh','x','zl'}, dimensions={0} | all-to-all | bytes 1310720 | tf_op jit(solution)/shard_map/all_to_all | solution.py:391
  108.6 0.0 copy-done.1
  108.6 0.0 copy-done.3
  108.6 0.0 copy-done.6
  108.6 0.0 copy-done.8
  108.6 1.6 %out.1 = bf16[4,80,768]{2,1,0:T(8,128)(2,1)} custom-call(bf16[16,80,256]{2,1,0:T(8,128)(2,1)S(1)} %all_to_all.15.attended, f32[4,80,1024]{2,1,0:T(8,128)S(1)} %copy-done.6, f32[4,80,768]{2,1,0:T(8,128)S(1)} %copy-done.8, bf16[4,80,768]{2,1,0:T(8,128)(2,1)S(1)} %copy-done.3, bf16[768,768]{1,0:T(8,128)(2,1)S(1)} %copy-done.1), custom_call_target="tpu_custom_call" | custom-call | flops 2000000000 | bytes 6000000 | tf_op jit(solution)/shard_map/out/pallas_call | solution.py:358
Async XLA Ops:
  6.6 25.0 %all-to-all-start = ((bf16[16,80,384]{2,1,0:T(8,128)(2,1)}), bf16[16,80,384]{2,1,0:T(8,128)(2,1)S(1)}, u32[]{:S(2)}, u32[]{:S(2)}) async-start(bf16[16,80,384]{2,1,0:T(8,128)(2,1)} %get-tuple-element.17), calls=%async_computation | async-start | bytes 1966080 | tf_op jit(solution)/shard_map/all_to_all | solution.py:391
  26.4 11.9 %copy-start.10 = (bf16[4,80,384]{2,1,0:T(8,128)(2,1)S(1)}, bf16[4,80,384]{2,1,0:T(8,128)(2,1)}, u32[]{:S(2)}) copy-start(bf16[4,80,384]{2,1,0:T(8,128)(2,1)} %get-tuple-element.22.cn) | copy-start | bytes 737284
  31.6 22.3 %collective-permute-start.1 = (bf16[16,80,384]{2,1,0:T(8,128)(2,1)S(1)}, bf16[16,80,384]{2,1,0:T(8,128)(2,1)}, u32[]{:S(2)}, u32[]{:S(2)}) collective-permute-start(bf16[16,80,384]{2,1,0:T(8,128)(2,1)S(1)} %all-to-all-done), channel_id=1, source_target_pairs={{0,12},{4,0},{8,4},{12,8},{1,13},{5,1},{9,5},{13,9},{2,14},{6,2},{... | collective-permute-start | bytes 2949128 | tf_op jit(solution)/shard_map/ppermute | solution.py:369
  34.6 22.8 %collective-permute-start = (bf16[16,80,384]{2,1,0:T(8,128)(2,1)S(1)}, bf16[16,80,384]{2,1,0:T(8,128)(2,1)}, u32[]{:S(2)}, u32[]{:S(2)}) collective-permute-start(bf16[16,80,384]{2,1,0:T(8,128)(2,1)S(1)} %all-to-all-done), channel_id=1, source_target_pairs={{0,4},{4,8},{8,12},{12,0},{1,5},{5,9},{9,13},{13,1},{2,6},{6,10},{... | collective-permute-start | bytes 2949128 | tf_op jit(solution)/shard_map/ppermute | solution.py:369
  34.6 33.4 %all-to-all-start.1 = ((bf16[16,80,896]{2,1,0:T(8,128)(2,1)}), bf16[16,80,896]{2,1,0:T(8,128)(2,1)S(1)}, u32[]{:S(2)}, u32[]{:S(2)}) async-start(bf16[16,80,896]{2,1,0:T(8,128)(2,1)} %bias.1), calls=%async_computation.1 | async-start | bytes 4587520 | tf_op jit(solution)/shard_map/all_to_all | solution.py:391
  38.4 1.3 %copy-start = (bf16[768,768]{1,0:T(8,128)(2,1)S(1)}, bf16[768,768]{1,0:T(8,128)(2,1)}, u32[]{:S(2)}) copy-start(bf16[768,768]{1,0:T(8,128)(2,1)} %wg.1) | copy-start | bytes 3538948
  39.7 1.1 copy-start.2
  40.7 1.4 %copy-start.4 = (bf16[768,1024]{1,0:T(8,128)(2,1)S(1)}, bf16[768,1024]{1,0:T(8,128)(2,1)}, u32[]{:S(2)}) copy-start(bf16[768,1024]{1,0:T(8,128)(2,1)} %constant.11.clone.place) | copy-start | bytes 4718596
  42.1 1.0 copy-start.9
  45.3 1.1 copy-start.5
  46.4 0.9 copy-start.7
  61.2 10.3 %collective-permute-start.3 = (bf16[8,80,384]{2,1,0:T(8,128)(2,1)}, bf16[8,80,384]{2,1,0:T(8,128)(2,1)}, u32[]{:S(2)}, u32[]{:S(2)}) collective-permute-start(bf16[8,80,384]{2,1,0:T(8,128)(2,1)} %slice.7), channel_id=1, source_target_pairs={{0,12},{4,0},{8,4},{12,8},{1,13},{5,1},{9,5},{13,9},{2,14},{6,2},{... | collective-permute-start | bytes 1474568 | tf_op jit(solution)/shard_map/ppermute | solution.py:369
  61.4 11.5 %collective-permute-start.2 = (bf16[8,80,384]{2,1,0:T(8,128)(2,1)}, bf16[8,80,384]{2,1,0:T(8,128)(2,1)}, u32[]{:S(2)}, u32[]{:S(2)}) collective-permute-start(bf16[8,80,384]{2,1,0:T(8,128)(2,1)} %slice.6), channel_id=1, source_target_pairs={{0,4},{4,8},{8,12},{12,0},{1,5},{5,9},{9,13},{13,1},{2,6},{6,10},{... | collective-permute-start | bytes 1474568 | tf_op jit(solution)/shard_map/ppermute | solution.py:369
  68.0 8.9 %collective-permute-start.4 = (bf16[16,80,896]{2,1,0:T(8,128)(2,1)S(1)}, bf16[16,80,896]{2,1,0:T(8,128)(2,1)S(1)}, u32[]{:S(2)}, u32[]{:S(2)}) collective-permute-start(bf16[16,80,896]{2,1,0:T(8,128)(2,1)S(1)} %all-to-all-done.1), channel_id=1, source_target_pairs={{0,1},{1,0},{2,3},{3,2},{4,5},{5,4},{6,7},{7,6},{8,9},{9,8},{10,11... | collective-permute-start | bytes 6881288 | tf_op jit(solution)/shard_map/ppermute | solution.py:399
  76.9 31.7 %copy-start.1 = (bf16[768,768]{1,0:T(8,128)(2,1)S(1)}, bf16[768,768]{1,0:T(8,128)(2,1)}, u32[]{:S(2)}) copy-start(bf16[768,768]{1,0:T(8,128)(2,1)} %wo.1) | copy-start | bytes 3538948
  76.9 31.6 %copy-start.3 = (bf16[4,80,768]{2,1,0:T(8,128)(2,1)S(1)}, bf16[4,80,768]{2,1,0:T(8,128)(2,1)}, u32[]{:S(2)}) copy-start(bf16[4,80,768]{2,1,0:T(8,128)(2,1)} %act.3) | copy-start | bytes 1474564
  76.9 31.6 %copy-start.6 = (f32[4,80,1024]{2,1,0:T(8,128)S(1)}, f32[4,80,1024]{2,1,0:T(8,128)}, u32[]{:S(2)}) copy-start(f32[4,80,1024]{2,1,0:T(8,128)} %copy-done.5) | copy-start | bytes 3932164
  76.9 31.6 %copy-start.8 = (f32[4,80,768]{2,1,0:T(8,128)S(1)}, f32[4,80,768]{2,1,0:T(8,128)}, u32[]{:S(2)}) copy-start(f32[4,80,768]{2,1,0:T(8,128)} %copy-done.7) | copy-start | bytes 2949124

commit v6 on v5

--- a/solution.py
+++ b/solution.py
@@ -14,7 +14,7 @@
 HEADS = 16
 HEAD = 48
 LANES = 128
-GROUP = 8
+GROUP = 16
 MARK_LANE = 95
 PAD_LANE = 96
 SUM_LANE = 97
@@ -229,8 +229,8 @@
             pair_q = pltpu.roll(pair_q.astype(F32), 64, axis=1).astype(BF)
         return jnp.where(lane < HEAD, pair_q, pad_one)
 
-    def scores(t, s, at, width):
-        part = lax.dot_general(query(t, s), keys[0, s, at:at + width], NT, preferred_element_type=F32)
+    def scores(mine, t, s, at, width):
+        part = lax.dot_general(mine, keys[0, s, at:at + width], NT, preferred_element_type=F32)
         columns = at % chunk
         bias = own if at // chunk % 2 == 0 else other
         bias = bias[pl.ds(t * T, T), at // chunk // 2, :, columns:columns + width].reshape(span, width)
@@ -246,14 +246,15 @@
         out[pl.ds(t * T, T), 0] = merged.reshape(T, tokens, LANES)
 
     pieces = [(t, s, at) for t in range(8 // T) for s in range(2) for at in range(0, 4 * chunk, PIECE)]
-    following = scores(*pieces[0], PIECE)
+    mine = {block: query(*block) for block in {piece[:2]: None for piece in pieces}}
+    following = scores(mine[pieces[0][:2]], *pieces[0], PIECE)
     top, total, pair, worst = None, None, [], jnp.float32(0.0)
     for i, (t, s, at) in enumerate(pieces):
         current = following
         if at == 0:
             top, total = jnp.max(current, axis=1, keepdims=True), None
         if i + 1 < len(pieces):
-            following = scores(*pieces[i + 1], PIECE)
+            following = scores(mine[pieces[i + 1][:2]], *pieces[i + 1], PIECE)
         part = values(jnp.exp2(current - top).astype(BF), s, at, PIECE)
         total = part if total is None else total + part
         if at == 4 * chunk - PIECE:
@@ -270,11 +271,12 @@
             pair = []
             for s in range(2):
                 top = total = None
+                row = query(t, s)
                 for at in range(0, 4 * chunk, chunk):
-                    peak = jnp.max(scores(t, s, at, chunk), axis=1, keepdims=True)
+                    peak = jnp.max(scores(row, t, s, at, chunk), axis=1, keepdims=True)
                     top = peak if top is None else jnp.maximum(top, peak)
                 for at in range(0, 4 * chunk, chunk):
-                    p = jnp.exp2(scores(t, s, at, chunk) - top).astype(BF)
+                    p = jnp.exp2(scores(row, t, s, at, chunk) - top).astype(BF)
                     part = values(p, s, at, chunk)
                     total = part if total is None else total + part
                 pair.append(total / total[:, SUM_LANE:SUM_LANE + 1])
@@ -363,6 +365,27 @@
         cost_estimate=pl.CostEstimate(flops=2_000_000_000, bytes_accessed=6_000_000, transcendentals=0),
         name="out",
     )(attended, gate, og, act, wo)
+
+
+def halves_kernel(first, second, first_out, second_out):
+    first_out[...] = first[...]
+    second_out[...] = second[...]
+
+
+def halves(first, second):
+    block = (first.shape[0] // 2,) + first.shape[1:]
+    low = pl.BlockSpec(block, lambda i: (0, 0, 0))
+    high = pl.BlockSpec(block, lambda i: (1, 0, 0))
+    return pl.pallas_call(
+        halves_kernel,
+        grid=(1,),
+        in_specs=[low, high],
+        out_specs=[low, low],
+        out_shape=[jax.ShapeDtypeStruct(block, first.dtype)] * 2,
+        compiler_params=pltpu.CompilerParams(vmem_limit_bytes=SMALL_VMEM_BYTES),
+        cost_estimate=pl.CostEstimate(flops=0, bytes_accessed=2_000_000, transcendentals=0),
+        name="halves",
+    )(first, second)
 
 
 def ring(block, step):
@@ -395,7 +418,8 @@
     own = exchange(bias)
     gate, out_gate = gates(modulated, cond_norm, placement(), w_gate, w_outgate)
     up, down, gate, out_gate = lax.optimization_barrier((up, down, gate, out_gate))
-    far = (ring(up[:HEADS // 2], 1), ring(down[HEADS // 2:], 3))
+    up_half, down_half = halves(up, down)
+    far = (ring(up_half, 1), ring(down_half, 3))
     other = lax.ppermute(own, "co", [(0, 1), (1, 0)])
     place = jnp.stack([lax.axis_index("co"), lax.axis_index("y")]).astype(jnp.int32)
     kv = [a.reshape(-1, 4, 2, tokens, kv.shape[-1]) for a in (kv, up, *far, down)]

time: 111 us -> 109 us (0.982)
  local copies, waits for them, and re-layouts: 10.5 us -> 6.82 us
  Pallas kernels: 43 us -> 44.9 us
  waiting for transfers between devices: 25 us -> 23.5 us
  starting transfers between devices: 16.7 us -> 17.9 us
    slice x2 -> x0, local copies, waits for them, and re-layouts: 3.74 us -> none  [per_device(): far = (ring(up[:HEADS // 2], 1), ring(down[HEADS // 2:], 3))]
    pallas_call x0 -> x1, Pallas kernels: none -> 2.2 us  [halves(): pl.pallas_call(halves_kernel, grid=(1,), in_specs=[low, high], out_specs=...]
    ppermute x4, waiting for transfers between devices: 15 us -> 13.1 us  [ring(): return lax.ppermute(block, 'y', [(i, (i + step) % 4) for i in range(4)])]
    ppermute x4, starting transfers between devices: 5.04 us -> 6.25 us  [ring(): return lax.ppermute(block, 'y', [(i, (i + step) % 4) for i in range(4)])]
  transfers between devices with their start and end apart: 7 -> 7, of which waited for: 6 -> 5; matrix products, arithmetic and copies ran while one was open for 3% -> 0% of each run, Pallas kernels for 16% -> 19%
where the time goes in v6:
time: 109 us; the launch traced here: 108 us
  Pallas kernels  44.9 us (41%)
  waiting for transfers between devices  23.5 us (22%)
  starting transfers between devices  17.9 us (16%)
  blocking collectives  14.8 us (14%)
  local copies, waits for them, and re-layouts  6.82 us (6%)
    pallas_call x1, Pallas kernels, attend(): pl.pallas_call(attend_kernel, grid=(2, 2), in_specs=[pl.BlockSpec((8, 1,...  16.9 us
    all_to_all x1, blocking collectives, per_device(): exchange = lambda a: lax.all_to_all(a, XZ, 0, 0, tiled=True)  14.8 us
    ppermute x4, waiting for transfers between devices, ring(): return lax.ppermute(block, 'y', [(i, (i + step) % 4) for i in range(4)])  13.1 us
    pallas_call x1, Pallas kernels, project_bias(): pl.pallas_call(bias_kernel, grid=(queries // step,), in_specs=[pl.BlockSp...  11.9 us
    all_to_all x2, starting transfers between devices, per_device(): exchange = lambda a: lax.all_to_all(a, XZ, 0, 0, tiled=True)  11.7 us
    all_to_all x2, waiting for transfers between devices, per_device(): exchange = lambda a: lax.all_to_all(a, XZ, 0, 0, tiled=True)  10.3 us
    unnamed x22, local copies, waits for them, and re-layouts  6.82 us
    pallas_call x1, Pallas kernels, project_qkv(): pl.pallas_call(qkv_kernel, grid=(steps,), in_specs=[whole(act), whole(con...  6.3 us
  transfers between devices with their start and end apart: 7, of which 5 were waited for; matrix products, arithmetic and copies ran while one was open for 0% of the time, Pallas kernels for 19%

profile of v6, /device:TPU:0, one launch (start us, length us, event | category | flops | bytes accessed | tf_op | source)
XLA Modules:
  0.0 108.1 jit_solution(5032880024539845868)
XLA Ops:
  0.0 6.3 %qkv.1 = (bf16[16,80,384]{2,1,0:T(8,128)(2,1)}, bf16[16,80,256]{2,1,0:T(8,128)(2,1)}, bf16[4,80,768]{2,1,0:T(8,128)(2,1)}, bf16[4,80,384]{2,1,0:T(8,128)(2,1)}) custom-call(bf16[4,80,768]{2,1,0:T(8,128)(2,1)} %act.3, bf16[4,80,384]{2,1,0:T(8,128)(2,1)} %cond.1, s32[1,80]{1,0:T(1,128)} %bitcast.18, bf16[384,768]{1,0:T(8,128)(2,1)} %ws.1, ...), custom_call_target="tpu_custom_call" | custom-call | flops 4000000000 | bytes 10000000 | tf_op jit(solution)/shard_map/qkv/pallas_call | solution.py:107
  6.3 8.0 %all-to-all-start = ((bf16[16,80,384]{2,1,0:T(8,128)(2,1)}), bf16[16,80,384]{2,1,0:T(8,128)(2,1)S(1)}, u32[]{:S(2)}, u32[]{:S(2)}) async-start(bf16[16,80,384]{2,1,0:T(8,128)(2,1)} %get-tuple-element.19), calls=%async_computation | async-start | bytes 1966080 | tf_op jit(solution)/shard_map/all_to_all | solution.py:414
  14.3 11.9 %bias.1 = bf16[16,80,896]{2,1,0:T(8,128)(2,1)} custom-call(bf16[80,640,128]{2,1,0:T(8,128)(2,1)} %pair.1, bf16[16,128]{1,0:T(8,128)(2,1)} %bitcast.17, bf16[16,80,256]{2,1,0:T(8,128)(2,1)} %get-tuple-element.20.q), custom_call_target="tpu_custom_call" | custom-call | flops 10000000000 | bytes 15000000 | tf_op jit(solution)/shard_map/bias/pallas_call | solution.py:152
  26.1 0.0 copy-start.10
  26.2 5.2 %all-to-all-done = bf16[16,80,384]{2,1,0:T(8,128)(2,1)S(1)} async-done(((bf16[16,80,384]{2,1,0:T(8,128)(2,1)}), bf16[16,80,384]{2,1,0:T(8,128)(2,1)S(1)}, u32[]{:S(2)}, u32[]{:S(2)}) %all-to-all-start) | async-done | bytes 983072 | tf_op jit(solution)/shard_map/all_to_all | solution.py:414
  31.3 3.0 %collective-permute-start.1 = (bf16[16,80,384]{2,1,0:T(8,128)(2,1)S(1)}, bf16[16,80,384]{2,1,0:T(8,128)(2,1)}, u32[]{:S(2)}, u32[]{:S(2)}) collective-permute-start(bf16[16,80,384]{2,1,0:T(8,128)(2,1)S(1)} %all-to-all-done), channel_id=1, source_target_pairs={{0,12},{4,0},{8,4},{12,8},{1,13},{5,1},{9,5},{13,9},{2,14},{6,2},{... | collective-permute-start | bytes 2949128 | tf_op jit(solution)/shard_map/ppermute | solution.py:392
  34.4 0.0 collective-permute-start
  34.4 3.7 %all-to-all-start.1 = ((bf16[16,80,896]{2,1,0:T(8,128)(2,1)}), bf16[16,80,896]{2,1,0:T(8,128)(2,1)S(1)}, u32[]{:S(2)}, u32[]{:S(2)}) async-start(bf16[16,80,896]{2,1,0:T(8,128)(2,1)} %bias.1), calls=%async_computation.1 | async-start | bytes 4587520 | tf_op jit(solution)/shard_map/all_to_all | solution.py:414
  38.1 0.0 copy-done.10
  38.1 0.0 copy-start
  38.1 1.3 %copy-done = bf16[768,768]{1,0:T(8,128)(2,1)S(1)} copy-done((bf16[768,768]{1,0:T(8,128)(2,1)S(1)}, bf16[768,768]{1,0:T(8,128)(2,1)}, u32[]{:S(2)}) %copy-start) | copy-done | bytes 1179672
  39.4 0.0 copy-start.2
  39.4 1.1 copy-done.2
  40.4 0.0 copy-start.4
  40.4 1.4 %copy-done.4 = bf16[768,1024]{1,0:T(8,128)(2,1)S(1)} copy-done((bf16[768,1024]{1,0:T(8,128)(2,1)S(1)}, bf16[768,1024]{1,0:T(8,128)(2,1)}, u32[]{:S(2)}) %copy-start.4) | copy-done | bytes 1572888
  41.8 0.0 copy-start.9
  41.8 1.0 copy-done.9
  42.9 2.1 %gates.1 = (f32[4,80,1024]{2,1,0:T(8,128)S(1)}, f32[4,80,768]{2,1,0:T(8,128)S(1)}) custom-call(bf16[4,80,768]{2,1,0:T(8,128)(2,1)S(1)} %copy-done.9, bf16[4,80,384]{2,1,0:T(8,128)(2,1)S(1)} %copy-done.10, bf16[768,1024]{1,0:T(8,128)(2,1)S(1)} %copy-done.4, bf16[768,768]{1,0:T(8,128)(2,1)S(1)} %copy-done, bf16[384,768]{1,0:T(8,128)(2,1)S(1)} %copy-done.2), custom_call_target="tpu_custom_call" | custom-call | flops 32000000000 | bytes 9000000 | tf_op jit(solution)/shard_map/gates/pallas_call | solution.py:321
  45.0 0.0 copy-start.5
  45.0 1.1 copy-done.5
  46.1 0.0 copy-start.7
  46.1 1.0 copy-done.7
  47.1 6.5 %collective-permute-done.1.second = bf16[16,80,384]{2,1,0:T(8,128)(2,1)} collective-permute-done((bf16[16,80,384]{2,1,0:T(8,128)(2,1)S(1)}, bf16[16,80,384]{2,1,0:T(8,128)(2,1)}, u32[]{:S(2)}, u32[]{:S(2)}) %collective-permute-start.1) | collective-permute-done | bytes 983072 | tf_op jit(solution)/shard_map/ppermute | solution.py:392
  53.6 3.5 %collective-permute-done.first = bf16[16,80,384]{2,1,0:T(8,128)(2,1)} collective-permute-done((bf16[16,80,384]{2,1,0:T(8,128)(2,1)S(1)}, bf16[16,80,384]{2,1,0:T(8,128)(2,1)}, u32[]{:S(2)}, u32[]{:S(2)}) %collective-permute-start) | collective-permute-done | bytes 983072 | tf_op jit(solution)/shard_map/ppermute | solution.py:392
  57.1 2.2 %halves.1 = (bf16[8,80,384]{2,1,0:T(8,128)(2,1)}, bf16[8,80,384]{2,1,0:T(8,128)(2,1)}) custom-call(bf16[16,80,384]{2,1,0:T(8,128)(2,1)} %collective-permute-done.first, bf16[16,80,384]{2,1,0:T(8,128)(2,1)} %collective-permute-done.1.second), custom_call_target="tpu_custom_call" | custom-call | bytes 2000000 | tf_op jit(solution)/shard_map/halves/pallas_call | solution.py:379
  59.3 0.0 collective-permute-start.2
  59.3 3.2 %collective-permute-start.3 = (bf16[8,80,384]{2,1,0:T(8,128)(2,1)}, bf16[8,80,384]{2,1,0:T(8,128)(2,1)}, u32[]{:S(2)}, u32[]{:S(2)}) collective-permute-start(bf16[8,80,384]{2,1,0:T(8,128)(2,1)} %get-tuple-element.30), channel_id=1, source_target_pairs={{0,12},{4,0},{8,4},{12,8},{1,13},{5,1},{9,5},{13,9},{2,14},{6,2},{... | collective-permute-start | bytes 1474568 | tf_op jit(solution)/shard_map/ppermute | solution.py:392
  62.6 0.1 pad_add_fusion.place
  62.6 5.1 %all-to-all-done.1 = bf16[16,80,896]{2,1,0:T(8,128)(2,1)S(1)} async-done(((bf16[16,80,896]{2,1,0:T(8,128)(2,1)}), bf16[16,80,896]{2,1,0:T(8,128)(2,1)S(1)}, u32[]{:S(2)}, u32[]{:S(2)}) %all-to-all-start.1) | async-done | bytes 2293792 | tf_op jit(solution)/shard_map/all_to_all | solution.py:414
  67.8 0.0 collective-permute-start.4
  67.8 3.1 %collective-permute-done.2 = bf16[8,80,384]{2,1,0:T(8,128)(2,1)} collective-permute-done((bf16[8,80,384]{2,1,0:T(8,128)(2,1)}, bf16[8,80,384]{2,1,0:T(8,128)(2,1)}, u32[]{:S(2)}, u32[]{:S(2)}) %collective-permute-start.2) | collective-permute-done | bytes 491552 | tf_op jit(solution)/shard_map/ppermute | solution.py:392
  70.9 0.0 collective-permute-done.3
  70.9 3.9 %lay.1.keys = bf16[2,4,2560,128]{3,2,1,0:T(8,128)(2,1)S(1)} custom-call(s32[2]{0:T(128)S(1)} %pad_add_fusion.place, bf16[2,4,2,80,384]{4,3,2,1,0:T(8,128)(2,1)S(1)} %bitcast.14, bf16[2,4,2,80,384]{4,3,2,1,0:T(8,128)(2,1)} %bitcast.6.up, bf16[1,4,2,80,384]{4,3,2,1,0:T(8,128)(2,1)} %bitcast.7.far_low, bf16[1,4,2,80,384]{4,3,2,1,0:T(8,128)(2,1)} %bitcast.8.far_high, ...), custom_call_target="tpu_custom_call" | custom-call | flops 40000000000 | bytes 10000000 | tf_op jit(solution)/shard_map/lay/pallas_call | solution.py:204
  74.8 0.0 collective-permute-done.4
  74.8 0.0 copy-start.1
  74.8 0.0 copy-start.3
  74.8 0.0 copy-start.6
  74.8 0.0 copy-start.8
  74.8 16.9 %attend.1 = bf16[8,2,80,256]{3,2,1,0:T(8,128)(2,1)S(1)} custom-call(bf16[8,2,80,896]{3,2,1,0:T(8,128)(2,1)S(1)} %bitcast.12, bf16[2,4,2560,128]{3,2,1,0:T(8,128)(2,1)S(1)} %lay.1.keys, bf16[8,2,80,896]{3,2,1,0:T(8,128)(2,1)S(1)} %bitcast.13, bf16[8,2,80,896]{3,2,1,0:T(8,128)(2,1)S(1)} %bitcast.16), custom_call_target="tpu_custom_call" | custom-call | flops 14000000000 | bytes 10000000 | tf_op jit(solution)/shard_map/attend/pallas_call | solution.py:293
  91.7 14.8 %all_to_all.15.attended = bf16[16,80,256]{2,1,0:T(8,128)(2,1)S(1)} all-to-all(bf16[16,80,256]{2,1,0:T(8,128)(2,1)S(1)} %bitcast.15), channel_id=1, replica_groups=mesh['zh'=2,'x'=4,'y'=4,'zl'=2,'co'=2] {'zh','x','zl'}, dimensions={0} | all-to-all | bytes 1310720 | tf_op jit(solution)/shard_map/all_to_all | solution.py:414
  106.5 0.0 copy-done.1
  106.5 0.0 copy-done.3
  106.5 0.0 copy-done.6
  106.5 0.0 copy-done.8
  106.5 1.6 %out.1 = bf16[4,80,768]{2,1,0:T(8,128)(2,1)} custom-call(bf16[16,80,256]{2,1,0:T(8,128)(2,1)S(1)} %all_to_all.15.attended, f32[4,80,1024]{2,1,0:T(8,128)S(1)} %copy-done.6, f32[4,80,768]{2,1,0:T(8,128)S(1)} %copy-done.8, bf16[4,80,768]{2,1,0:T(8,128)(2,1)S(1)} %copy-done.3, bf16[768,768]{1,0:T(8,128)(2,1)S(1)} %copy-done.1), custom_call_target="tpu_custom_call" | custom-call | flops 2000000000 | bytes 6000000 | tf_op jit(solution)/shard_map/out/pallas_call | solution.py:360
Async XLA Ops:
  6.3 25.0 %all-to-all-start = ((bf16[16,80,384]{2,1,0:T(8,128)(2,1)}), bf16[16,80,384]{2,1,0:T(8,128)(2,1)S(1)}, u32[]{:S(2)}, u32[]{:S(2)}) async-start(bf16[16,80,384]{2,1,0:T(8,128)(2,1)} %get-tuple-element.19), calls=%async_computation | async-start | bytes 1966080 | tf_op jit(solution)/shard_map/all_to_all | solution.py:414
  26.1 11.9 %copy-start.10 = (bf16[4,80,384]{2,1,0:T(8,128)(2,1)S(1)}, bf16[4,80,384]{2,1,0:T(8,128)(2,1)}, u32[]{:S(2)}) copy-start(bf16[4,80,384]{2,1,0:T(8,128)(2,1)} %get-tuple-element.24.cn) | copy-start | bytes 737284
  31.3 22.3 %collective-permute-start.1 = (bf16[16,80,384]{2,1,0:T(8,128)(2,1)S(1)}, bf16[16,80,384]{2,1,0:T(8,128)(2,1)}, u32[]{:S(2)}, u32[]{:S(2)}) collective-permute-start(bf16[16,80,384]{2,1,0:T(8,128)(2,1)S(1)} %all-to-all-done), channel_id=1, source_target_pairs={{0,12},{4,0},{8,4},{12,8},{1,13},{5,1},{9,5},{13,9},{2,14},{6,2},{... | collective-permute-start | bytes 2949128 | tf_op jit(solution)/shard_map/ppermute | solution.py:392
  34.4 22.8 %collective-permute-start = (bf16[16,80,384]{2,1,0:T(8,128)(2,1)S(1)}, bf16[16,80,384]{2,1,0:T(8,128)(2,1)}, u32[]{:S(2)}, u32[]{:S(2)}) collective-permute-start(bf16[16,80,384]{2,1,0:T(8,128)(2,1)S(1)} %all-to-all-done), channel_id=1, source_target_pairs={{0,4},{4,8},{8,12},{12,0},{1,5},{5,9},{9,13},{13,1},{2,6},{6,10},{... | collective-permute-start | bytes 2949128 | tf_op jit(solution)/shard_map/ppermute | solution.py:392
  34.4 33.4 %all-to-all-start.1 = ((bf16[16,80,896]{2,1,0:T(8,128)(2,1)}), bf16[16,80,896]{2,1,0:T(8,128)(2,1)S(1)}, u32[]{:S(2)}, u32[]{:S(2)}) async-start(bf16[16,80,896]{2,1,0:T(8,128)(2,1)} %bias.1), calls=%async_computation.1 | async-start | bytes 4587520 | tf_op jit(solution)/shard_map/all_to_all | solution.py:414
  38.1 1.3 %copy-start = (bf16[768,768]{1,0:T(8,128)(2,1)S(1)}, bf16[768,768]{1,0:T(8,128)(2,1)}, u32[]{:S(2)}) copy-start(bf16[768,768]{1,0:T(8,128)(2,1)} %wg.1) | copy-start | bytes 3538948
  39.4 1.1 copy-start.2
  40.4 1.4 %copy-start.4 = (bf16[768,1024]{1,0:T(8,128)(2,1)S(1)}, bf16[768,1024]{1,0:T(8,128)(2,1)}, u32[]{:S(2)}) copy-start(bf16[768,1024]{1,0:T(8,128)(2,1)} %constant.11.clone.place) | copy-start | bytes 4718596
  41.8 1.0 copy-start.9
  45.0 1.1 copy-start.5
  46.1 1.0 copy-start.7
  59.3 11.5 %collective-permute-start.2 = (bf16[8,80,384]{2,1,0:T(8,128)(2,1)}, bf16[8,80,384]{2,1,0:T(8,128)(2,1)}, u32[]{:S(2)}, u32[]{:S(2)}) collective-permute-start(bf16[8,80,384]{2,1,0:T(8,128)(2,1)} %get-tuple-element.29), channel_id=1, source_target_pairs={{0,4},{4,8},{8,12},{12,0},{1,5},{5,9},{9,13},{13,1},{2,6},{6,10},{... | collective-permute-start | bytes 1474568 | tf_op jit(solution)/shard_map/ppermute | solution.py:392
  59.3 11.5 %collective-permute-start.3 = (bf16[8,80,384]{2,1,0:T(8,128)(2,1)}, bf16[8,80,384]{2,1,0:T(8,128)(2,1)}, u32[]{:S(2)}, u32[]{:S(2)}) collective-permute-start(bf16[8,80,384]{2,1,0:T(8,128)(2,1)} %get-tuple-element.30), channel_id=1, source_target_pairs={{0,12},{4,0},{8,4},{12,8},{1,13},{5,1},{9,5},{13,9},{2,14},{6,2},{... | collective-permute-start | bytes 1474568 | tf_op jit(solution)/shard_map/ppermute | solution.py:392
  67.8 7.0 %collective-permute-start.4 = (bf16[16,80,896]{2,1,0:T(8,128)(2,1)S(1)}, bf16[16,80,896]{2,1,0:T(8,128)(2,1)S(1)}, u32[]{:S(2)}, u32[]{:S(2)}) collective-permute-start(bf16[16,80,896]{2,1,0:T(8,128)(2,1)S(1)} %all-to-all-done.1), channel_id=1, source_target_pairs={{0,1},{1,0},{2,3},{3,2},{4,5},{5,4},{6,7},{7,6},{8,9},{9,8},{10,11... | collective-permute-start | bytes 6881288 | tf_op jit(solution)/shard_map/ppermute | solution.py:423
  74.8 31.7 %copy-start.1 = (bf16[768,768]{1,0:T(8,128)(2,1)S(1)}, bf16[768,768]{1,0:T(8,128)(2,1)}, u32[]{:S(2)}) copy-start(bf16[768,768]{1,0:T(8,128)(2,1)} %wo.1) | copy-start | bytes 3538948
  74.8 31.7 %copy-start.3 = (bf16[4,80,768]{2,1,0:T(8,128)(2,1)S(1)}, bf16[4,80,768]{2,1,0:T(8,128)(2,1)}, u32[]{:S(2)}) copy-start(bf16[4,80,768]{2,1,0:T(8,128)(2,1)} %act.3) | copy-start | bytes 1474564
  74.8 31.7 %copy-start.6 = (f32[4,80,1024]{2,1,0:T(8,128)S(1)}, f32[4,80,1024]{2,1,0:T(8,128)}, u32[]{:S(2)}) copy-start(f32[4,80,1024]{2,1,0:T(8,128)} %copy-done.5) | copy-start | bytes 3932164
  74.8 31.7 %copy-start.8 = (f32[4,80,768]{2,1,0:T(8,128)S(1)}, f32[4,80,768]{2,1,0:T(8,128)}, u32[]{:S(2)}) copy-start(f32[4,80,768]{2,1,0:T(8,128)} %copy-done.7) | copy-start | bytes 2949124

commit v7 on v6

--- a/solution.py
+++ b/solution.py
@@ -289,7 +289,7 @@
 def attend(keys, own, other):
     tokens = own.shape[2]
     chunk = 8 * tokens
-    b_spec = pl.BlockSpec((8, 2, tokens, chunk), lambda z, p: (0, 0, 0, 0))
+    b_spec = pl.BlockSpec(memory_space=pltpu.VMEM)
     return pl.pallas_call(
         attend_kernel,
         grid=(2, 2),
@@ -367,21 +367,25 @@
     )(attended, gate, og, act, wo)
 
 
-def halves_kernel(first, second, first_out, second_out):
-    first_out[...] = first[...]
-    second_out[...] = second[...]
+def halves_kernel(first, second, first_out, second_out, sem):
+    count = first_out.shape[0]
+    low = pltpu.make_async_copy(first.at[pl.ds(0, count)], first_out, sem.at[0])
+    high = pltpu.make_async_copy(second.at[pl.ds(count, count)], second_out, sem.at[1])
+    low.start()
+    high.start()
+    low.wait()
+    high.wait()
 
 
 def halves(first, second):
     block = (first.shape[0] // 2,) + first.shape[1:]
-    low = pl.BlockSpec(block, lambda i: (0, 0, 0))
-    high = pl.BlockSpec(block, lambda i: (1, 0, 0))
+    anywhere = pl.BlockSpec(memory_space=pl.ANY)
     return pl.pallas_call(
         halves_kernel,
-        grid=(1,),
-        in_specs=[low, high],
-        out_specs=[low, low],
+        in_specs=[anywhere] * 2,
+        out_specs=[anywhere] * 2,
         out_shape=[jax.ShapeDtypeStruct(block, first.dtype)] * 2,
+        scratch_shapes=[pltpu.SemaphoreType.DMA((2,))],
         compiler_params=pltpu.CompilerParams(vmem_limit_bytes=SMALL_VMEM_BYTES),
         cost_estimate=pl.CostEstimate(flops=0, bytes_accessed=2_000_000, transcendentals=0),
         name="halves",

time: 109 us -> 137 us (1.26)
  Pallas kernels: 44.9 us -> 73.3 us
    pallas_call x1, Pallas kernels: 2.2 us -> 30.9 us  [halves(): pl.pallas_call(halves_kernel, in_specs=[anywhere] * 2, out_specs=[anywher...]
    all_to_all x2, waiting for transfers between devices: 10.3 us -> 5.19 us  [per_device(): exchange = lambda a: lax.all_to_all(a, XZ, 0, 0, tiled=True)]
    ppermute x4, waiting for transfers between devices: 13.1 us -> 18.1 us  [ring(): return lax.ppermute(block, 'y', [(i, (i + step) % 4) for i in range(4)])]
  transfers between devices with their start and end apart: 7 -> 7, of which waited for: 5 -> 4; matrix products, arithmetic and copies ran while one was open for 0% -> 0% of each run, Pallas kernels for 19% -> 36%
where the time goes in v7:
time: 137 us
  Pallas kernels  73.3 us (54%)
  waiting for transfers between devices  23.3 us (17%)
  starting transfers between devices  18.2 us (13%)
  blocking collectives  14.8 us (11%)
  local copies, waits for them, and re-layouts  6.82 us (5%)
    pallas_call x1, Pallas kernels, halves(): pl.pallas_call(halves_kernel, in_specs=[anywhere] * 2, out_specs=[anywher...  30.9 us
    ppermute x4, waiting for transfers between devices, ring(): return lax.ppermute(block, 'y', [(i, (i + step) % 4) for i in range(4)])  18.1 us
    pallas_call x1, Pallas kernels, attend(): pl.pallas_call(attend_kernel, grid=(2, 2), in_specs=[pl.BlockSpec((8, 1,...  16.5 us
    all_to_all x1, blocking collectives, per_device(): exchange = lambda a: lax.all_to_all(a, XZ, 0, 0, tiled=True)  14.8 us
    pallas_call x1, Pallas kernels, project_bias(): pl.pallas_call(bias_kernel, grid=(queries // step,), in_specs=[pl.BlockSp...  11.9 us
    all_to_all x2, starting transfers between devices, per_device(): exchange = lambda a: lax.all_to_all(a, XZ, 0, 0, tiled=True)  11.7 us
    unnamed x22, local copies, waits for them, and re-layouts  6.82 us
    ppermute x4, starting transfers between devices, ring(): return lax.ppermute(block, 'y', [(i, (i + step) % 4) for i in range(4)])  6.31 us
  transfers between devices with their start and end apart: 7, of which 4 were waited for; matrix products, arithmetic and copies ran while one was open for 0% of the time, Pallas kernels for 36%

profile of v7, /device:TPU:0, one launch (start us, length us, event | category | flops | bytes accessed | tf_op | source)
XLA Modules:
  0.0 136.5 jit_solution(14020266758891471789)
XLA Ops:
  0.0 6.3 %qkv.1 = (bf16[16,80,384]{2,1,0:T(8,128)(2,1)}, bf16[16,80,256]{2,1,0:T(8,128)(2,1)}, bf16[4,80,768]{2,1,0:T(8,128)(2,1)}, bf16[4,80,384]{2,1,0:T(8,128)(2,1)}) custom-call(bf16[4,80,768]{2,1,0:T(8,128)(2,1)} %act.3, bf16[4,80,384]{2,1,0:T(8,128)(2,1)} %cond.1, s32[1,80]{1,0:T(1,128)} %bitcast.18, bf16[384,768]{1,0:T(8,128)(2,1)} %ws.1, ...), custom_call_target="tpu_custom_call" | custom-call | flops 4000000000 | bytes 10000000 | tf_op jit(solution)/shard_map/qkv/pallas_call | solution.py:107
  6.3 8.0 %all-to-all-start = ((bf16[16,80,384]{2,1,0:T(8,128)(2,1)}), bf16[16,80,384]{2,1,0:T(8,128)(2,1)S(1)}, u32[]{:S(2)}, u32[]{:S(2)}) async-start(bf16[16,80,384]{2,1,0:T(8,128)(2,1)} %get-tuple-element.19), calls=%async_computation | async-start | bytes 1966080 | tf_op jit(solution)/shard_map/all_to_all | solution.py:418
  14.3 11.9 %bias.1 = bf16[16,80,896]{2,1,0:T(8,128)(2,1)} custom-call(bf16[80,640,128]{2,1,0:T(8,128)(2,1)} %pair.1, bf16[16,128]{1,0:T(8,128)(2,1)} %bitcast.17, bf16[16,80,256]{2,1,0:T(8,128)(2,1)} %get-tuple-element.20.q), custom_call_target="tpu_custom_call" | custom-call | flops 10000000000 | bytes 15000000 | tf_op jit(solution)/shard_map/bias/pallas_call | solution.py:152
  26.1 0.0 copy-start.10
  26.2 5.2 %all-to-all-done = bf16[16,80,384]{2,1,0:T(8,128)(2,1)S(1)} async-done(((bf16[16,80,384]{2,1,0:T(8,128)(2,1)}), bf16[16,80,384]{2,1,0:T(8,128)(2,1)S(1)}, u32[]{:S(2)}, u32[]{:S(2)}) %all-to-all-start) | async-done | bytes 983072 | tf_op jit(solution)/shard_map/all_to_all | solution.py:418
  31.3 3.0 %collective-permute-start.1 = (bf16[16,80,384]{2,1,0:T(8,128)(2,1)S(1)}, bf16[16,80,384]{2,1,0:T(8,128)(2,1)}, u32[]{:S(2)}, u32[]{:S(2)}) collective-permute-start(bf16[16,80,384]{2,1,0:T(8,128)(2,1)S(1)} %all-to-all-done), channel_id=1, source_target_pairs={{0,12},{4,0},{8,4},{12,8},{1,13},{5,1},{9,5},{13,9},{2,14},{6,2},{... | collective-permute-start | bytes 2949128 | tf_op jit(solution)/shard_map/ppermute | solution.py:396
  34.4 0.0 collective-permute-start
  34.4 3.7 %all-to-all-start.1 = ((bf16[16,80,896]{2,1,0:T(8,128)(2,1)}), bf16[16,80,896]{2,1,0:T(8,128)(2,1)S(1)}, u32[]{:S(2)}, u32[]{:S(2)}) async-start(bf16[16,80,896]{2,1,0:T(8,128)(2,1)} %bias.1), calls=%async_computation.1 | async-start | bytes 4587520 | tf_op jit(solution)/shard_map/all_to_all | solution.py:418
  38.1 0.0 copy-done.10
  38.1 0.0 copy-start
  38.1 1.3 copy-done
  39.4 0.0 copy-start.2
  39.4 1.1 copy-done.2
  40.4 0.0 copy-start.4
  40.4 1.4 %copy-done.4 = bf16[768,1024]{1,0:T(8,128)(2,1)S(1)} copy-done((bf16[768,1024]{1,0:T(8,128)(2,1)S(1)}, bf16[768,1024]{1,0:T(8,128)(2,1)}, u32[]{:S(2)}) %copy-start.4) | copy-done | bytes 1572888
  41.8 0.0 copy-start.9
  41.8 1.0 copy-done.9
  42.9 2.1 %gates.1 = (f32[4,80,1024]{2,1,0:T(8,128)S(1)}, f32[4,80,768]{2,1,0:T(8,128)S(1)}) custom-call(bf16[4,80,768]{2,1,0:T(8,128)(2,1)S(1)} %copy-done.9, bf16[4,80,384]{2,1,0:T(8,128)(2,1)S(1)} %copy-done.10, bf16[768,1024]{1,0:T(8,128)(2,1)S(1)} %copy-done.4, bf16[768,768]{1,0:T(8,128)(2,1)S(1)} %copy-done, bf16[384,768]{1,0:T(8,128)(2,1)S(1)} %copy-done.2), custom_call_target="tpu_custom_call" | custom-call | flops 32000000000 | bytes 9000000 | tf_op jit(solution)/shard_map/gates/pallas_call | solution.py:321
  45.0 0.0 copy-start.5
  45.0 1.1 copy-done.5
  46.1 0.0 copy-start.7
  46.1 1.0 copy-done.7
  47.1 6.5 %collective-permute-done.1.second = bf16[16,80,384]{2,1,0:T(8,128)(2,1)} collective-permute-done((bf16[16,80,384]{2,1,0:T(8,128)(2,1)S(1)}, bf16[16,80,384]{2,1,0:T(8,128)(2,1)}, u32[]{:S(2)}, u32[]{:S(2)}) %collective-permute-start.1) | collective-permute-done | bytes 983072 | tf_op jit(solution)/shard_map/ppermute | solution.py:396
  53.6 3.5 %collective-permute-done.first = bf16[16,80,384]{2,1,0:T(8,128)(2,1)} collective-permute-done((bf16[16,80,384]{2,1,0:T(8,128)(2,1)S(1)}, bf16[16,80,384]{2,1,0:T(8,128)(2,1)}, u32[]{:S(2)}, u32[]{:S(2)}) %collective-permute-start) | collective-permute-done | bytes 983072 | tf_op jit(solution)/shard_map/ppermute | solution.py:396
  57.1 30.9 %halves.1 = (bf16[8,80,384]{2,1,0:T(8,128)(2,1)}, bf16[8,80,384]{2,1,0:T(8,128)(2,1)}) custom-call(bf16[16,80,384]{2,1,0:T(8,128)(2,1)} %collective-permute-done.first, bf16[16,80,384]{2,1,0:T(8,128)(2,1)} %collective-permute-done.1.second), custom_call_target="tpu_custom_call" | custom-call | bytes 2000000 | tf_op jit(solution)/shard_map/halves/pallas_call | solution.py:383
  88.0 0.1 collective-permute-start.2
  88.1 3.2 %collective-permute-start.3 = (bf16[8,80,384]{2,1,0:T(8,128)(2,1)}, bf16[8,80,384]{2,1,0:T(8,128)(2,1)}, u32[]{:S(2)}, u32[]{:S(2)}) collective-permute-start(bf16[8,80,384]{2,1,0:T(8,128)(2,1)} %get-tuple-element.30), channel_id=1, source_target_pairs={{0,12},{4,0},{8,4},{12,8},{1,13},{5,1},{9,5},{13,9},{2,14},{6,2},{... | collective-permute-start | bytes 1474568 | tf_op jit(solution)/shard_map/ppermute | solution.py:396
  91.3 0.1 pad_add_fusion.place
  91.4 0.0 all-to-all-done.1
  91.4 0.2 collective-permute-start.4
  91.6 8.0 %collective-permute-done.2 = bf16[8,80,384]{2,1,0:T(8,128)(2,1)} collective-permute-done((bf16[8,80,384]{2,1,0:T(8,128)(2,1)}, bf16[8,80,384]{2,1,0:T(8,128)(2,1)}, u32[]{:S(2)}, u32[]{:S(2)}) %collective-permute-start.2) | collective-permute-done | bytes 491552 | tf_op jit(solution)/shard_map/ppermute | solution.py:396
  99.6 0.0 collective-permute-done.3
  99.6 3.9 %lay.1.keys = bf16[2,4,2560,128]{3,2,1,0:T(8,128)(2,1)S(1)} custom-call(s32[2]{0:T(128)S(1)} %pad_add_fusion.place, bf16[2,4,2,80,384]{4,3,2,1,0:T(8,128)(2,1)S(1)} %bitcast.14, bf16[2,4,2,80,384]{4,3,2,1,0:T(8,128)(2,1)} %bitcast.6.up, bf16[1,4,2,80,384]{4,3,2,1,0:T(8,128)(2,1)} %bitcast.7.far_low, bf16[1,4,2,80,384]{4,3,2,1,0:T(8,128)(2,1)} %bitcast.8.far_high, ...), custom_call_target="tpu_custom_call" | custom-call | flops 40000000000 | bytes 10000000 | tf_op jit(solution)/shard_map/lay/pallas_call | solution.py:204
  103.6 0.0 collective-permute-done.4
  103.6 0.0 copy-start.1
  103.6 0.0 copy-start.3
  103.6 0.0 copy-start.6
  103.6 0.0 copy-start.8
  103.6 16.5 %attend.1 = bf16[8,2,80,256]{3,2,1,0:T(8,128)(2,1)S(1)} custom-call(bf16[8,2,80,896]{3,2,1,0:T(8,128)(2,1)S(1)} %bitcast.12, bf16[2,4,2560,128]{3,2,1,0:T(8,128)(2,1)S(1)} %lay.1.keys, bf16[8,2,80,896]{3,2,1,0:T(8,128)(2,1)S(1)} %bitcast.13, bf16[8,2,80,896]{3,2,1,0:T(8,128)(2,1)S(1)} %bitcast.16), custom_call_target="tpu_custom_call" | custom-call | flops 14000000000 | bytes 10000000 | tf_op jit(solution)/shard_map/attend/pallas_call | solution.py:293
  120.1 14.8 %all_to_all.15.attended = bf16[16,80,256]{2,1,0:T(8,128)(2,1)S(1)} all-to-all(bf16[16,80,256]{2,1,0:T(8,128)(2,1)S(1)} %bitcast.15), channel_id=1, replica_groups=mesh['zh'=2,'x'=4,'y'=4,'zl'=2,'co'=2] {'zh','x','zl'}, dimensions={0} | all-to-all | bytes 1310720 | tf_op jit(solution)/shard_map/all_to_all | solution.py:418
  134.9 0.0 copy-done.1
  134.9 0.0 copy-done.3
  134.9 0.0 copy-done.6
  134.9 0.0 copy-done.8
  134.9 1.6 %out.1 = bf16[4,80,768]{2,1,0:T(8,128)(2,1)} custom-call(bf16[16,80,256]{2,1,0:T(8,128)(2,1)S(1)} %all_to_all.15.attended, f32[4,80,1024]{2,1,0:T(8,128)S(1)} %copy-done.6, f32[4,80,768]{2,1,0:T(8,128)S(1)} %copy-done.8, bf16[4,80,768]{2,1,0:T(8,128)(2,1)S(1)} %copy-done.3, bf16[768,768]{1,0:T(8,128)(2,1)S(1)} %copy-done.1), custom_call_target="tpu_custom_call" | custom-call | flops 2000000000 | bytes 6000000 | tf_op jit(solution)/shard_map/out/pallas_call | solution.py:360
Async XLA Ops:
  6.3 25.0 %all-to-all-start = ((bf16[16,80,384]{2,1,0:T(8,128)(2,1)}), bf16[16,80,384]{2,1,0:T(8,128)(2,1)S(1)}, u32[]{:S(2)}, u32[]{:S(2)}) async-start(bf16[16,80,384]{2,1,0:T(8,128)(2,1)} %get-tuple-element.19), calls=%async_computation | async-start | bytes 1966080 | tf_op jit(solution)/shard_map/all_to_all | solution.py:418
  26.1 11.9 %copy-start.10 = (bf16[4,80,384]{2,1,0:T(8,128)(2,1)S(1)}, bf16[4,80,384]{2,1,0:T(8,128)(2,1)}, u32[]{:S(2)}) copy-start(bf16[4,80,384]{2,1,0:T(8,128)(2,1)} %get-tuple-element.24.cn) | copy-start | bytes 737284
  31.3 22.3 %collective-permute-start.1 = (bf16[16,80,384]{2,1,0:T(8,128)(2,1)S(1)}, bf16[16,80,384]{2,1,0:T(8,128)(2,1)}, u32[]{:S(2)}, u32[]{:S(2)}) collective-permute-start(bf16[16,80,384]{2,1,0:T(8,128)(2,1)S(1)} %all-to-all-done), channel_id=1, source_target_pairs={{0,12},{4,0},{8,4},{12,8},{1,13},{5,1},{9,5},{13,9},{2,14},{6,2},{... | collective-permute-start | bytes 2949128 | tf_op jit(solution)/shard_map/ppermute | solution.py:396
  34.4 22.8 %collective-permute-start = (bf16[16,80,384]{2,1,0:T(8,128)(2,1)S(1)}, bf16[16,80,384]{2,1,0:T(8,128)(2,1)}, u32[]{:S(2)}, u32[]{:S(2)}) collective-permute-start(bf16[16,80,384]{2,1,0:T(8,128)(2,1)S(1)} %all-to-all-done), channel_id=1, source_target_pairs={{0,4},{4,8},{8,12},{12,0},{1,5},{5,9},{9,13},{13,1},{2,6},{6,10},{... | collective-permute-start | bytes 2949128 | tf_op jit(solution)/shard_map/ppermute | solution.py:396
  34.4 57.1 %all-to-all-start.1 = ((bf16[16,80,896]{2,1,0:T(8,128)(2,1)}), bf16[16,80,896]{2,1,0:T(8,128)(2,1)S(1)}, u32[]{:S(2)}, u32[]{:S(2)}) async-start(bf16[16,80,896]{2,1,0:T(8,128)(2,1)} %bias.1), calls=%async_computation.1 | async-start | bytes 4587520 | tf_op jit(solution)/shard_map/all_to_all | solution.py:418
  38.1 1.3 copy-start
  39.4 1.1 copy-start.2
  40.4 1.4 %copy-start.4 = (bf16[768,1024]{1,0:T(8,128)(2,1)S(1)}, bf16[768,1024]{1,0:T(8,128)(2,1)}, u32[]{:S(2)}) copy-start(bf16[768,1024]{1,0:T(8,128)(2,1)} %constant.11.clone.place) | copy-start | bytes 4718596
  41.8 1.0 copy-start.9
  45.0 1.1 copy-start.5
  46.1 1.0 copy-start.7
  88.0 11.6 %collective-permute-start.2 = (bf16[8,80,384]{2,1,0:T(8,128)(2,1)}, bf16[8,80,384]{2,1,0:T(8,128)(2,1)}, u32[]{:S(2)}, u32[]{:S(2)}) collective-permute-start(bf16[8,80,384]{2,1,0:T(8,128)(2,1)} %get-tuple-element.29), channel_id=1, source_target_pairs={{0,4},{4,8},{8,12},{12,0},{1,5},{5,9},{9,13},{13,1},{2,6},{6,10},{... | collective-permute-start | bytes 1474568 | tf_op jit(solution)/shard_map/ppermute | solution.py:396
  88.1 11.5 %collective-permute-start.3 = (bf16[8,80,384]{2,1,0:T(8,128)(2,1)}, bf16[8,80,384]{2,1,0:T(8,128)(2,1)}, u32[]{:S(2)}, u32[]{:S(2)}) collective-permute-start(bf16[8,80,384]{2,1,0:T(8,128)(2,1)} %get-tuple-element.30), channel_id=1, source_target_pairs={{0,12},{4,0},{8,4},{12,8},{1,13},{5,1},{9,5},{13,9},{2,14},{6,2},{... | collective-permute-start | bytes 1474568 | tf_op jit(solution)/shard_map/ppermute | solution.py:396
  91.4 12.1 %collective-permute-start.4 = (bf16[16,80,896]{2,1,0:T(8,128)(2,1)S(1)}, bf16[16,80,896]{2,1,0:T(8,128)(2,1)S(1)}, u32[]{:S(2)}, u32[]{:S(2)}) collective-permute-start(bf16[16,80,896]{2,1,0:T(8,128)(2,1)S(1)} %all-to-all-done.1), channel_id=1, source_target_pairs={{0,1},{1,0},{2,3},{3,2},{4,5},{5,4},{6,7},{7,6},{8,9},{9,8},{10,11... | collective-permute-start | bytes 6881288 | tf_op jit(solution)/shard_map/ppermute | solution.py:427
  103.6 31.3 %copy-start.1 = (bf16[768,768]{1,0:T(8,128)(2,1)S(1)}, bf16[768,768]{1,0:T(8,128)(2,1)}, u32[]{:S(2)}) copy-start(bf16[768,768]{1,0:T(8,128)(2,1)} %wo.1) | copy-start | bytes 3538948
  103.6 31.3 %copy-start.3 = (bf16[4,80,768]{2,1,0:T(8,128)(2,1)S(1)}, bf16[4,80,768]{2,1,0:T(8,128)(2,1)}, u32[]{:S(2)}) copy-start(bf16[4,80,768]{2,1,0:T(8,128)(2,1)} %act.3) | copy-start | bytes 1474564
  103.6 31.3 %copy-start.6 = (f32[4,80,1024]{2,1,0:T(8,128)S(1)}, f32[4,80,1024]{2,1,0:T(8,128)}, u32[]{:S(2)}) copy-start(f32[4,80,1024]{2,1,0:T(8,128)} %copy-done.5) | copy-start | bytes 3932164
  103.6 31.3 %copy-start.8 = (f32[4,80,768]{2,1,0:T(8,128)S(1)}, f32[4,80,768]{2,1,0:T(8,128)}, u32[]{:S(2)}) copy-start(f32[4,80,768]{2,1,0:T(8,128)} %copy-done.7) | copy-start | bytes 2949124

commit v8 on v6

--- a/solution.py
+++ b/solution.py
@@ -289,7 +289,7 @@
 def attend(keys, own, other):
     tokens = own.shape[2]
     chunk = 8 * tokens
-    b_spec = pl.BlockSpec((8, 2, tokens, chunk), lambda z, p: (0, 0, 0, 0))
+    b_spec = pl.BlockSpec(memory_space=pltpu.VMEM)
     return pl.pallas_call(
         attend_kernel,
         grid=(2, 2),

time: 109 us -> 108 us (level)
  no operation moved by 1% of the time
where the time goes in v8:
time: 108 us
  Pallas kernels  44.6 us (41%)
  waiting for transfers between devices  23.5 us (22%)
  starting transfers between devices  17.9 us (17%)
  blocking collectives  14.8 us (14%)
  local copies, waits for them, and re-layouts  6.82 us (6%)
    pallas_call x1, Pallas kernels, attend(): pl.pallas_call(attend_kernel, grid=(2, 2), in_specs=[pl.BlockSpec((8, 1,...  16.5 us
    all_to_all x1, blocking collectives, per_device(): exchange = lambda a: lax.all_to_all(a, XZ, 0, 0, tiled=True)  14.8 us
    ppermute x4, waiting for transfers between devices, ring(): return lax.ppermute(block, 'y', [(i, (i + step) % 4) for i in range(4)])  13.1 us
    pallas_call x1, Pallas kernels, project_bias(): pl.pallas_call(bias_kernel, grid=(queries // step,), in_specs=[pl.BlockSp...  11.9 us
    all_to_all x2, starting transfers between devices, per_device(): exchange = lambda a: lax.all_to_all(a, XZ, 0, 0, tiled=True)  11.7 us
    all_to_all x2, waiting for transfers between devices, per_device(): exchange = lambda a: lax.all_to_all(a, XZ, 0, 0, tiled=True)  10.3 us
    unnamed x22, local copies, waits for them, and re-layouts  6.82 us
    pallas_call x1, Pallas kernels, project_qkv(): pl.pallas_call(qkv_kernel, grid=(steps,), in_specs=[whole(act), whole(con...  6.3 us
  transfers between devices with their start and end apart: 7, of which 5 were waited for; matrix products, arithmetic and copies ran while one was open for 0% of the time, Pallas kernels for 19%

profile of v8, /device:TPU:0, one launch (start us, length us, event | category | flops | bytes accessed | tf_op | source)
XLA Modules:
  0.0 107.8 jit_solution(5288878033390704394)
XLA Ops:
  0.0 6.3 %qkv.1 = (bf16[16,80,384]{2,1,0:T(8,128)(2,1)}, bf16[16,80,256]{2,1,0:T(8,128)(2,1)}, bf16[4,80,768]{2,1,0:T(8,128)(2,1)}, bf16[4,80,384]{2,1,0:T(8,128)(2,1)}) custom-call(bf16[4,80,768]{2,1,0:T(8,128)(2,1)} %act.3, bf16[4,80,384]{2,1,0:T(8,128)(2,1)} %cond.1, s32[1,80]{1,0:T(1,128)} %bitcast.18, bf16[384,768]{1,0:T(8,128)(2,1)} %ws.1, ...), custom_call_target="tpu_custom_call" | custom-call | flops 4000000000 | bytes 10000000 | tf_op jit(solution)/shard_map/qkv/pallas_call | solution.py:107
  6.3 8.0 %all-to-all-start = ((bf16[16,80,384]{2,1,0:T(8,128)(2,1)}), bf16[16,80,384]{2,1,0:T(8,128)(2,1)S(1)}, u32[]{:S(2)}, u32[]{:S(2)}) async-start(bf16[16,80,384]{2,1,0:T(8,128)(2,1)} %get-tuple-element.19), calls=%async_computation | async-start | bytes 1966080 | tf_op jit(solution)/shard_map/all_to_all | solution.py:414
  14.3 11.9 %bias.1 = bf16[16,80,896]{2,1,0:T(8,128)(2,1)} custom-call(bf16[80,640,128]{2,1,0:T(8,128)(2,1)} %pair.1, bf16[16,128]{1,0:T(8,128)(2,1)} %bitcast.17, bf16[16,80,256]{2,1,0:T(8,128)(2,1)} %get-tuple-element.20.q), custom_call_target="tpu_custom_call" | custom-call | flops 10000000000 | bytes 15000000 | tf_op jit(solution)/shard_map/bias/pallas_call | solution.py:152
  26.1 0.0 copy-start.10
  26.2 5.2 %all-to-all-done = bf16[16,80,384]{2,1,0:T(8,128)(2,1)S(1)} async-done(((bf16[16,80,384]{2,1,0:T(8,128)(2,1)}), bf16[16,80,384]{2,1,0:T(8,128)(2,1)S(1)}, u32[]{:S(2)}, u32[]{:S(2)}) %all-to-all-start) | async-done | bytes 983072 | tf_op jit(solution)/shard_map/all_to_all | solution.py:414
  31.3 3.0 %collective-permute-start.1 = (bf16[16,80,384]{2,1,0:T(8,128)(2,1)S(1)}, bf16[16,80,384]{2,1,0:T(8,128)(2,1)}, u32[]{:S(2)}, u32[]{:S(2)}) collective-permute-start(bf16[16,80,384]{2,1,0:T(8,128)(2,1)S(1)} %all-to-all-done), channel_id=1, source_target_pairs={{0,12},{4,0},{8,4},{12,8},{1,13},{5,1},{9,5},{13,9},{2,14},{6,2},{... | collective-permute-start | bytes 2949128 | tf_op jit(solution)/shard_map/ppermute | solution.py:392
  34.4 0.0 collective-permute-start
  34.4 3.7 %all-to-all-start.1 = ((bf16[16,80,896]{2,1,0:T(8,128)(2,1)}), bf16[16,80,896]{2,1,0:T(8,128)(2,1)S(1)}, u32[]{:S(2)}, u32[]{:S(2)}) async-start(bf16[16,80,896]{2,1,0:T(8,128)(2,1)} %bias.1), calls=%async_computation.1 | async-start | bytes 4587520 | tf_op jit(solution)/shard_map/all_to_all | solution.py:414
  38.1 0.0 copy-done.10
  38.1 0.0 copy-start
  38.1 1.3 %copy-done = bf16[768,768]{1,0:T(8,128)(2,1)S(1)} copy-done((bf16[768,768]{1,0:T(8,128)(2,1)S(1)}, bf16[768,768]{1,0:T(8,128)(2,1)}, u32[]{:S(2)}) %copy-start) | copy-done | bytes 1179672
  39.4 0.0 copy-start.2
  39.4 1.1 copy-done.2
  40.4 0.0 copy-start.4
  40.4 1.4 %copy-done.4 = bf16[768,1024]{1,0:T(8,128)(2,1)S(1)} copy-done((bf16[768,1024]{1,0:T(8,128)(2,1)S(1)}, bf16[768,1024]{1,0:T(8,128)(2,1)}, u32[]{:S(2)}) %copy-start.4) | copy-done | bytes 1572888
  41.8 0.0 copy-start.9
  41.8 1.0 copy-done.9
  42.9 2.1 %gates.1 = (f32[4,80,1024]{2,1,0:T(8,128)S(1)}, f32[4,80,768]{2,1,0:T(8,128)S(1)}) custom-call(bf16[4,80,768]{2,1,0:T(8,128)(2,1)S(1)} %copy-done.9, bf16[4,80,384]{2,1,0:T(8,128)(2,1)S(1)} %copy-done.10, bf16[768,1024]{1,0:T(8,128)(2,1)S(1)} %copy-done.4, bf16[768,768]{1,0:T(8,128)(2,1)S(1)} %copy-done, bf16[384,768]{1,0:T(8,128)(2,1)S(1)} %copy-done.2), custom_call_target="tpu_custom_call" | custom-call | flops 32000000000 | bytes 9000000 | tf_op jit(solution)/shard_map/gates/pallas_call | solution.py:321
  45.0 0.0 copy-start.5
  45.0 1.1 copy-done.5
  46.1 0.0 copy-start.7
  46.1 1.0 copy-done.7
  47.1 6.5 %collective-permute-done.1.second = bf16[16,80,384]{2,1,0:T(8,128)(2,1)} collective-permute-done((bf16[16,80,384]{2,1,0:T(8,128)(2,1)S(1)}, bf16[16,80,384]{2,1,0:T(8,128)(2,1)}, u32[]{:S(2)}, u32[]{:S(2)}) %collective-permute-start.1) | collective-permute-done | bytes 983072 | tf_op jit(solution)/shard_map/ppermute | solution.py:392
  53.6 3.5 %collective-permute-done.first = bf16[16,80,384]{2,1,0:T(8,128)(2,1)} collective-permute-done((bf16[16,80,384]{2,1,0:T(8,128)(2,1)S(1)}, bf16[16,80,384]{2,1,0:T(8,128)(2,1)}, u32[]{:S(2)}, u32[]{:S(2)}) %collective-permute-start) | collective-permute-done | bytes 983072 | tf_op jit(solution)/shard_map/ppermute | solution.py:392
  57.1 2.2 %halves.1 = (bf16[8,80,384]{2,1,0:T(8,128)(2,1)}, bf16[8,80,384]{2,1,0:T(8,128)(2,1)}) custom-call(bf16[16,80,384]{2,1,0:T(8,128)(2,1)} %collective-permute-done.first, bf16[16,80,384]{2,1,0:T(8,128)(2,1)} %collective-permute-done.1.second), custom_call_target="tpu_custom_call" | custom-call | bytes 2000000 | tf_op jit(solution)/shard_map/halves/pallas_call | solution.py:379
  59.3 0.0 collective-permute-start.2
  59.3 3.2 %collective-permute-start.3 = (bf16[8,80,384]{2,1,0:T(8,128)(2,1)}, bf16[8,80,384]{2,1,0:T(8,128)(2,1)}, u32[]{:S(2)}, u32[]{:S(2)}) collective-permute-start(bf16[8,80,384]{2,1,0:T(8,128)(2,1)} %get-tuple-element.30), channel_id=1, source_target_pairs={{0,12},{4,0},{8,4},{12,8},{1,13},{5,1},{9,5},{13,9},{2,14},{6,2},{... | collective-permute-start | bytes 1474568 | tf_op jit(solution)/shard_map/ppermute | solution.py:392
  62.6 0.1 pad_add_fusion.place
  62.6 5.1 %all-to-all-done.1 = bf16[16,80,896]{2,1,0:T(8,128)(2,1)S(1)} async-done(((bf16[16,80,896]{2,1,0:T(8,128)(2,1)}), bf16[16,80,896]{2,1,0:T(8,128)(2,1)S(1)}, u32[]{:S(2)}, u32[]{:S(2)}) %all-to-all-start.1) | async-done | bytes 2293792 | tf_op jit(solution)/shard_map/all_to_all | solution.py:414
  67.8 0.0 collective-permute-start.4
  67.8 3.1 %collective-permute-done.2 = bf16[8,80,384]{2,1,0:T(8,128)(2,1)} collective-permute-done((bf16[8,80,384]{2,1,0:T(8,128)(2,1)}, bf16[8,80,384]{2,1,0:T(8,128)(2,1)}, u32[]{:S(2)}, u32[]{:S(2)}) %collective-permute-start.2) | collective-permute-done | bytes 491552 | tf_op jit(solution)/shard_map/ppermute | solution.py:392
  70.9 0.0 collective-permute-done.3
  70.9 3.9 %lay.1.keys = bf16[2,4,2560,128]{3,2,1,0:T(8,128)(2,1)S(1)} custom-call(s32[2]{0:T(128)S(1)} %pad_add_fusion.place, bf16[2,4,2,80,384]{4,3,2,1,0:T(8,128)(2,1)S(1)} %bitcast.14, bf16[2,4,2,80,384]{4,3,2,1,0:T(8,128)(2,1)} %bitcast.6.up, bf16[1,4,2,80,384]{4,3,2,1,0:T(8,128)(2,1)} %bitcast.7.far_low, bf16[1,4,2,80,384]{4,3,2,1,0:T(8,128)(2,1)} %bitcast.8.far_high, ...), custom_call_target="tpu_custom_call" | custom-call | flops 40000000000 | bytes 10000000 | tf_op jit(solution)/shard_map/lay/pallas_call | solution.py:204
  74.8 0.0 collective-permute-done.4
  74.8 0.0 copy-start.1
  74.8 0.0 copy-start.3
  74.8 0.0 copy-start.6
  74.8 0.0 copy-start.8
  74.8 16.5 %attend.1 = bf16[8,2,80,256]{3,2,1,0:T(8,128)(2,1)S(1)} custom-call(bf16[8,2,80,896]{3,2,1,0:T(8,128)(2,1)S(1)} %bitcast.12, bf16[2,4,2560,128]{3,2,1,0:T(8,128)(2,1)S(1)} %lay.1.keys, bf16[8,2,80,896]{3,2,1,0:T(8,128)(2,1)S(1)} %bitcast.13, bf16[8,2,80,896]{3,2,1,0:T(8,128)(2,1)S(1)} %bitcast.16), custom_call_target="tpu_custom_call" | custom-call | flops 14000000000 | bytes 10000000 | tf_op jit(solution)/shard_map/attend/pallas_call | solution.py:293
  91.4 14.8 %all_to_all.15.attended = bf16[16,80,256]{2,1,0:T(8,128)(2,1)S(1)} all-to-all(bf16[16,80,256]{2,1,0:T(8,128)(2,1)S(1)} %bitcast.15), channel_id=1, replica_groups=mesh['zh'=2,'x'=4,'y'=4,'zl'=2,'co'=2] {'zh','x','zl'}, dimensions={0} | all-to-all | bytes 1310720 | tf_op jit(solution)/shard_map/all_to_all | solution.py:414
  106.1 0.0 copy-done.1
  106.1 0.0 copy-done.3
  106.1 0.0 copy-done.6
  106.1 0.0 copy-done.8
  106.2 1.6 %out.1 = bf16[4,80,768]{2,1,0:T(8,128)(2,1)} custom-call(bf16[16,80,256]{2,1,0:T(8,128)(2,1)S(1)} %all_to_all.15.attended, f32[4,80,1024]{2,1,0:T(8,128)S(1)} %copy-done.6, f32[4,80,768]{2,1,0:T(8,128)S(1)} %copy-done.8, bf16[4,80,768]{2,1,0:T(8,128)(2,1)S(1)} %copy-done.3, bf16[768,768]{1,0:T(8,128)(2,1)S(1)} %copy-done.1), custom_call_target="tpu_custom_call" | custom-call | flops 2000000000 | bytes 6000000 | tf_op jit(solution)/shard_map/out/pallas_call | solution.py:360
Async XLA Ops:
  6.3 25.0 %all-to-all-start = ((bf16[16,80,384]{2,1,0:T(8,128)(2,1)}), bf16[16,80,384]{2,1,0:T(8,128)(2,1)S(1)}, u32[]{:S(2)}, u32[]{:S(2)}) async-start(bf16[16,80,384]{2,1,0:T(8,128)(2,1)} %get-tuple-element.19), calls=%async_computation | async-start | bytes 1966080 | tf_op jit(solution)/shard_map/all_to_all | solution.py:414
  26.1 11.9 %copy-start.10 = (bf16[4,80,384]{2,1,0:T(8,128)(2,1)S(1)}, bf16[4,80,384]{2,1,0:T(8,128)(2,1)}, u32[]{:S(2)}) copy-start(bf16[4,80,384]{2,1,0:T(8,128)(2,1)} %get-tuple-element.24.cn) | copy-start | bytes 737284
  31.3 22.3 %collective-permute-start.1 = (bf16[16,80,384]{2,1,0:T(8,128)(2,1)S(1)}, bf16[16,80,384]{2,1,0:T(8,128)(2,1)}, u32[]{:S(2)}, u32[]{:S(2)}) collective-permute-start(bf16[16,80,384]{2,1,0:T(8,128)(2,1)S(1)} %all-to-all-done), channel_id=1, source_target_pairs={{0,12},{4,0},{8,4},{12,8},{1,13},{5,1},{9,5},{13,9},{2,14},{6,2},{... | collective-permute-start | bytes 2949128 | tf_op jit(solution)/shard_map/ppermute | solution.py:392
  34.4 22.8 %collective-permute-start = (bf16[16,80,384]{2,1,0:T(8,128)(2,1)S(1)}, bf16[16,80,384]{2,1,0:T(8,128)(2,1)}, u32[]{:S(2)}, u32[]{:S(2)}) collective-permute-start(bf16[16,80,384]{2,1,0:T(8,128)(2,1)S(1)} %all-to-all-done), channel_id=1, source_target_pairs={{0,4},{4,8},{8,12},{12,0},{1,5},{5,9},{9,13},{13,1},{2,6},{6,10},{... | collective-permute-start | bytes 2949128 | tf_op jit(solution)/shard_map/ppermute | solution.py:392
  34.4 33.4 %all-to-all-start.1 = ((bf16[16,80,896]{2,1,0:T(8,128)(2,1)}), bf16[16,80,896]{2,1,0:T(8,128)(2,1)S(1)}, u32[]{:S(2)}, u32[]{:S(2)}) async-start(bf16[16,80,896]{2,1,0:T(8,128)(2,1)} %bias.1), calls=%async_computation.1 | async-start | bytes 4587520 | tf_op jit(solution)/shard_map/all_to_all | solution.py:414
  38.1 1.3 %copy-start = (bf16[768,768]{1,0:T(8,128)(2,1)S(1)}, bf16[768,768]{1,0:T(8,128)(2,1)}, u32[]{:S(2)}) copy-start(bf16[768,768]{1,0:T(8,128)(2,1)} %wg.1) | copy-start | bytes 3538948
  39.4 1.1 copy-start.2
  40.4 1.4 %copy-start.4 = (bf16[768,1024]{1,0:T(8,128)(2,1)S(1)}, bf16[768,1024]{1,0:T(8,128)(2,1)}, u32[]{:S(2)}) copy-start(bf16[768,1024]{1,0:T(8,128)(2,1)} %constant.11.clone.place) | copy-start | bytes 4718596
  41.8 1.0 copy-start.9
  45.0 1.1 copy-start.5
  46.1 1.0 copy-start.7
  59.3 11.5 %collective-permute-start.2 = (bf16[8,80,384]{2,1,0:T(8,128)(2,1)}, bf16[8,80,384]{2,1,0:T(8,128)(2,1)}, u32[]{:S(2)}, u32[]{:S(2)}) collective-permute-start(bf16[8,80,384]{2,1,0:T(8,128)(2,1)} %get-tuple-element.29), channel_id=1, source_target_pairs={{0,4},{4,8},{8,12},{12,0},{1,5},{5,9},{9,13},{13,1},{2,6},{6,10},{... | collective-permute-start | bytes 1474568 | tf_op jit(solution)/shard_map/ppermute | solution.py:392
  59.3 11.5 %collective-permute-start.3 = (bf16[8,80,384]{2,1,0:T(8,128)(2,1)}, bf16[8,80,384]{2,1,0:T(8,128)(2,1)}, u32[]{:S(2)}, u32[]{:S(2)}) collective-permute-start(bf16[8,80,384]{2,1,0:T(8,128)(2,1)} %get-tuple-element.30), channel_id=1, source_target_pairs={{0,12},{4,0},{8,4},{12,8},{1,13},{5,1},{9,5},{13,9},{2,14},{6,2},{... | collective-permute-start | bytes 1474568 | tf_op jit(solution)/shard_map/ppermute | solution.py:392
  67.8 7.0 %collective-permute-start.4 = (bf16[16,80,896]{2,1,0:T(8,128)(2,1)S(1)}, bf16[16,80,896]{2,1,0:T(8,128)(2,1)S(1)}, u32[]{:S(2)}, u32[]{:S(2)}) collective-permute-start(bf16[16,80,896]{2,1,0:T(8,128)(2,1)S(1)} %all-to-all-done.1), channel_id=1, source_target_pairs={{0,1},{1,0},{2,3},{3,2},{4,5},{5,4},{6,7},{7,6},{8,9},{9,8},{10,11... | collective-permute-start | bytes 6881288 | tf_op jit(solution)/shard_map/ppermute | solution.py:423
  74.8 31.3 %copy-start.1 = (bf16[768,768]{1,0:T(8,128)(2,1)S(1)}, bf16[768,768]{1,0:T(8,128)(2,1)}, u32[]{:S(2)}) copy-start(bf16[768,768]{1,0:T(8,128)(2,1)} %wo.1) | copy-start | bytes 3538948
  74.8 31.3 %copy-start.3 = (bf16[4,80,768]{2,1,0:T(8,128)(2,1)S(1)}, bf16[4,80,768]{2,1,0:T(8,128)(2,1)}, u32[]{:S(2)}) copy-start(bf16[4,80,768]{2,1,0:T(8,128)(2,1)} %act.3) | copy-start | bytes 1474564
  74.8 31.3 %copy-start.6 = (f32[4,80,1024]{2,1,0:T(8,128)S(1)}, f32[4,80,1024]{2,1,0:T(8,128)}, u32[]{:S(2)}) copy-start(f32[4,80,1024]{2,1,0:T(8,128)} %copy-done.5) | copy-start | bytes 3932164
  74.8 31.3 %copy-start.8 = (f32[4,80,768]{2,1,0:T(8,128)S(1)}, f32[4,80,768]{2,1,0:T(8,128)}, u32[]{:S(2)}) copy-start(f32[4,80,768]{2,1,0:T(8,128)} %copy-done.7) | copy-start | bytes 2949124
